TPU v7x, 256 devices: a whole 4x4x8 slice. The times are simulated.
256 devices in a mesh: aa: 16 (over z, x_lo), ba: 16 (over y, x_hi, core).
Axes of the slice: x: 4 (x_hi: 2, x_lo: 2; x = x_hi * 2 + x_lo), y: 4, z: 8, core: 2. Of those that a mesh axis runs over, the one named last changes fastest.
Arguments:
- b_vo: bfloat16 [128, 48, 4096], P('aa'), may hold values from -6 to 6
- b_vv: bfloat16 [16, 768, 4096], P('ba', None, 'aa'), may hold values from -0.09375 to 0.09375
- amplitudes: bfloat16 [768, 2304], P('ba'), may hold values from -0.21875 to 0.21875
- pair_amps: bfloat16 [128, 16, 2304], P('aa', 'ba'), may hold values from -0.875 to 0.875
- coulomb_occ: bfloat16 [48, 2304], replicated, may hold values from -6 to 6
- eps_occ: float32 [48], replicated, may hold values from -2 to -0.5
- eps_vir: float32 [768], replicated, may hold values from 0.2 to 3
- c_index: int32 [1], replicated, may hold values from 0 to 767
- a_index: int32 [128], P('aa'), may hold values from 0 to 767
- b_index: int32 [16], P('ba'), may hold values from 0 to 767
Outputs:
- gamma_vo: float32 [128, 48, 4096], P('aa', None, 'ba')
- vir_density: float32 [128, 8], P('aa')
All inputs are finite; a program needn't handle non-finite values.
Results may differ from a plain program's by a relative error of at most 0.0026.
Values may be sent and summed in bfloat16 or wider, within the bound.
No kernel may reach another device: no remote copies, remote signals or barrier semaphores. Data moves between devices by JAX's collectives and lax.ppermute only.
A program may use at most 64 MiB of HBM per device.

v0:
```python
import jax
import jax.numpy as jnp
from jax import lax
from jax.sharding import PartitionSpec as P


def lookup_energy(indices, table):
    labels = lax.broadcasted_iota(jnp.int32, (indices.shape[0], table.shape[0]), 1)
    return jnp.sum(jnp.where(indices[:, None] == labels, table[None, :], 0.0), axis=1)


def contract_last(left, right):
    return lax.dot_general(
        left, right, (((1,), (1,)), ((), ())), preferred_element_type=jnp.float32
    )


def body(
    b_vo, b_vv, amplitudes, pair_amps, coulomb_occ, eps_occ, eps_vir, c_index, a_index, b_index
):
    count_a, occupied, aux_all = b_vo.shape
    count_b, virtuals, aux_piece = b_vv.shape
    pair_cols = amplitudes.shape[1]
    vo_rows = b_vo.reshape(count_a * occupied, aux_all)
    piece = lax.all_gather(b_vv, "aa", axis=2, tiled=True)
    width = piece.shape[2]
    integrals = contract_last(vo_rows, piece.reshape(count_b * virtuals, width))
    x_rows = integrals.astype(jnp.bfloat16).reshape(count_a, occupied, count_b, virtuals)
    x_rows = x_rows.transpose(0, 2, 1, 3).reshape(count_a * count_b * occupied, virtuals)
    hole_term = jnp.dot(
        pair_amps.reshape(count_a * count_b * occupied, occupied),
        coulomb_occ,
        preferred_element_type=jnp.float32,
    )
    amp_whole = lax.all_gather(amplitudes, "ba", axis=0, tiled=True)
    triples = jnp.dot(x_rows, amp_whole, preferred_element_type=jnp.float32) - hole_term
    occ_three = (eps_occ[:, None, None] + eps_occ[None, :, None] + eps_occ[None, None, :]).reshape(
        occupied, pair_cols
    )
    energy_a = lookup_energy(a_index, eps_vir)
    energy_b = lookup_energy(b_index, eps_vir)
    energy_c = lookup_energy(c_index, eps_vir)[0]
    denom = (
        occ_three[None, None]
        - energy_a[:, None, None, None]
        - energy_b[None, :, None, None]
        - energy_c
    )
    ratio = (triples.reshape(count_a, count_b, occupied, pair_cols) / denom).astype(jnp.bfloat16)
    partial_density = jnp.einsum("abiq,cbiq->ac", ratio, ratio, preferred_element_type=jnp.float32)
    total_b = count_b * lax.axis_size("ba")
    density = lax.psum(partial_density, "ba") / (total_b * occupied * occupied)
    ratio_rows = ratio.reshape(count_a * count_b * occupied, pair_cols)
    left = contract_last(ratio_rows, amp_whole)
    left = left.astype(jnp.bfloat16).reshape(count_a, count_b, occupied, virtuals)
    left = left.transpose(0, 2, 1, 3).reshape(count_a * occupied, count_b * virtuals)
    piece = lax.all_gather(b_vv, "aa", axis=2, tiled=True)
    gamma_terms = jnp.dot(
        left, piece.reshape(count_b * virtuals, piece.shape[2]), preferred_element_type=jnp.float32
    )
    gamma = lax.psum_scatter(gamma_terms, "ba", scatter_dimension=1, tiled=True)
    return (gamma.reshape(count_a, occupied, gamma.shape[1]), density)


def solution(mesh):
    placed = (
        P("aa", None, None),
        P("ba", None, "aa"),
        P("ba", None),
        P("aa", "ba", None),
        P(),
        P(),
        P(),
        P(),
        P("aa"),
        P("ba"),
    )
    return jax.shard_map(
        body,
        mesh=mesh,
        in_specs=placed,
        out_specs=(P("aa", None, "ba"), P("aa", None)),
        check_vma=False,
    )
```

profile of v0, /device:TPU:96, one launch (start us, length us, event | category | flops | bytes accessed | tf_op | source)
XLA Modules:
  0.0 363.6 jit_solution(17432830512840726130)
XLA Ops:
  7.2 0.0 copy-start
  7.2 0.0 copy-start.2
  7.2 0.0 all-gather.5.cloned.1.call-start
  7.2 0.7 all-gather.5.cloned.1.call-update
  7.9 0.0 all-gather.3.cloned.1.call-start
  8.0 0.7 all-gather.3.cloned.1.call-update
  8.7 0.0 reduce-scatter.2.cloned.1.call-start
  10.0 0.9 select_reduce_fusion
  10.9 0.1 sub.86
  11.0 0.1 sub.87
  11.0 0.1 broadcast_reduce_fusion
  11.1 0.1 sub.77
  11.2 0.7 add.44
  11.9 0.1 add.48
  12.0 0.9 reshape.118
  12.9 0.8 broadcast_add_fusion.1
  13.7 1.4 add.46
  15.1 2.5 add.47
  17.6 0.0 copy-done.2
  17.6 0.7 select_reduce_fusion.2
  18.3 1.8 broadcast_add_fusion
  20.1 50.0 %all-gather.5.cloned.1.call-done = bf16[768,2304]{1,0:T(8,128)(2,1)} async-done(((bf16[48,2304]{1,0:T(8,128)(2,1)}), bf16[768,2304]{1,0:T(8,128)(2,1)}) %all-gather.5.cloned.1.call-update) | async-done | bytes 3538960 | tf_op jit(solution)/shard_map/all_gather | solution.py:35
  70.1 153.7 %all-gather.3.cloned.1.call-done = bf16[1,768,4096]{2,1,0:T(8,128)(2,1)} async-done(((bf16[1,768,256]{2,1,0:T(8,128)(2,1)}), bf16[1,768,4096]{2,1,0:T(8,128)(2,1)}) %all-gather.3.cloned.1.call-update) | async-done | bytes 6291472 | tf_op jit(solution)/shard_map/all_gather | solution.py:25
  223.8 0.0 copy-done
  223.8 0.0 copy-start.1
  223.8 11.1 %fusion.21 = f32[384,2304]{1,0:T(8,128)} fusion(bf16[768,2304]{1,0:T(8,128)(2,1)} %all-gather.5.cloned.1.call-done, bf16[384,4096]{1,0:T(8,128)(2,1)S(1)} %bitcast.46, bf16[1,768,4096]{2,1,0:T(8,128)(2,1)} %all-gather.3.cloned.1.call-done), kind=kOutput, calls=%fused_computation.20 | convolution fusion | flops 3775168512 | bytes 16515072 | tf_op jit(solution)/shard_map/dot_general | solution.py:36
  234.9 0.0 copy-done.1
  234.9 6.9 %fusion.11 = (bf16[384,2304]{1,0:T(8,128)(2,1)}, bf16[384,2304]{1,0:T(8,128)(2,1)}) fusion(f32[384]{0:T(512)S(1)} %sub.87, f32[48,2304]{1,0:T(8,128)} %broadcast_add_fusion, f32[]{:T(128)} %get-tuple-element.3, f32[]{:T(128)} %get-tuple-element.2, f32[384]{0:T(512)S(1)} %sub.77, f32[384,2304]{1,0:T(8,128)} %fusion.21, bf16[384,48]{1,0:T(8,128)(2,1)S(1)} %reshape.118, ...), kind=kOutput, calls=%fused_computation.14 | convolution fusion | flops 94666752 | bytes 7781384 | tf_op jit(solution)/shard_map/dot_general | solution.py:30
  241.7 11.5 %fusion = f32[384,4096]{1,0:T(8,128)} fusion(bf16[1,768,4096]{2,1,0:T(8,128)(2,1)} %all-gather.3.cloned.1.call-done, bf16[384,2304]{1,0:T(8,128)(2,1)} %get-tuple-element.5, bf16[768,2304]{1,0:T(8,128)(2,1)} %all-gather.5.cloned.1.call-done), kind=kOutput, calls=%fused_computation | convolution fusion | flops 3775168512 | bytes 17891328 | tf_op jit(solution)/shard_map/dot_general | solution.py:58
  253.3 0.0 reduce-scatter.2.cloned.1.call-update
  253.3 3.9 %fusion.17 = f32[8,8]{1,0:T(8,128)S(1)} fusion(bf16[8,48,2304]{2,1,0:T(8,128)(2,1)} %bitcast.47), kind=kOutput, calls=%fused_computation.19 | convolution fusion | flops 14155776 | bytes 1769728 | tf_op jit(solution)/shard_map/abiq,cbiq->ac/dot_general | solution.py:50
  257.2 33.5 %psum.7 = f32[8,8]{1,0:T(8,128)S(1)} all-reduce(f32[8,8]{1,0:T(8,128)S(1)} %fusion.17), channel_id=1, replica_groups=mesh['aa'=16,'ba'=16] {'ba'}, use_global_device_ids=true, to_apply=%region_4.5 | all-reduce | flops 64 | bytes 512 | tf_op jit(solution)/shard_map/psum | solution.py:52
  290.8 0.6 broadcast_multiply_fusion
  291.4 65.7 %reduce-scatter.2.cloned.1.call-done = f32[384,256]{1,0:T(8,128)} async-done(((f32[384,4096]{1,0:T(8,128)}), f32[384,256]{1,0:T(8,128)}) %reduce-scatter.2.cloned.1.call-update) | async-done | bytes 393232 | tf_op jit(solution)/shard_map/reduce_scatter | solution.py:61
Async XLA Ops:
  7.2 216.6 %copy-start = (bf16[8,48,4096]{2,1,0:T(8,128)(2,1)S(1)}, bf16[8,48,4096]{2,1,0:T(8,128)(2,1)}, u32[]{:S(2)}) copy-start(bf16[8,48,4096]{2,1,0:T(8,128)(2,1)} %param.10) | copy-start | bytes 9437188
  7.2 10.4 %copy-start.2 = (f32[768]{0:T(1024)S(1)}, f32[768]{0:T(1024)}, u32[]{:S(2)}) copy-start(f32[768]{0:T(1024)} %param.16) | copy-start | bytes 9220
  7.2 62.9 %all-gather.5.cloned.1.call-start = ((), (), s32[]{:S(2)}) async-start(), calls=%async_computation.2 | async-start | bytes 3760128 | tf_op jit(solution)/shard_map/all_gather | solution.py:35
  7.9 215.9 %all-gather.3.cloned.1.call-start = ((), (), s32[]{:S(2)}) async-start(), calls=%async_computation.1 | async-start | bytes 6684672 | tf_op jit(solution)/shard_map/all_gather | solution.py:25
  8.7 348.4 %reduce-scatter.2.cloned.1.call-start = ((), (), s32[]{:S(2)}) async-start(), calls=%async_computation.3 | async-start | bytes 6684672 | tf_op jit(solution)/shard_map/reduce_scatter | solution.py:61
  223.8 11.1 %copy-start.1 = (bf16[48,2304]{1,0:T(8,128)(2,1)S(1)}, bf16[48,2304]{1,0:T(8,128)(2,1)}, u32[]{:S(2)}) copy-start(bf16[48,2304]{1,0:T(8,128)(2,1)} %param.14) | copy-start | bytes 663556
Sparse Core Ops, SparseCore 0:
  10.8 59.2 all-gather.4
  71.8 151.9 all-gather.2
  253.4 103.5 reduce-scatter.1
where the time goes:
time: 365 us; the launch traced here: 364 us
  waiting for transfers between devices  271 us (74%)
  blocking collectives  33.5 us (9%)
  matrix products  33.4 us (9%)
  between operations  15.1 us (4%)
  local copies, waits for them, and re-layouts  5.89 us (2%)
  other arithmetic  4.78 us (1%)
    all_gather x1, waiting for transfers between devices, body(): piece = lax.all_gather(b_vv, 'aa', axis=2, tiled=True)  154 us
    reduce_scatter x1, waiting for transfers between devices, body(): gamma = lax.psum_scatter(gamma_terms, 'ba', scatter_dimension=1, tiled=True)  65.7 us
    all_gather x1, waiting for transfers between devices, body(): amp_whole = lax.all_gather(amplitudes, 'ba', axis=0, tiled=True)  50 us
    psum x1, blocking collectives, body(): density = lax.psum(partial_density, 'ba') / (total_b * occupied * occupied)  33.5 us
    dot_general x1, matrix products, body(): jnp.dot(left, piece.reshape(count_b * virtuals, piece.shape[2]), preferre...  11.5 us
    dot_general x1, matrix products, body(): jnp.dot(x_rows, amp_whole, preferred_element_type=jnp.float32) - hole_term  11.1 us
  transfers between devices with their start and end apart: 3, of which 3 were waited for; matrix products, arithmetic and copies ran while one was open for 4% of the time, Pallas kernels for 0%

commit v1 on v0

v1 whole, which is shorter than its diff:
```python
import functools

import jax
import jax.numpy as jnp
from jax import lax
from jax.experimental import pallas as pl
from jax.experimental.pallas import tpu as pltpu
from jax.sharding import PartitionSpec as P

NZ = 8
NY = 4
RANKS = 16
VMEM_LIMIT = 52 * 1024 * 1024
TILE = 768
NT = (((1,), (1,)), ((), ()))


def shift_perm(step):
    return [(i, (i + step) % RANKS) for i in range(RANKS)]


def swap_perm(bit):
    return [(i, i ^ bit) for i in range(RANKS)]


def along_z(x, step):
    return lax.ppermute(x, "aa", shift_perm(2 * step))


def swap_x_lo(x):
    return lax.ppermute(x, "aa", swap_perm(1))


def along_y(x, step):
    return lax.ppermute(x, "ba", shift_perm(4 * step))


def swap_x_hi(x):
    return lax.ppermute(x, "ba", swap_perm(2))


def swap_core(x):
    return lax.ppermute(x, "ba", swap_perm(1))


def together(*arrays):
    return lax.optimization_barrier(arrays)


VMEM = pl.BlockSpec(memory_space=pltpu.VMEM)
SMEM = pl.BlockSpec(memory_space=pltpu.SMEM)
HBM = pl.BlockSpec(memory_space=pltpu.HBM)


def where_am_i():
    aa, ba = lax.axis_index("aa"), lax.axis_index("ba")
    z, x_lo = aa // 2, aa % 2
    y, x_hi, core = ba // 4, (ba // 2) % 2, ba % 2
    return z, x_lo, y, x_hi, core


def column_start(place, width):
    z, x_lo = where_am_i()[:2]
    column = (z + place % NZ) % NZ * 2 + (x_lo if place < NZ else 1 - x_lo)
    return pl.multiple_of(column * width, width)


def fetch(pairs, sems):
    copies = [pltpu.make_async_copy(*pair, sems.at[n]) for n, pair in enumerate(pairs)]
    for copy in copies:
        copy.start()
    return copies


def fetch_columns(places, a_ref, a_buf, sems):
    width = a_buf.shape[2]
    columns = [pl.ds(column_start(place, width), width) for place in places]
    return fetch([(a_ref.at[:, c], a_buf.at[n]) for n, c in enumerate(columns)], sems)


def terms_kernel(a_index_ref, b_index_ref, c_index_ref, table_ref, eps_ref, row_ref, col_ref):
    occupied = eps_ref.shape[1]
    along = lambda axis, shape: lax.broadcasted_iota(jnp.int32, shape, axis)
    square = (occupied, occupied)
    eps = jnp.sum(
        jnp.where(along(0, square) == along(1, square), eps_ref[...], 0.0), axis=1, keepdims=True
    )
    energy_b, energy_c = table_ref[b_index_ref[0]], table_ref[c_index_ref[0]]
    for n in range(a_index_ref.shape[0]):
        row_ref[n * occupied : (n + 1) * occupied] = (
            eps - table_ref[a_index_ref[n]] - energy_b - energy_c
        )
    wide = (occupied, col_ref.shape[1])
    picked = lambda labels: jnp.sum(
        jnp.where(along(0, wide) == labels, eps, 0.0), axis=0, keepdims=True
    )
    col_ref[...] = picked(along(1, wide) // occupied) + picked(along(1, wide) % occupied)


def energy_terms(tables):
    occupied = tables[-1].shape[1]
    return pl.pallas_call(
        terms_kernel,
        out_shape=(
            jax.ShapeDtypeStruct((tables[0].shape[0] * occupied, 1), jnp.float32),
            jax.ShapeDtypeStruct((1, occupied * occupied), jnp.float32),
        ),
        in_specs=[SMEM] * 4 + [VMEM],
        out_specs=(VMEM, VMEM),
        compiler_params=pltpu.CompilerParams(vmem_limit_bytes=VMEM_LIMIT),
    )(*tables)


def add_kernel(places, first, a_ref, *refs):
    count = len(places)
    pieces, rest = refs[:count], refs[count:]
    if not first:
        before_ref, rest = rest[0], rest[2:]
    out_ref, stack_ref, a_buf, a_sems, p_buf, p_sems, sems = rest
    copies = fetch_columns(places, a_ref, a_buf, a_sems)
    loads = fetch([(piece, p_buf.at[n]) for n, piece in enumerate(pieces)], p_sems)
    stores = []
    for n, place in enumerate(places):
        loads[n].wait()
        store = pltpu.make_async_copy(p_buf.at[n], stack_ref.at[place], sems.at[n])
        store.start()
        stores.append(store)
        copies[n].wait()
        terms = lax.dot_general(a_buf[n], p_buf[n], NT, preferred_element_type=jnp.float32)
        if n:
            out_ref[...] += terms
        else:
            out_ref[...] = terms if first else before_ref[...] + terms
    for store in stores:
        store.wait()


def add_products(places, pieces, a, before):
    rows = a.shape[0]
    virtuals, width = pieces[0].shape
    first = before is None
    count = len(pieces)
    return pl.pallas_call(
        functools.partial(add_kernel, places, first),
        out_shape=(
            jax.ShapeDtypeStruct((rows, virtuals), jnp.float32),
            jax.ShapeDtypeStruct((2 * NZ, virtuals, width), pieces[0].dtype),
        ),
        in_specs=[HBM] * (1 + count) + ([] if first else [VMEM, HBM]),
        out_specs=(VMEM, HBM),
        scratch_shapes=[
            pltpu.VMEM((count, rows, width), a.dtype),
            pltpu.SemaphoreType.DMA((count,)),
            pltpu.VMEM((count, virtuals, width), a.dtype),
            pltpu.SemaphoreType.DMA((count,)),
            pltpu.SemaphoreType.DMA((count,)),
        ],
        input_output_aliases={} if first else {2 + count: 1},
        compiler_params=pltpu.CompilerParams(vmem_limit_bytes=VMEM_LIMIT),
        cost_estimate=pl.CostEstimate(
            flops=2 * rows * virtuals * width * count,
            bytes_accessed=2 * virtuals * width * count,
            transcendentals=0,
        ),
    )(a, *pieces, *([] if first else before))


def gather_pieces(piece, amplitudes, pair_rows, a, tables):
    own, other = {0: piece}, {}
    get = lambda n: other[n - NZ] if n >= NZ else own[n]
    add = lambda places, before=None: add_products(places, [get(n) for n in places], a, before)
    own[7], own[1], other[0], amp_hi = together(
        along_z(piece, 1), along_z(piece, -1), swap_x_lo(piece), swap_x_hi(amplitudes)
    )
    amp_own = lax.all_gather(
        jnp.stack([amplitudes, amp_hi]),
        "ba",
        axis=0,
        axis_index_groups=[[n + 4 * m for m in range(NY)] for n in range(4)],
    )
    sums = add([0, 1, 7, NZ])
    own[6], own[2], other[1], sums, pair_rows = together(
        along_z(own[7], 1), along_z(own[1], -1), swap_x_lo(own[1]), sums, pair_rows
    )
    sums = add([2, 6, NZ + 1], sums)
    own[5], own[3], other[7], sums, terms = together(
        along_z(own[6], 1), along_z(own[2], -1), swap_x_lo(own[7]), sums, energy_terms(tables)
    )
    sums = add([3, 5, NZ + 7], sums)
    own[4], other[2], other[3], sums, amp_own = together(
        along_z(own[5], 1), along_z(other[1], -1), swap_x_lo(own[3]), sums, amp_own
    )
    amp_other = swap_core(amp_own)
    other[6], other[4], other[5] = (
        along_z(other[7], 1), along_z(other[3], -1), swap_x_lo(own[5])
    )
    sums, stack = add([4, NZ + 2, NZ + 3], sums)
    late = [NZ + 4, NZ + 5, NZ + 6]
    return late, [get(n) for n in late], sums, stack, terms, pair_rows, amp_own, amp_other


def chosen_copies(goes, passed, stack_ref, buf, sems):
    z, x_lo, _, x_hi, core = where_am_i()
    first = jnp.where(x_lo == core, goes, 1 - goes) * NZ + (z + x_hi + passed) % 2
    return [
        pltpu.make_async_copy(stack_ref.at[first + 2 * j], buf.at[j], sems.at[j]) for j in range(NY)
    ]


def gamma_dots(left, waits, buf, out_ref):
    rows = left.shape[0]
    for j in range(NY):
        waits[j].wait()
        out_ref[j * rows : (j + 1) * rows] = jnp.dot(
            left, buf[j], preferred_element_type=jnp.float32
        )


def middle_kernel(late, a_ref, *refs):
    count = len(late)
    pieces, (before_ref, row_ref, col_ref, pair_ref, coulomb_ref), rest = (
        refs[:count], refs[count : count + 5], refs[count + 5 :]
    )
    amp_own_ref, amp_other_ref, _, stack_ref, left_ref, keep_ref, sent_ref, *rest = rest
    a_buf, a_sems, p_buf, p_sems, sems, total, gram = rest[:7]
    keep_buf, keep_sems, sent_buf, sent_sems, amp_ref, amp_sems = rest[7:]
    a_copies = fetch_columns(late, a_ref, a_buf, a_sems)
    loads = fetch([(piece, p_buf.at[n]) for n, piece in enumerate(pieces)], p_sems)
    _, _, _, x_hi, core = where_am_i()
    part = amp_own_ref.shape[2]
    amp_copies = []
    for n in range(NY):
        for other_hi in range(2):
            for other_core, ref in enumerate((amp_own_ref, amp_other_ref)):
                hi = 1 - x_hi if other_hi else x_hi
                owner = (n * 2 + hi) * 2 + (1 - core if other_core else core)
                target = amp_ref.at[pl.ds(pl.multiple_of(owner * part, part), part)]
                amp_copies.append((ref.at[n, other_hi], target))
    amp_copies = fetch(amp_copies, amp_sems)
    stores = []
    products = before_ref[...]
    for n, place in enumerate(late):
        loads[n].wait()
        store = pltpu.make_async_copy(p_buf.at[n], stack_ref.at[place], sems.at[n])
        store.start()
        stores.append(store)
        a_copies[n].wait()
        products += lax.dot_general(a_buf[n], p_buf[n], NT, preferred_element_type=jnp.float32)
    x = products.astype(jnp.bfloat16)
    for store in stores:
        store.wait()
    sent_copies = chosen_copies(1, 1, stack_ref, sent_buf, sent_sems)
    keep_copies = chosen_copies(0, 1, stack_ref, keep_buf, keep_sems)
    for copy in amp_copies:
        copy.wait()
    for copy in sent_copies + keep_copies:
        copy.start()
    tiles = [slice(n, n + TILE) for n in range(0, amp_ref.shape[1], TILE)]
    for n, tile in enumerate(tiles):
        triples = jnp.dot(
            x, amp_ref[:, tile], preferred_element_type=jnp.float32
        ) - jnp.dot(pair_ref[...], coulomb_ref[:, tile], preferred_element_type=jnp.float32)
        ratio = (triples / (row_ref[...] + col_ref[:, tile])).astype(jnp.bfloat16)
        terms = lax.dot_general(ratio, amp_ref[:, tile], NT, preferred_element_type=jnp.float32)
        pairs = lax.dot_general(ratio, ratio, NT, preferred_element_type=jnp.float32)
        if n == 0:
            total[...] = terms
            gram[...] = pairs
        else:
            total[...] += terms
            gram[...] += pairs
    left_ref[...] = total[...].astype(left_ref.dtype)

    gamma_dots(left_ref[...], sent_copies, sent_buf, sent_ref)
    gamma_dots(left_ref[...], keep_copies, keep_buf, keep_ref)

    rows, occupied = pair_ref.shape
    width = keep_ref.shape[1]
    count = rows // occupied
    block = (occupied, rows)
    same = lax.broadcasted_iota(jnp.int32, block, 0) == lax.broadcasted_iota(jnp.int32, block, 1) % occupied
    picked = jnp.concatenate(
        [
            jnp.where(same, gram[n * occupied : (n + 1) * occupied], 0.0).sum(0, keepdims=True)
            for n in range(count)
        ]
    )
    owner = lax.broadcasted_iota(jnp.int32, (rows, width), 0) // occupied
    place = lax.broadcasted_iota(jnp.int32, (rows, width), 1)
    density = jnp.dot(
        picked,
        jnp.where(owner == place, 1.0, 0.0),
        precision=lax.Precision.HIGHEST,
        preferred_element_type=jnp.float32,
    )
    for out_ref in (keep_ref, sent_ref):
        out_ref[NY * rows : NY * rows + count] = density
        out_ref[NY * rows + count :] = jnp.zeros((16 - count, width), jnp.float32)


def middle(late, pieces, a, sums, stack, terms, pair_rows, coulomb, amp_own, amp_other):
    rows, virtuals = sums.shape
    width = pieces[0].shape[1]
    pair_cols = coulomb.shape[1]
    count = len(late)
    block = jax.ShapeDtypeStruct((NY * rows + 16, width), jnp.float32)
    buf = pltpu.VMEM((NY, virtuals, width), jnp.bfloat16)
    return pl.pallas_call(
        functools.partial(middle_kernel, late),
        out_shape=(
            jax.ShapeDtypeStruct(stack.shape, stack.dtype),
            jax.ShapeDtypeStruct((rows, virtuals), jnp.bfloat16),
            block,
            block,
        ),
        in_specs=[HBM] * (1 + count) + [VMEM] * 5 + [HBM] * 3,
        out_specs=(HBM, VMEM, VMEM, VMEM),
        scratch_shapes=[
            pltpu.VMEM((count, rows, width), a.dtype),
            pltpu.SemaphoreType.DMA((count,)),
            pltpu.VMEM((count, virtuals, width), a.dtype),
            pltpu.SemaphoreType.DMA((count,)),
            pltpu.SemaphoreType.DMA((count,)),
            pltpu.VMEM((rows, virtuals), jnp.float32),
            pltpu.VMEM((rows, rows), jnp.float32),
            buf,
            pltpu.SemaphoreType.DMA((NY,)),
            buf,
            pltpu.SemaphoreType.DMA((NY,)),
            pltpu.VMEM((virtuals, pair_cols), jnp.bfloat16),
            pltpu.SemaphoreType.DMA((RANKS,)),
        ],
        input_output_aliases={1 + count + 7: 0},
        compiler_params=pltpu.CompilerParams(vmem_limit_bytes=VMEM_LIMIT),
    )(a, *pieces, sums, *terms, pair_rows, coulomb, amp_own, amp_other, stack)


def rest_kernel(left_ref, stack_ref, keep_ref, sent_ref, keep_buf, keep_sems, sent_buf, sent_sems):
    sent_copies = chosen_copies(1, 0, stack_ref, sent_buf, sent_sems)
    keep_copies = chosen_copies(0, 0, stack_ref, keep_buf, keep_sems)
    for copy in sent_copies + keep_copies:
        copy.start()
    gamma_dots(left_ref[...], sent_copies, sent_buf, sent_ref)
    gamma_dots(left_ref[...], keep_copies, keep_buf, keep_ref)


def gamma_rest(left, stack):
    rows, virtuals = left.shape
    width = stack.shape[2]
    block = jax.ShapeDtypeStruct((NY * rows, width), jnp.float32)
    buf = pltpu.VMEM((NY, virtuals, width), jnp.bfloat16)
    return pl.pallas_call(
        rest_kernel,
        out_shape=(block, block),
        in_specs=[VMEM, HBM],
        out_specs=(VMEM, VMEM),
        scratch_shapes=[buf, pltpu.SemaphoreType.DMA((NY,))] * 2,
        compiler_params=pltpu.CompilerParams(vmem_limit_bytes=VMEM_LIMIT),
        cost_estimate=pl.CostEstimate(
            flops=4 * rows * virtuals * width * NY,
            bytes_accessed=4 * virtuals * width * NY,
            transcendentals=0,
        ),
    )(left, stack)


def two_parts(values):
    high = values.astype(jnp.bfloat16)
    return high, (values - high.astype(jnp.float32)).astype(jnp.bfloat16)


def route_kernel(with_density, kept_ref, recv_ref, mine_ref, *refs):
    messages = refs[:3]
    rows = mine_ref.shape[0]
    z, _, y, x_hi, _ = where_am_i()
    odd = (z + x_hi + with_density) % 2
    for j in range(NY):
        away = ((z + 2 * j + odd) % NZ // 2 - y + NY) % NY
        part = slice(j * rows, (j + 1) * rows)
        terms = kept_ref[part] + recv_ref[part]
        for n, ref in enumerate((mine_ref, *messages)):
            @pl.when(away == n)
            def _():
                ref[:rows] = terms.astype(ref.dtype)

    if with_density:
        density = kept_ref[NY * rows :] + recv_ref[NY * rows :]
        refs[3][...] = density
        high, low = two_parts(density)
        for ref in messages:
            ref[rows : rows + 16] = high
            ref[rows + 16 :] = low


def route(rows, kept, received, with_density):
    width = kept.shape[1]
    message = jax.ShapeDtypeStruct((rows + 32 * with_density, width), jnp.bfloat16)
    out = [jax.ShapeDtypeStruct((rows, width), jnp.float32)] + [message] * 3
    if with_density:
        out.append(jax.ShapeDtypeStruct((16, width), jnp.float32))
    return pl.pallas_call(
        functools.partial(route_kernel, with_density),
        out_shape=out,
        in_specs=[VMEM, VMEM],
        out_specs=[VMEM] * len(out),
        compiler_params=pltpu.CompilerParams(vmem_limit_bytes=VMEM_LIMIT),
    )(kept, received)


def wide(ref, first, rows):
    return ref[first : first + rows].astype(jnp.float32)


def passed_kernel(mine_ref, density_ref, a_ref, b_ref, c_ref, send_ref, kept_ref):
    rows = mine_ref.shape[0]
    arrived = (a_ref, b_ref, c_ref)
    total = mine_ref[...] + sum(wide(ref, 0, rows) for ref in arrived)
    send_ref[:rows] = total.astype(send_ref.dtype)
    density = density_ref[...]
    for ref in arrived:
        density += wide(ref, rows, 16) + wide(ref, rows + 16, 16)
    kept_ref[...] = density
    high, low = two_parts(density)
    send_ref[rows : rows + 16] = high
    send_ref[rows + 16 :] = low


def passed_sum(mine, density, arrived):
    rows, width = mine.shape
    return pl.pallas_call(
        passed_kernel,
        out_shape=(
            jax.ShapeDtypeStruct((rows + 32, width), jnp.bfloat16),
            jax.ShapeDtypeStruct(density.shape, jnp.float32),
        ),
        in_specs=[VMEM] * 5,
        out_specs=(VMEM,) * 2,
        compiler_params=pltpu.CompilerParams(vmem_limit_bytes=VMEM_LIMIT),
    )(mine, density, *arrived)


def last_kernel(scale, mine_ref, a_ref, b_ref, c_ref, density_ref, recv_ref, gamma_ref, out_ref):
    rows = mine_ref.shape[0]
    total = mine_ref[...] + sum(wide(ref, 0, rows) for ref in (a_ref, b_ref, c_ref))
    gamma_ref[...] = total + wide(recv_ref, 0, rows)
    arrived = wide(recv_ref, rows, 16) + wide(recv_ref, rows + 16, 16)
    out_ref[...] = (density_ref[...] + arrived) / scale


def last_sum(scale, mine, arrived, density, received):
    return pl.pallas_call(
        functools.partial(last_kernel, scale),
        out_shape=(
            jax.ShapeDtypeStruct(mine.shape, jnp.float32),
            jax.ShapeDtypeStruct(density.shape, jnp.float32),
        ),
        in_specs=[VMEM] * 6,
        out_specs=(VMEM, VMEM),
        compiler_params=pltpu.CompilerParams(vmem_limit_bytes=VMEM_LIMIT),
    )(mine, *arrived, density, received)


def to_owners(messages):
    one, two, three = messages
    return along_y(one, 1), along_y(two, 2), along_y(three, -1)


def body(
    b_vo, b_vv, amplitudes, pair_amps, coulomb_occ, eps_occ, eps_vir, c_index, a_index, b_index
):
    count_a, occupied, aux_all = b_vo.shape
    rows = count_a * occupied
    virtuals = b_vv.shape[1]
    pair_cols = amplitudes.shape[1]
    vo_rows = b_vo.reshape(rows, aux_all)
    tables = (a_index, b_index, c_index, eps_vir, eps_occ.reshape(1, occupied))
    late, pieces, sums, stack, terms, pair_rows, amp_own, amp_other = gather_pieces(
        b_vv[0], amplitudes, pair_amps.reshape(rows, occupied), vo_rows, tables
    )
    stack, left, keep_b, sent_b = middle(
        late, pieces, vo_rows, sums, stack, terms, pair_rows, coulomb_occ, amp_own, amp_other
    )
    came_b, left = together(swap_core(sent_b), left)
    keep_a, sent_a = gamma_rest(left, stack)
    came_a = swap_core(sent_a)
    mine, *messages, density = route(rows, keep_b, came_b, True)
    arrived = to_owners(messages)
    mine_keep, *messages = route(rows, keep_a, came_a, False)
    arrived_keep = to_owners(messages)
    send, density = passed_sum(mine, density, arrived)
    scale = lax.axis_size("ba") * occupied * occupied
    gamma, density = last_sum(scale, mine_keep, arrived_keep, density, swap_x_hi(send))
    return gamma.reshape(count_a, occupied, gamma.shape[1]), density[:count_a, :count_a]


def solution(mesh):
    placed = (
        P("aa", None, None),
        P("ba", None, "aa"),
        P("ba", None),
        P("aa", "ba", None),
        P(),
        P(),
        P(),
        P(),
        P("aa"),
        P("ba"),
    )
    return jax.shard_map(
        body,
        mesh=mesh,
        in_specs=placed,
        out_specs=(P("aa", None, "ba"), P("aa", None)),
        check_vma=False,
    )
```

time: 365 us -> 149 us (0.41)
  waiting for transfers between devices: 271 us -> 48.7 us
  Pallas kernels: 0 us -> 45.3 us
  blocking collectives: 33.5 us -> 0 us
  matrix products: 33.4 us -> 0 us
  starting transfers between devices: 0.11 us -> 32.1 us
    all_gather x2 -> x1, waiting for transfers between devices: 204 us -> 0.01 us  [gather_pieces(): lax.all_gather(jnp.stack([amplitudes, amp_hi]), 'ba', axis=0, axis_index_...]
    reduce_scatter x1 -> x0, waiting for transfers between devices: 65.7 us -> none  [body(): gamma = lax.psum_scatter(gamma_terms, 'ba', scatter_dimension=1, tiled=True)]
    ppermute x0 -> x26, waiting for transfers between devices: none -> 48.6 us  [the longest x6 15.9 us: along_y(): return lax.ppermute(x, 'ba', shift_perm(4 * step))]
    pallas_call x0 -> x11, Pallas kernels: none -> 45.3 us  [the longest x4 18.4 us: add_products(): pl.pallas_call(functools.partial(add_kernel, places, first), out_shape=(j...]
    psum x1 -> x0, blocking collectives: 33.5 us -> none  [body(): density = lax.psum(partial_density, 'ba') / (total_b * occupied * occupied)]
    dot_general x4 -> x0, matrix products: 33.4 us -> none  [the longest x1 11.5 us: body(): jnp.dot(left, piece.reshape(count_b * virtuals, piece.shape[2]), preferre...]
    ppermute x0 -> x26, starting transfers between devices: none -> 32 us  [the longest x6 11.2 us: along_y(): return lax.ppermute(x, 'ba', shift_perm(4 * step))]
    add x4 -> x0, local copies, waits for them, and re-layouts: 4.64 us -> none  [body(): eps_occ[:, None, None] + eps_occ[None, :, None] + eps_occ[None, None, :]]
  transfers between devices with their start and end apart: 3 -> 27, of which waited for: 3 -> 14; matrix products, arithmetic and copies ran while one was open for 4% -> 1% of each run, Pallas kernels for 0% -> 16%
where the time goes in v1:
time: 149 us
  waiting for transfers between devices  48.7 us (33%)
  Pallas kernels  45.3 us (30%)
  starting transfers between devices  32.1 us (22%)
  between operations  15.5 us (10%)
  local copies, waits for them, and re-layouts  5.43 us (4%)
  other arithmetic  1.74 us (1%)
    pallas_call x4, Pallas kernels, add_products(): pl.pallas_call(functools.partial(add_kernel, places, first), out_shape=(j...  18.4 us
    ppermute x6, waiting for transfers between devices, along_y(): return lax.ppermute(x, 'ba', shift_perm(4 * step))  15.9 us
    pallas_call x1, Pallas kernels, middle(): pl.pallas_call(functools.partial(middle_kernel, late), out_shape=(jax.Sha...  14.7 us
    ppermute x10, waiting for transfers between devices, along_z(): return lax.ppermute(x, 'aa', shift_perm(2 * step))  11.4 us
    ppermute x6, starting transfers between devices, along_y(): return lax.ppermute(x, 'ba', shift_perm(4 * step))  11.2 us
    ppermute x10, starting transfers between devices, along_z(): return lax.ppermute(x, 'aa', shift_perm(2 * step))  10.7 us
    ppermute x2, waiting for transfers between devices, swap_x_hi(): return lax.ppermute(x, 'ba', swap_perm(2))  10.5 us
    ppermute x5, waiting for transfers between devices, swap_x_lo(): return lax.ppermute(x, 'aa', swap_perm(1))  7.2 us
  transfers between devices with their start and end apart: 27, of which 14 were waited for; matrix products, arithmetic and copies ran while one was open for 1% of the time, Pallas kernels for 16%

profile of v1, /device:TPU:96, one launch (start us, length us, event | category | flops | bytes accessed | tf_op | source)
XLA Modules:
  0.0 148.7 jit_solution(13608632597087941387)
XLA Ops:
  7.2 1.6 %collective-permute-start.2 = (bf16[768,256]{1,0:T(8,128)(2,1)}, bf16[768,256]{1,0:T(8,128)(2,1)S(1)}, u32[]{:S(2)}, u32[]{:S(2)}) collective-permute-start(bf16[768,256]{1,0:T(8,128)(2,1)} %bitcast.9), channel_id=1, source_target_pairs={{0,16},{16,0},{32,48},{48,32},{64,80},{80,64},{96,112},{112,96},{1... | collective-permute-start | bytes 1179656 | tf_op jit(solution)/shard_map/ppermute | solution.py:31
  8.9 3.1 %collective-permute-start = (bf16[768,256]{1,0:T(8,128)(2,1)}, bf16[768,256]{1,0:T(8,128)(2,1)S(1)}, u32[]{:S(2)}, u32[]{:S(2)}) collective-permute-start(bf16[768,256]{1,0:T(8,128)(2,1)} %bitcast.11), channel_id=1, source_target_pairs={{0,32},{16,48},{32,64},{48,80},{64,96},{80,112},{96,128},{112,144}... | collective-permute-start | bytes 1179656 | tf_op jit(solution)/shard_map/ppermute | solution.py:27
  12.0 2.7 %collective-permute-start.3 = (bf16[48,2304]{1,0:T(8,128)(2,1)}, bf16[48,2304]{1,0:T(8,128)(2,1)S(1)}, u32[]{:S(2)}, u32[]{:S(2)}) collective-permute-start(bf16[48,2304]{1,0:T(8,128)(2,1)} %param.12), channel_id=1, source_target_pairs={{0,2},{1,3},{2,0},{3,1},{4,6},{5,7},{6,4},{7,5},{8,10},{9,11},{10,... | collective-permute-start | bytes 663560 | tf_op jit(solution)/shard_map/ppermute | solution.py:39
  14.8 10.5 %collective-permute-done.3 = bf16[48,2304]{1,0:T(8,128)(2,1)S(1)} collective-permute-done((bf16[48,2304]{1,0:T(8,128)(2,1)}, bf16[48,2304]{1,0:T(8,128)(2,1)S(1)}, u32[]{:S(2)}, u32[]{:S(2)}) %collective-permute-start.3) | collective-permute-done | bytes 221216 | tf_op jit(solution)/shard_map/ppermute | solution.py:39
  25.3 1.7 %pad_maximum_fusion = bf16[2,48,2304]{2,1,0:T(8,128)(2,1)} fusion(bf16[1,48,2304]{2,1,0:T(8,128)(2,1)S(1)} %bitcast.22, bf16[1,48,2304]{2,1,0:T(8,128)(2,1)} %bitcast.21), kind=kLoop, calls=%fused_computation | loop fusion | flops 221184 | bytes 884736 | tf_op jit(solution)/shard_map/stack | solution.py:176
  27.1 3.2 %collective-permute-start.4 = (bf16[768,256]{1,0:T(8,128)(2,1)S(1)}, bf16[768,256]{1,0:T(8,128)(2,1)S(1)}, u32[]{:S(2)}, u32[]{:S(2)}) collective-permute-start(bf16[768,256]{1,0:T(8,128)(2,1)S(1)} %collective-permute-done.refs_2_), channel_id=1, source_target_pairs={{0,32},{16,48},{32,64},{48,80},{64,96},{80,112},{96,128},{112,144}... | collective-permute-start | bytes 1179656 | tf_op jit(solution)/shard_map/ppermute | solution.py:27
  30.5 0.9 reshape.17.refs_6_
  31.4 1.9 %collective-permute-start.9 = (bf16[768,256]{1,0:T(8,128)(2,1)S(1)}, bf16[768,256]{1,0:T(8,128)(2,1)S(1)}, u32[]{:S(2)}, u32[]{:S(2)}) collective-permute-start(bf16[768,256]{1,0:T(8,128)(2,1)S(1)} %collective-permute-done.refs_2_), channel_id=1, source_target_pairs={{0,16},{16,0},{32,48},{48,32},{64,80},{80,64},{96,112},{112,96},{1... | collective-permute-start | bytes 1179656 | tf_op jit(solution)/shard_map/ppermute | solution.py:31
  33.3 4.0 %shard_map.113 = (f32[384,768]{1,0:T(8,128)}, bf16[16,768,256]{2,1,0:T(8,128)(2,1)}) custom-call(bf16[384,4096]{1,0:T(8,128)(2,1)} %bitcast.14, bf16[768,256]{1,0:T(8,128)(2,1)S(1)} %bitcast.12, bf16[768,256]{1,0:T(8,128)(2,1)S(1)} %collective-permute-done.1.refs_1_, bf16[768,256]{1,0:T(8,128)(2,1)S(1)} %collective-permute-done.refs_2_, ...), custom_call_target="tpu_custom_call" | custom-call | flops 603979776 | bytes 1572864 | tf_op jit(solution)/shard_map/pallas_call | solution.py:143
  37.3 0.5 collective-permute-done.4.refs_1_
  37.8 4.5 %collective-permute-done.6.refs_2_ = bf16[768,256]{1,0:T(8,128)(2,1)S(1)} collective-permute-done((bf16[768,256]{1,0:T(8,128)(2,1)S(1)}, bf16[768,256]{1,0:T(8,128)(2,1)S(1)}, u32[]{:S(2)}, u32[]{:S(2)}) %collective-permute-start.6) | collective-permute-done | bytes 393248 | tf_op jit(solution)/shard_map/ppermute | solution.py:31
  42.3 1.0 collective-permute-start.7
  43.4 1.0 collective-permute-start.8
  45.7 0.9 shard_map.115
  46.7 4.8 %shard_map.114 = (f32[384,768]{1,0:T(8,128)}, bf16[16,768,256]{2,1,0:T(8,128)(2,1)}) custom-call(bf16[384,4096]{1,0:T(8,128)(2,1)} %bitcast.15, bf16[768,256]{1,0:T(8,128)(2,1)S(1)} %collective-permute-done.5.refs_0_, bf16[768,256]{1,0:T(8,128)(2,1)S(1)} %collective-permute-done.4.refs_1_, ...), custom_call_target="tpu_custom_call", output_to_operand_aliasing={{1}: (5, {})} | custom-call | flops 452984832 | bytes 1179648 | tf_op jit(solution)/shard_map/pallas_call | solution.py:143
  51.5 4.2 %collective-permute-done.8.refs_0_ = bf16[768,256]{1,0:T(8,128)(2,1)S(1)} collective-permute-done((bf16[768,256]{1,0:T(8,128)(2,1)S(1)}, bf16[768,256]{1,0:T(8,128)(2,1)S(1)}, u32[]{:S(2)}, u32[]{:S(2)}) %collective-permute-start.8) | collective-permute-done | bytes 393248 | tf_op jit(solution)/shard_map/ppermute | solution.py:27
  55.7 1.2 collective-permute-start.12
  56.9 4.9 %shard_map.116 = (f32[384,768]{1,0:T(8,128)}, bf16[16,768,256]{2,1,0:T(8,128)(2,1)}) custom-call(bf16[384,4096]{1,0:T(8,128)(2,1)} %bitcast.16, bf16[768,256]{1,0:T(8,128)(2,1)S(1)} %collective-permute-done.8.refs_0_, bf16[768,256]{1,0:T(8,128)(2,1)S(1)} %collective-permute-done.7.refs_1_, ...), custom_call_target="tpu_custom_call", output_to_operand_aliasing={{1}: (5, {})} | custom-call | flops 452984832 | bytes 1179648 | tf_op jit(solution)/shard_map/pallas_call | solution.py:143
  61.8 1.7 %collective-permute-done.12.refs_2_ = bf16[768,256]{1,0:T(8,128)(2,1)S(1)} collective-permute-done((bf16[768,256]{1,0:T(8,128)(2,1)S(1)}, bf16[768,256]{1,0:T(8,128)(2,1)S(1)}, u32[]{:S(2)}, u32[]{:S(2)}) %collective-permute-start.12) | collective-permute-done | bytes 393248 | tf_op jit(solution)/shard_map/ppermute | solution.py:31
  63.5 1.2 collective-permute-done.10.refs_0_
  64.6 1.3 collective-permute-start.15
  65.9 0.9 collective-permute-start.14
  66.8 0.8 collective-permute-start.13
  67.6 4.8 %shard_map.117 = (f32[384,768]{1,0:T(8,128)}, bf16[16,768,256]{2,1,0:T(8,128)(2,1)}) custom-call(bf16[384,4096]{1,0:T(8,128)(2,1)} %bitcast.17, bf16[768,256]{1,0:T(8,128)(2,1)S(1)} %collective-permute-done.10.refs_0_, bf16[768,256]{1,0:T(8,128)(2,1)S(1)} %collective-permute-done.11.refs_1_, ...), custom_call_target="tpu_custom_call", output_to_operand_aliasing={{1}: (5, {})} | custom-call | flops 452984832 | bytes 1179648 | tf_op jit(solution)/shard_map/pallas_call | solution.py:143
  72.4 3.8 %collective-permute-done.15.refs_2_ = bf16[768,256]{1,0:T(8,128)(2,1)S(1)} collective-permute-done((bf16[768,256]{1,0:T(8,128)(2,1)S(1)}, bf16[768,256]{1,0:T(8,128)(2,1)S(1)}, u32[]{:S(2)}, u32[]{:S(2)}) %collective-permute-start.15) | collective-permute-done | bytes 393248 | tf_op jit(solution)/shard_map/ppermute | solution.py:27
  76.2 0.9 collective-permute-done.14.refs_1_
  77.1 1.8 %collective-permute-done.13.refs_0_ = bf16[768,256]{1,0:T(8,128)(2,1)S(1)} collective-permute-done((bf16[768,256]{1,0:T(8,128)(2,1)S(1)}, bf16[768,256]{1,0:T(8,128)(2,1)S(1)}, u32[]{:S(2)}, u32[]{:S(2)}) %collective-permute-start.13) | collective-permute-done | bytes 393248 | tf_op jit(solution)/shard_map/ppermute | solution.py:27
  78.9 1.3 copy-done.6
  80.2 14.7 %shard_map.118 = (bf16[16,768,256]{2,1,0:T(8,128)(2,1)}, bf16[384,768]{1,0:T(8,128)(2,1)}, f32[1552,256]{1,0:T(8,128)}, f32[1552,256]{1,0:T(8,128)}) custom-call(bf16[384,4096]{1,0:T(8,128)(2,1)} %bitcast.18, bf16[768,256]{1,0:T(8,128)(2,1)S(1)} %collective-permute-done.13.refs_0_, ...), custom_call_target="tpu_custom_call", output_to_operand_aliasing={{0}: (11, {})} | custom-call | tf_op jit(solution)/shard_map/pallas_call | solution.py:308
  95.2 3.6 %collective-permute-done.17.recv_ref = f32[1552,256]{1,0:T(8,128)S(1)} collective-permute-done((f32[1552,256]{1,0:T(8,128)}, f32[1552,256]{1,0:T(8,128)S(1)}, u32[]{:S(2)}, u32[]{:S(2)}) %collective-permute-start.17) | collective-permute-done | bytes 1589280 | tf_op jit(solution)/shard_map/ppermute | solution.py:43
  98.9 1.5 copy-done
  100.3 6.0 %shard_map.119 = (f32[1536,256]{1,0:T(8,128)}, f32[1536,256]{1,0:T(8,128)}) custom-call(bf16[384,768]{1,0:T(8,128)(2,1)S(1)} %copy-done, bf16[16,768,256]{2,1,0:T(8,128)(2,1)} %get-tuple-element.92.stack_ref), custom_call_target="tpu_custom_call" | custom-call | flops 1207959552 | bytes 3145728 | tf_op jit(solution)/shard_map/pallas_call | solution.py:352
  106.6 2.2 %shard_map.121 = (f32[384,256]{1,0:T(8,128)S(1)}, bf16[416,256]{1,0:T(8,128)(2,1)S(1)}, bf16[416,256]{1,0:T(8,128)(2,1)S(1)}, bf16[416,256]{1,0:T(8,128)(2,1)S(1)}, f32[16,256]{1,0:T(8,128)S(1)}) custom-call(f32[1552,256]{1,0:T(8,128)} %get-tuple-element.99.kept_ref, f32[1552,256]{1,0:T(8,128)} %copy-done.7), custom_call_target="tpu_custom_call" | custom-call | tf_op jit(solution)/shard_map/pallas_call | solution.py:401
  108.7 1.7 %collective-permute-start.22 = (bf16[416,256]{1,0:T(8,128)(2,1)S(1)}, bf16[416,256]{1,0:T(8,128)(2,1)S(1)}, u32[]{:S(2)}, u32[]{:S(2)}) collective-permute-start(bf16[416,256]{1,0:T(8,128)(2,1)S(1)} %get-tuple-element.103), channel_id=1, source_target_pairs={{0,4},{1,5},{2,6},{3,7},{4,8},{5,9},{6,10},{7,11},{8,12},{9,13},{1... | collective-permute-start | bytes 638984 | tf_op jit(solution)/shard_map/ppermute | solution.py:35
  110.4 2.9 %collective-permute-start.23 = (bf16[416,256]{1,0:T(8,128)(2,1)S(1)}, bf16[416,256]{1,0:T(8,128)(2,1)S(1)}, u32[]{:S(2)}, u32[]{:S(2)}) collective-permute-start(bf16[416,256]{1,0:T(8,128)(2,1)S(1)} %get-tuple-element.104), channel_id=1, source_target_pairs={{0,8},{1,9},{2,10},{3,11},{4,12},{5,13},{6,14},{7,15},{8,0},{9,1},... | collective-permute-start | bytes 638984 | tf_op jit(solution)/shard_map/ppermute | solution.py:35
  113.3 1.3 collective-permute-start.24
  114.7 3.0 %collective-permute-done.22.a_ref = bf16[416,256]{1,0:T(8,128)(2,1)S(1)} collective-permute-done((bf16[416,256]{1,0:T(8,128)(2,1)S(1)}, bf16[416,256]{1,0:T(8,128)(2,1)S(1)}, u32[]{:S(2)}, u32[]{:S(2)}) %collective-permute-start.22) | collective-permute-done | bytes 213024 | tf_op jit(solution)/shard_map/ppermute | solution.py:35
  117.6 5.7 %collective-permute-done.23.b_ref = bf16[416,256]{1,0:T(8,128)(2,1)S(1)} collective-permute-done((bf16[416,256]{1,0:T(8,128)(2,1)S(1)}, bf16[416,256]{1,0:T(8,128)(2,1)S(1)}, u32[]{:S(2)}, u32[]{:S(2)}) %collective-permute-start.23) | collective-permute-done | bytes 213024 | tf_op jit(solution)/shard_map/ppermute | solution.py:35
  123.5 1.2 collective-permute-start.25
  124.7 1.2 copy-done.8
  125.8 2.1 %shard_map.120 = (f32[384,256]{1,0:T(8,128)S(1)}, bf16[384,256]{1,0:T(8,128)(2,1)S(1)}, bf16[384,256]{1,0:T(8,128)(2,1)S(1)}, bf16[384,256]{1,0:T(8,128)(2,1)S(1)}) custom-call(f32[1536,256]{1,0:T(8,128)} %get-tuple-element.93.kept_ref, f32[1536,256]{1,0:T(8,128)} %copy-done.8), custom_call_target="tpu_custom_call" | custom-call | tf_op jit(solution)/shard_map/pallas_call | solution.py:401
  128.0 1.3 collective-permute-start.19
  129.3 2.4 %collective-permute-start.20 = (bf16[384,256]{1,0:T(8,128)(2,1)S(1)}, bf16[384,256]{1,0:T(8,128)(2,1)S(1)}, u32[]{:S(2)}, u32[]{:S(2)}) collective-permute-start(bf16[384,256]{1,0:T(8,128)(2,1)S(1)} %get-tuple-element.97), channel_id=1, source_target_pairs={{0,8},{1,9},{2,10},{3,11},{4,12},{5,13},{6,14},{7,15},{8,0},{9,1},... | collective-permute-start | bytes 589832 | tf_op jit(solution)/shard_map/ppermute | solution.py:35
  131.7 1.6 %collective-permute-start.21 = (bf16[384,256]{1,0:T(8,128)(2,1)S(1)}, bf16[384,256]{1,0:T(8,128)(2,1)S(1)}, u32[]{:S(2)}, u32[]{:S(2)}) collective-permute-start(bf16[384,256]{1,0:T(8,128)(2,1)S(1)} %get-tuple-element.98), channel_id=1, source_target_pairs={{0,12},{1,13},{2,14},{3,15},{4,0},{5,1},{6,2},{7,3},{8,4},{9,5},{1... | collective-permute-start | bytes 589832 | tf_op jit(solution)/shard_map/ppermute | solution.py:35
  133.3 2.5 %collective-permute-done.19.a_ref = bf16[384,256]{1,0:T(8,128)(2,1)S(1)} collective-permute-done((bf16[384,256]{1,0:T(8,128)(2,1)S(1)}, bf16[384,256]{1,0:T(8,128)(2,1)S(1)}, u32[]{:S(2)}, u32[]{:S(2)}) %collective-permute-start.19) | collective-permute-done | bytes 196640 | tf_op jit(solution)/shard_map/ppermute | solution.py:35
  135.8 4.7 %collective-permute-done.20.b_ref = bf16[384,256]{1,0:T(8,128)(2,1)S(1)} collective-permute-done((bf16[384,256]{1,0:T(8,128)(2,1)S(1)}, bf16[384,256]{1,0:T(8,128)(2,1)S(1)}, u32[]{:S(2)}, u32[]{:S(2)}) %collective-permute-start.20) | collective-permute-done | bytes 196640 | tf_op jit(solution)/shard_map/ppermute | solution.py:35
  140.4 0.9 shard_map.123
  141.3 0.6 slice.3
  (39 shorter events, 1.2 us)
Async XLA Ops:
  7.2 26.2 %copy-start.1 = (bf16[1,768,256]{2,1,0:T(8,128)(2,1)S(1)}, bf16[1,768,256]{2,1,0:T(8,128)(2,1)}, u32[]{:S(2)}) copy-start(bf16[1,768,256]{2,1,0:T(8,128)(2,1)} %param.11) | copy-start | bytes 1179652
  7.2 57.5 %all-gather.3.cloned.1.call-start = ((), (), s32[]{:S(2)}) async-start(), calls=%async_computation | async-start | bytes 2211840 | tf_op jit(solution)/shard_map/all_gather | solution.py:175
  7.2 18.1 %collective-permute-start.2 = (bf16[768,256]{1,0:T(8,128)(2,1)}, bf16[768,256]{1,0:T(8,128)(2,1)S(1)}, u32[]{:S(2)}, u32[]{:S(2)}) collective-permute-start(bf16[768,256]{1,0:T(8,128)(2,1)} %bitcast.9), channel_id=1, source_target_pairs={{0,16},{16,0},{32,48},{48,32},{64,80},{80,64},{96,112},{112,96},{1... | collective-permute-start | bytes 1179656 | tf_op jit(solution)/shard_map/ppermute | solution.py:31
  8.8 16.5 %collective-permute-start.1 = (bf16[768,256]{1,0:T(8,128)(2,1)}, bf16[768,256]{1,0:T(8,128)(2,1)S(1)}, u32[]{:S(2)}, u32[]{:S(2)}) collective-permute-start(bf16[768,256]{1,0:T(8,128)(2,1)} %bitcast.10), channel_id=1, source_target_pairs={{0,224},{16,240},{32,0},{48,16},{64,32},{80,48},{96,64},{112,80},{... | collective-permute-start | bytes 1179656 | tf_op jit(solution)/shard_map/ppermute | solution.py:27
  8.9 16.4 %collective-permute-start = (bf16[768,256]{1,0:T(8,128)(2,1)}, bf16[768,256]{1,0:T(8,128)(2,1)S(1)}, u32[]{:S(2)}, u32[]{:S(2)}) collective-permute-start(bf16[768,256]{1,0:T(8,128)(2,1)} %bitcast.11), channel_id=1, source_target_pairs={{0,32},{16,48},{32,64},{48,80},{64,96},{80,112},{96,128},{112,144}... | collective-permute-start | bytes 1179656 | tf_op jit(solution)/shard_map/ppermute | solution.py:27
  12.0 13.3 %collective-permute-start.3 = (bf16[48,2304]{1,0:T(8,128)(2,1)}, bf16[48,2304]{1,0:T(8,128)(2,1)S(1)}, u32[]{:S(2)}, u32[]{:S(2)}) collective-permute-start(bf16[48,2304]{1,0:T(8,128)(2,1)} %param.12), channel_id=1, source_target_pairs={{0,2},{1,3},{2,0},{3,1},{4,6},{5,7},{6,4},{7,5},{8,10},{9,11},{10,... | collective-permute-start | bytes 663560 | tf_op jit(solution)/shard_map/ppermute | solution.py:39
  27.1 10.7 %collective-permute-start.4 = (bf16[768,256]{1,0:T(8,128)(2,1)S(1)}, bf16[768,256]{1,0:T(8,128)(2,1)S(1)}, u32[]{:S(2)}, u32[]{:S(2)}) collective-permute-start(bf16[768,256]{1,0:T(8,128)(2,1)S(1)} %collective-permute-done.refs_2_), channel_id=1, source_target_pairs={{0,32},{16,48},{32,64},{48,80},{64,96},{80,112},{96,128},{112,144}... | collective-permute-start | bytes 1179656 | tf_op jit(solution)/shard_map/ppermute | solution.py:27
  30.3 12.1 %collective-permute-start.6 = (bf16[768,256]{1,0:T(8,128)(2,1)S(1)}, bf16[768,256]{1,0:T(8,128)(2,1)S(1)}, u32[]{:S(2)}, u32[]{:S(2)}) collective-permute-start(bf16[768,256]{1,0:T(8,128)(2,1)S(1)} %collective-permute-done.1.refs_1_), channel_id=1, source_target_pairs={{0,16},{16,0},{32,48},{48,32},{64,80},{80,64},{96,112},{112,96},{1... | collective-permute-start | bytes 1179656 | tf_op jit(solution)/shard_map/ppermute | solution.py:31
  30.5 11.8 %collective-permute-start.5 = (bf16[768,256]{1,0:T(8,128)(2,1)S(1)}, bf16[768,256]{1,0:T(8,128)(2,1)S(1)}, u32[]{:S(2)}, u32[]{:S(2)}) collective-permute-start(bf16[768,256]{1,0:T(8,128)(2,1)S(1)} %collective-permute-done.1.refs_1_), channel_id=1, source_target_pairs={{0,224},{16,240},{32,0},{48,16},{64,32},{80,48},{96,64},{112,80},{... | collective-permute-start | bytes 1179656 | tf_op jit(solution)/shard_map/ppermute | solution.py:27
  31.4 20.1 %collective-permute-start.9 = (bf16[768,256]{1,0:T(8,128)(2,1)S(1)}, bf16[768,256]{1,0:T(8,128)(2,1)S(1)}, u32[]{:S(2)}, u32[]{:S(2)}) collective-permute-start(bf16[768,256]{1,0:T(8,128)(2,1)S(1)} %collective-permute-done.refs_2_), channel_id=1, source_target_pairs={{0,16},{16,0},{32,48},{48,32},{64,80},{80,64},{96,112},{112,96},{1... | collective-permute-start | bytes 1179656 | tf_op jit(solution)/shard_map/ppermute | solution.py:31
  33.3 12.3 %copy-start.3 = (f32[768]{0:T(1024)S(1)}, f32[768]{0:T(1024)}, u32[]{:S(2)}) copy-start(f32[768]{0:T(1024)} %table_ref.1) | copy-start | bytes 9220
  33.3 12.4 %copy-start.4 = (s32[8]{0:T(128)S(1)}, s32[8]{0:T(128)}, u32[]{:S(2)}) copy-start(s32[8]{0:T(128)} %a_index_ref.1) | copy-start | bytes 100
  33.3 12.4 %copy-start.5 = (f32[48]{0:T(128)S(1)}, f32[48]{0:T(128)}, u32[]{:S(2)}) copy-start(f32[48]{0:T(128)} %param.15) | copy-start | bytes 580
  42.3 9.2 %collective-permute-start.7 = (bf16[768,256]{1,0:T(8,128)(2,1)S(1)}, bf16[768,256]{1,0:T(8,128)(2,1)S(1)}, u32[]{:S(2)}, u32[]{:S(2)}) collective-permute-start(bf16[768,256]{1,0:T(8,128)(2,1)S(1)} %collective-permute-done.4.refs_1_), channel_id=1, source_target_pairs={{0,32},{16,48},{32,64},{48,80},{64,96},{80,112},{96,128},{112,144}... | collective-permute-start | bytes 1179656 | tf_op jit(solution)/shard_map/ppermute | solution.py:27
  43.4 12.3 %collective-permute-start.8 = (bf16[768,256]{1,0:T(8,128)(2,1)S(1)}, bf16[768,256]{1,0:T(8,128)(2,1)S(1)}, u32[]{:S(2)}, u32[]{:S(2)}) collective-permute-start(bf16[768,256]{1,0:T(8,128)(2,1)S(1)} %collective-permute-done.5.refs_0_), channel_id=1, source_target_pairs={{0,224},{16,240},{32,0},{48,16},{64,32},{80,48},{96,64},{112,80},{... | collective-permute-start | bytes 1179656 | tf_op jit(solution)/shard_map/ppermute | solution.py:27
  46.6 15.1 %collective-permute-start.11 = (bf16[768,256]{1,0:T(8,128)(2,1)S(1)}, bf16[768,256]{1,0:T(8,128)(2,1)S(1)}, u32[]{:S(2)}, u32[]{:S(2)}) collective-permute-start(bf16[768,256]{1,0:T(8,128)(2,1)S(1)} %collective-permute-done.6.refs_2_), channel_id=1, source_target_pairs={{0,224},{16,240},{32,0},{48,16},{64,32},{80,48},{96,64},{112,80},{... | collective-permute-start | bytes 1179656 | tf_op jit(solution)/shard_map/ppermute | solution.py:27
  55.7 7.8 %collective-permute-start.12 = (bf16[768,256]{1,0:T(8,128)(2,1)S(1)}, bf16[768,256]{1,0:T(8,128)(2,1)S(1)}, u32[]{:S(2)}, u32[]{:S(2)}) collective-permute-start(bf16[768,256]{1,0:T(8,128)(2,1)S(1)} %collective-permute-done.8.refs_0_), channel_id=1, source_target_pairs={{0,16},{16,0},{32,48},{48,32},{64,80},{80,64},{96,112},{112,96},{1... | collective-permute-start | bytes 1179656 | tf_op jit(solution)/shard_map/ppermute | solution.py:31
  56.9 7.8 %collective-permute-start.10 = (bf16[768,256]{1,0:T(8,128)(2,1)S(1)}, bf16[768,256]{1,0:T(8,128)(2,1)S(1)}, u32[]{:S(2)}, u32[]{:S(2)}) collective-permute-start(bf16[768,256]{1,0:T(8,128)(2,1)S(1)} %collective-permute-done.7.refs_1_), channel_id=1, source_target_pairs={{0,32},{16,48},{32,64},{48,80},{64,96},{80,112},{96,128},{112,144}... | collective-permute-start | bytes 1179656 | tf_op jit(solution)/shard_map/ppermute | solution.py:27
  64.6 15.5 %copy-start.2 = (bf16[48,2304]{1,0:T(8,128)(2,1)S(1)}, bf16[48,2304]{1,0:T(8,128)(2,1)}, u32[]{:S(2)}) copy-start(bf16[48,2304]{1,0:T(8,128)(2,1)} %refs_7_.1) | copy-start | bytes 663556
  64.6 14.3 %collective-permute-start.16 = (bf16[4,2,48,2304]{3,2,1,0:T(8,128)(2,1)}, bf16[4,2,48,2304]{3,2,1,0:T(8,128)(2,1)S(1)}, u32[]{:S(2)}, u32[]{:S(2)}) collective-permute-start(bf16[4,2,48,2304]{3,2,1,0:T(8,128)(2,1)} %bitcast.19), channel_id=1, source_target_pairs={{0,1},{1,0},{2,3},{3,2},{4,5},{5,4},{6,7},{7,6},{8,9},{9,8},{10,11... | collective-permute-start | bytes 5308424 | tf_op jit(solution)/shard_map/ppermute | solution.py:43
  64.6 11.5 %collective-permute-start.15 = (bf16[768,256]{1,0:T(8,128)(2,1)S(1)}, bf16[768,256]{1,0:T(8,128)(2,1)S(1)}, u32[]{:S(2)}, u32[]{:S(2)}) collective-permute-start(bf16[768,256]{1,0:T(8,128)(2,1)S(1)} %collective-permute-done.9.refs_2_), channel_id=1, source_target_pairs={{0,32},{16,48},{32,64},{48,80},{64,96},{80,112},{96,128},{112,144}... | collective-permute-start | bytes 1179656 | tf_op jit(solution)/shard_map/ppermute | solution.py:27
  65.9 11.2 %collective-permute-start.14 = (bf16[768,256]{1,0:T(8,128)(2,1)S(1)}, bf16[768,256]{1,0:T(8,128)(2,1)S(1)}, u32[]{:S(2)}, u32[]{:S(2)}) collective-permute-start(bf16[768,256]{1,0:T(8,128)(2,1)S(1)} %collective-permute-done.7.refs_1_), channel_id=1, source_target_pairs={{0,16},{16,0},{32,48},{48,32},{64,80},{80,64},{96,112},{112,96},{1... | collective-permute-start | bytes 1179656 | tf_op jit(solution)/shard_map/ppermute | solution.py:31
  66.8 12.1 %collective-permute-start.13 = (bf16[768,256]{1,0:T(8,128)(2,1)S(1)}, bf16[768,256]{1,0:T(8,128)(2,1)S(1)}, u32[]{:S(2)}, u32[]{:S(2)}) collective-permute-start(bf16[768,256]{1,0:T(8,128)(2,1)S(1)} %collective-permute-done.12.refs_2_), channel_id=1, source_target_pairs={{0,224},{16,240},{32,0},{48,16},{64,32},{80,48},{96,64},{112,80},{... | collective-permute-start | bytes 1179656 | tf_op jit(solution)/shard_map/ppermute | solution.py:27
  78.9 1.3 copy-start.6
  94.9 4.0 %collective-permute-start.17 = (f32[1552,256]{1,0:T(8,128)}, f32[1552,256]{1,0:T(8,128)S(1)}, u32[]{:S(2)}, u32[]{:S(2)}) collective-permute-start(f32[1552,256]{1,0:T(8,128)} %get-tuple-element.89), channel_id=1, source_target_pairs={{0,1},{1,0},{2,3},{3,2},{4,5},{5,4},{6,7},{7,6},{8,9},{9,8},{10,11... | collective-permute-start | bytes 4767752 | tf_op jit(solution)/shard_map/ppermute | solution.py:43
  98.9 7.5 %copy-start.7 = (f32[1552,256]{1,0:T(8,128)}, f32[1552,256]{1,0:T(8,128)S(1)}, u32[]{:S(2)}) copy-start(f32[1552,256]{1,0:T(8,128)S(1)} %collective-permute-done.17.recv_ref) | copy-start | bytes 4767748
  98.9 1.5 copy-start
  106.3 18.3 %collective-permute-start.18 = (f32[1536,256]{1,0:T(8,128)}, f32[1536,256]{1,0:T(8,128)S(1)}, u32[]{:S(2)}, u32[]{:S(2)}) collective-permute-start(f32[1536,256]{1,0:T(8,128)} %get-tuple-element.94), channel_id=1, source_target_pairs={{0,1},{1,0},{2,3},{3,2},{4,5},{5,4},{6,7},{7,6},{8,9},{9,8},{10,11... | collective-permute-start | bytes 4718600 | tf_op jit(solution)/shard_map/ppermute | solution.py:43
  108.7 8.9 %collective-permute-start.22 = (bf16[416,256]{1,0:T(8,128)(2,1)S(1)}, bf16[416,256]{1,0:T(8,128)(2,1)S(1)}, u32[]{:S(2)}, u32[]{:S(2)}) collective-permute-start(bf16[416,256]{1,0:T(8,128)(2,1)S(1)} %get-tuple-element.103), channel_id=1, source_target_pairs={{0,4},{1,5},{2,6},{3,7},{4,8},{5,9},{6,10},{7,11},{8,12},{9,13},{1... | collective-permute-start | bytes 638984 | tf_op jit(solution)/shard_map/ppermute | solution.py:35
  110.4 13.0 %collective-permute-start.23 = (bf16[416,256]{1,0:T(8,128)(2,1)S(1)}, bf16[416,256]{1,0:T(8,128)(2,1)S(1)}, u32[]{:S(2)}, u32[]{:S(2)}) collective-permute-start(bf16[416,256]{1,0:T(8,128)(2,1)S(1)} %get-tuple-element.104), channel_id=1, source_target_pairs={{0,8},{1,9},{2,10},{3,11},{4,12},{5,13},{6,14},{7,15},{8,0},{9,1},... | collective-permute-start | bytes 638984 | tf_op jit(solution)/shard_map/ppermute | solution.py:35
  113.3 10.1 %collective-permute-start.24 = (bf16[416,256]{1,0:T(8,128)(2,1)S(1)}, bf16[416,256]{1,0:T(8,128)(2,1)S(1)}, u32[]{:S(2)}, u32[]{:S(2)}) collective-permute-start(bf16[416,256]{1,0:T(8,128)(2,1)S(1)} %get-tuple-element.105), channel_id=1, source_target_pairs={{0,12},{1,13},{2,14},{3,15},{4,0},{5,1},{6,2},{7,3},{8,4},{9,5},{1... | collective-permute-start | bytes 638984 | tf_op jit(solution)/shard_map/ppermute | solution.py:35
  123.5 9.8 %collective-permute-start.25 = (bf16[416,256]{1,0:T(8,128)(2,1)S(1)}, bf16[416,256]{1,0:T(8,128)(2,1)S(1)}, u32[]{:S(2)}, u32[]{:S(2)}) collective-permute-start(bf16[416,256]{1,0:T(8,128)(2,1)S(1)} %get-tuple-element.107), channel_id=1, source_target_pairs={{0,2},{1,3},{2,0},{3,1},{4,6},{5,7},{6,4},{7,5},{8,10},{9,11},{10,... | collective-permute-start | bytes 638984 | tf_op jit(solution)/shard_map/ppermute | solution.py:39
  124.7 1.2 copy-start.8
  128.0 7.8 %collective-permute-start.19 = (bf16[384,256]{1,0:T(8,128)(2,1)S(1)}, bf16[384,256]{1,0:T(8,128)(2,1)S(1)}, u32[]{:S(2)}, u32[]{:S(2)}) collective-permute-start(bf16[384,256]{1,0:T(8,128)(2,1)S(1)} %get-tuple-element.96), channel_id=1, source_target_pairs={{0,4},{1,5},{2,6},{3,7},{4,8},{5,9},{6,10},{7,11},{8,12},{9,13},{1... | collective-permute-start | bytes 589832 | tf_op jit(solution)/shard_map/ppermute | solution.py:35
  129.3 11.1 %collective-permute-start.20 = (bf16[384,256]{1,0:T(8,128)(2,1)S(1)}, bf16[384,256]{1,0:T(8,128)(2,1)S(1)}, u32[]{:S(2)}, u32[]{:S(2)}) collective-permute-start(bf16[384,256]{1,0:T(8,128)(2,1)S(1)} %get-tuple-element.97), channel_id=1, source_target_pairs={{0,8},{1,9},{2,10},{3,11},{4,12},{5,13},{6,14},{7,15},{8,0},{9,1},... | collective-permute-start | bytes 589832 | tf_op jit(solution)/shard_map/ppermute | solution.py:35
  131.7 8.7 %collective-permute-start.21 = (bf16[384,256]{1,0:T(8,128)(2,1)S(1)}, bf16[384,256]{1,0:T(8,128)(2,1)S(1)}, u32[]{:S(2)}, u32[]{:S(2)}) collective-permute-start(bf16[384,256]{1,0:T(8,128)(2,1)S(1)} %get-tuple-element.98), channel_id=1, source_target_pairs={{0,12},{1,13},{2,14},{3,15},{4,0},{5,1},{6,2},{7,3},{8,4},{9,5},{1... | collective-permute-start | bytes 589832 | tf_op jit(solution)/shard_map/ppermute | solution.py:35
Sparse Core Ops, SparseCore 0:
  27.2 30.4 all-gather.2

commit v2 on v0

v2 whole, which is shorter than its diff:
```python
import functools

import jax
import jax.numpy as jnp
from jax import lax
from jax.experimental import pallas as pl
from jax.experimental.pallas import tpu as pltpu
from jax.sharding import PartitionSpec as P

NZ = 8
NY = 4
RANKS = 16
VMEM_LIMIT = 24 * 1024 * 1024
SMALL_LIMIT = 16 * 1024 * 1024
TILE = 768
NT = (((1,), (1,)), ((), ()))


def shift_perm(step):
    return [(i, (i + step) % RANKS) for i in range(RANKS)]


def swap_perm(bit):
    return [(i, i ^ bit) for i in range(RANKS)]


def along_z(x, step):
    return lax.ppermute(x, "aa", shift_perm(2 * step))


def swap_x_lo(x):
    return lax.ppermute(x, "aa", swap_perm(1))


def along_y(x, step):
    return lax.ppermute(x, "ba", shift_perm(4 * step))


def swap_x_hi(x):
    return lax.ppermute(x, "ba", swap_perm(2))


def swap_core(x):
    return lax.ppermute(x, "ba", swap_perm(1))


def together(*arrays):
    return lax.optimization_barrier(arrays)


VMEM = pl.BlockSpec(memory_space=pltpu.VMEM)
SMEM = pl.BlockSpec(memory_space=pltpu.SMEM)


def where_am_i():
    aa, ba = lax.axis_index("aa"), lax.axis_index("ba")
    z, x_lo = aa // 2, aa % 2
    y, x_hi, core = ba // 4, (ba // 2) % 2, ba % 2
    return z, x_lo, y, x_hi, core


def column_start(place, width):
    z, x_lo = where_am_i()[:2]
    column = (z + place % NZ) % NZ * 2 + (x_lo if place < NZ else 1 - x_lo)
    return pl.multiple_of(column * width, width)


def columns_of(a_ref, place, width):
    return a_ref[:, pl.ds(column_start(place, width), width)]


def terms_kernel(a_index_ref, b_index_ref, c_index_ref, table_ref, eps_ref, row_ref, col_ref):
    occupied = eps_ref.shape[1]
    along = lambda axis, shape: lax.broadcasted_iota(jnp.int32, shape, axis)
    square = (occupied, occupied)
    eps = jnp.sum(
        jnp.where(along(0, square) == along(1, square), eps_ref[...], 0.0), axis=1, keepdims=True
    )
    energy_b, energy_c = table_ref[b_index_ref[0]], table_ref[c_index_ref[0]]
    for n in range(a_index_ref.shape[0]):
        row_ref[n * occupied : (n + 1) * occupied] = (
            eps - table_ref[a_index_ref[n]] - energy_b - energy_c
        )
    wide = (occupied, col_ref.shape[1])
    picked = lambda labels: jnp.sum(
        jnp.where(along(0, wide) == labels, eps, 0.0), axis=0, keepdims=True
    )
    col_ref[...] = picked(along(1, wide) // occupied) + picked(along(1, wide) % occupied)


def energy_terms(tables):
    occupied = tables[-1].shape[1]
    return pl.pallas_call(
        terms_kernel,
        out_shape=(
            jax.ShapeDtypeStruct((tables[0].shape[0] * occupied, 1), jnp.float32),
            jax.ShapeDtypeStruct((1, occupied * occupied), jnp.float32),
        ),
        in_specs=[SMEM] * 4 + [VMEM],
        out_specs=(VMEM, VMEM),
        compiler_params=pltpu.CompilerParams(vmem_limit_bytes=SMALL_LIMIT),
    )(*tables)


def pack_kernel(*refs):
    for n, ref in enumerate(refs[:-1]):
        refs[-1][n] = ref[...]


def pack(arrays):
    return pl.pallas_call(
        pack_kernel,
        out_shape=jax.ShapeDtypeStruct((len(arrays), *arrays[0].shape), arrays[0].dtype),
        in_specs=[VMEM] * len(arrays),
        out_specs=VMEM,
        compiler_params=pltpu.CompilerParams(vmem_limit_bytes=SMALL_LIMIT),
    )(*arrays)


def add_kernel(places, first, a_ref, *refs):
    count = len(places)
    pieces, rest = refs[:count], refs[count:]
    if first:
        out_ref, stack_ref = rest
    else:
        before_ref, _, out_ref, stack_ref = rest
    for n, (place, piece) in enumerate(zip(places, pieces)):
        stack_ref[place] = piece[...]
        terms = lax.dot_general(
            columns_of(a_ref, place, piece.shape[1]),
            piece[...],
            NT,
            preferred_element_type=jnp.float32,
        )
        if n:
            out_ref[...] += terms
        else:
            out_ref[...] = terms if first else before_ref[...] + terms


def add_products(places, pieces, a, before=()):
    rows = a.shape[0]
    virtuals, width = pieces[0].shape
    count = len(pieces)
    return pl.pallas_call(
        functools.partial(add_kernel, places, not before),
        out_shape=(
            jax.ShapeDtypeStruct((rows, virtuals), jnp.float32),
            jax.ShapeDtypeStruct((2 * NZ, virtuals, width), pieces[0].dtype),
        ),
        in_specs=[VMEM] * (1 + count + len(before)),
        out_specs=(VMEM, VMEM),
        input_output_aliases={1 + count: 0, 2 + count: 1} if before else {},
        compiler_params=pltpu.CompilerParams(vmem_limit_bytes=VMEM_LIMIT),
        cost_estimate=pl.CostEstimate(
            flops=2 * rows * virtuals * width * count,
            bytes_accessed=2 * virtuals * width * count,
            transcendentals=0,
        ),
    )(a, *pieces, *before)


def gather_pieces(piece, amplitudes, pair_rows, a, tables):
    own, other = {0: piece}, {}
    get = lambda n: other[n - NZ] if n >= NZ else own[n]
    add = lambda places, **rest: add_products(places, [get(n) for n in places], a, **rest)
    own[7], own[1], other[0], amp_hi, terms, pair_rows = together(
        along_z(piece, 1),
        along_z(piece, -1),
        swap_x_lo(piece),
        swap_x_hi(amplitudes),
        energy_terms(tables),
        pair_rows,
    )
    amp = pack([amplitudes, amp_hi])
    sums = add([0, 1, 7, NZ])
    own[6], own[2], other[1], sums, amp_up, amp_down = together(
        along_z(own[7], 1),
        along_z(own[1], -1),
        swap_x_lo(own[1]),
        sums,
        along_y(amp, -1),
        along_y(amp, 1),
    )
    sums = add([2, 6, NZ + 1], before=sums)
    own[5], own[3], other[7], sums, amp_far = together(
        along_z(own[6], 1), along_z(own[2], -1), swap_x_lo(own[7]), sums, along_y(amp_up, -1)
    )
    amp_own = pack([amp, amp_up, amp_far, amp_down])
    sums = add([3, 5, NZ + 7], before=sums)
    own[4], other[2], other[3], sums, amp_other = together(
        along_z(own[5], 1), along_z(other[1], -1), swap_x_lo(own[3]), sums, swap_core(amp_own)
    )
    other[6], other[4], other[5] = (
        along_z(other[7], 1), along_z(other[3], -1), swap_x_lo(own[5])
    )
    sums, stack = add([4, NZ + 2, NZ + 3], before=sums)
    late = [NZ + 4, NZ + 5, NZ + 6]
    return late, [get(n) for n in late], sums, stack, terms, pair_rows, amp_own, amp_other


def gamma_dots(goes, left, stack_ref, out_ref):
    z, x_lo, y, x_hi, core = where_am_i()
    first = jnp.where(x_lo == core, goes, 1 - goes) * NZ
    rows = left.shape[0]
    for n in range(NZ):
        target = (y + n) % NY * 2 + (x_hi if n < NY else 1 - x_hi)
        out_ref[n * rows : (n + 1) * rows] = jnp.dot(
            left, stack_ref[first + (target - z + NZ) % NZ], preferred_element_type=jnp.float32
        ).astype(out_ref.dtype)


def middle_kernel(late, a_ref, *refs):
    count = len(late)
    pieces, (before_ref, row_ref, col_ref, pair_ref, coulomb_ref), rest = (
        refs[:count], refs[count : count + 5], refs[count + 5 :]
    )
    amp_refs, (_, stack_ref, keep_ref, sent_ref, *rest) = rest[:2], rest[2:]
    left_ref, total, gram, amp_ref = rest
    products = before_ref[...]
    for place, piece in zip(late, pieces):
        stack_ref[place] = piece[...]
        products += lax.dot_general(
            columns_of(a_ref, place, piece.shape[1]),
            piece[...],
            NT,
            preferred_element_type=jnp.float32,
        )
    x = products.astype(jnp.bfloat16)

    _, _, y, x_hi, core = where_am_i()
    part = amp_refs[0].shape[2]
    for other_core, ref in enumerate(amp_refs):
        for n in range(NY):
            for other_hi in range(2):
                hi = 1 - x_hi if other_hi else x_hi
                owner = ((y + n) % NY * 2 + hi) * 2 + (1 - core if other_core else core)
                target = pl.ds(pl.multiple_of(owner * part, part), part)
                amp_ref[target] = ref[n, other_hi]
    tiles = [slice(n, n + TILE) for n in range(0, amp_ref.shape[1], TILE)]
    for n, tile in enumerate(tiles):
        triples = jnp.dot(
            x, amp_ref[:, tile], preferred_element_type=jnp.float32
        ) - jnp.dot(pair_ref[...], coulomb_ref[:, tile], preferred_element_type=jnp.float32)
        ratio = (triples / (row_ref[...] + col_ref[:, tile])).astype(jnp.bfloat16)
        terms = lax.dot_general(ratio, amp_ref[:, tile], NT, preferred_element_type=jnp.float32)
        pairs = lax.dot_general(ratio, ratio, NT, preferred_element_type=jnp.float32)
        if n == 0:
            total[...] = terms
            gram[...] = pairs
        else:
            total[...] += terms
            gram[...] += pairs
    left_ref[...] = total[...].astype(left_ref.dtype)

    gamma_dots(1, left_ref[...], stack_ref, sent_ref)
    gamma_dots(0, left_ref[...], stack_ref, keep_ref)

    rows, occupied = pair_ref.shape
    width = keep_ref.shape[1]
    count = rows // occupied
    block = (occupied, rows)
    same = lax.broadcasted_iota(jnp.int32, block, 0) == lax.broadcasted_iota(jnp.int32, block, 1) % occupied
    picked = jnp.concatenate(
        [
            jnp.where(same, gram[n * occupied : (n + 1) * occupied], 0.0).sum(0, keepdims=True)
            for n in range(count)
        ]
    )
    owner = lax.broadcasted_iota(jnp.int32, (rows, width), 0) // occupied
    place = lax.broadcasted_iota(jnp.int32, (rows, width), 1)
    density = jnp.dot(
        picked,
        jnp.where(owner == place, 1.0, 0.0),
        precision=lax.Precision.HIGHEST,
        preferred_element_type=jnp.float32,
    )
    density = jnp.concatenate([density, jnp.zeros((16 - count, width), jnp.float32)])
    keep_ref[NZ * rows :] = density
    put_parts(sent_ref, NZ * rows, density)


def middle(late, pieces, a, sums, stack, terms, pair_rows, coulomb, amps):
    rows, virtuals = sums.shape
    width = pieces[0].shape[1]
    pair_cols = coulomb.shape[1]
    return pl.pallas_call(
        functools.partial(middle_kernel, late),
        out_shape=(
            jax.ShapeDtypeStruct(stack.shape, stack.dtype),
            jax.ShapeDtypeStruct((NZ * rows + 16, width), jnp.float32),
            jax.ShapeDtypeStruct((NZ * rows + 32, width), jnp.bfloat16),
        ),
        in_specs=[VMEM] * (7 + len(late) + len(amps)),
        out_specs=(VMEM,) * 3,
        input_output_aliases={6 + len(late) + len(amps): 0},
        scratch_shapes=[
            pltpu.VMEM((rows, virtuals), jnp.bfloat16),
            pltpu.VMEM((rows, virtuals), jnp.float32),
            pltpu.VMEM((rows, rows), jnp.float32),
            pltpu.VMEM((virtuals, pair_cols), jnp.bfloat16),
        ],
        compiler_params=pltpu.CompilerParams(vmem_limit_bytes=VMEM_LIMIT),
    )(a, *pieces, sums, *terms, pair_rows, coulomb, *amps, stack)


def put_parts(ref, first, values):
    high = values.astype(jnp.bfloat16)
    ref[first : first + 16] = high
    ref[first + 16 : first + 32] = (values - high.astype(jnp.float32)).astype(jnp.bfloat16)


def wide(ref, first, rows):
    return ref[first : first + rows].astype(jnp.float32)


def got_parts(ref, first):
    return wide(ref, first, 16) + wide(ref, first + 16, 16)


def first_kernel(kept_ref, recv_ref, mine_ref, one_ref, two_ref, three_ref, keep_ref, send_ref, out_ref):
    half = mine_ref.shape[0] // 2
    rows = 2 * half
    for hi in range(2):
        for n, ref in enumerate((mine_ref, one_ref, two_ref, three_ref)):
            first = (hi * NY + n) * rows
            upper = kept_ref[first : first + half] + wide(recv_ref, first, half)
            ref[hi * half : (hi + 1) * half] = upper.astype(ref.dtype)
            lower = kept_ref[first + half : first + rows] + wide(recv_ref, first + half, half)
            ref = send_ref if hi else keep_ref
            ref[n * half : (n + 1) * half] = lower.astype(ref.dtype)
    density = kept_ref[NZ * rows :] + got_parts(recv_ref, NZ * rows)
    out_ref[...] = density
    put_parts(send_ref, NY * half, density)


def first_sums(kept, received):
    rows, width = (kept.shape[0] - 16) // NZ, kept.shape[1]
    shape = lambda n, kind: jax.ShapeDtypeStruct((n, width), kind)
    message = shape(rows, jnp.bfloat16)
    return pl.pallas_call(
        first_kernel,
        out_shape=(
            shape(rows, jnp.float32),
            message,
            message,
            message,
            shape(NY * rows // 2, jnp.float32),
            shape(NY * rows // 2 + 32, jnp.bfloat16),
            shape(16, jnp.float32),
        ),
        in_specs=[VMEM] * 2,
        out_specs=(VMEM,) * 7,
        compiler_params=pltpu.CompilerParams(vmem_limit_bytes=SMALL_LIMIT),
    )(kept, received)


def second_kernel(
    mine_ref, a_ref, b_ref, c_ref, keep_ref, recv_ref, density_ref,
    upper_ref, send_ref, lower_ref, one_ref, two_ref, three_ref, out_ref,
):
    half = upper_ref.shape[0]
    for hi, ref in enumerate((upper_ref, send_ref)):
        first = hi * half
        arrived = sum(wide(other, first, half) for other in (a_ref, b_ref, c_ref))
        ref[...] = (mine_ref[first : first + half] + arrived).astype(ref.dtype)
    density = density_ref[...] + got_parts(recv_ref, NY * half)
    out_ref[...] = density
    for n, ref in enumerate((lower_ref, one_ref, two_ref, three_ref)):
        first = n * half
        total = keep_ref[first : first + half] + wide(recv_ref, first, half)
        ref[:half] = total.astype(ref.dtype)
        if n:
            put_parts(ref, half, density)


def second_sums(mine, arrived, keep, received, density):
    half, width = mine.shape[0] // 2, mine.shape[1]
    shape = lambda n, kind: jax.ShapeDtypeStruct((n, width), kind)
    message = shape(half + 32, jnp.bfloat16)
    return pl.pallas_call(
        second_kernel,
        out_shape=(
            shape(half, jnp.float32),
            shape(half, jnp.bfloat16),
            shape(half, jnp.float32),
            message,
            message,
            message,
            shape(16, jnp.float32),
        ),
        in_specs=[VMEM] * 7,
        out_specs=(VMEM,) * 7,
        compiler_params=pltpu.CompilerParams(vmem_limit_bytes=SMALL_LIMIT),
    )(mine, *arrived, keep, received, density)


def last_kernel(
    scale, upper_ref, recv_ref, lower_ref, a_ref, b_ref, c_ref, density_ref, gamma_ref, out_ref
):
    half = upper_ref.shape[0]
    gamma_ref[:half] = upper_ref[...] + wide(recv_ref, 0, half)
    arrived = (a_ref, b_ref, c_ref)
    gamma_ref[half:] = lower_ref[...] + sum(wide(ref, 0, half) for ref in arrived)
    density = density_ref[...] + sum(got_parts(ref, half) for ref in arrived)
    count = out_ref.shape[0]
    out_ref[...] = density[:count, :count] / scale


def last_sums(scale, count, upper, received, lower, arrived, density):
    half, width = upper.shape
    return pl.pallas_call(
        functools.partial(last_kernel, scale),
        out_shape=(
            jax.ShapeDtypeStruct((2 * half, width), jnp.float32),
            jax.ShapeDtypeStruct((count, count), jnp.float32),
        ),
        in_specs=[VMEM] * 7,
        out_specs=(VMEM, VMEM),
        compiler_params=pltpu.CompilerParams(vmem_limit_bytes=SMALL_LIMIT),
    )(upper, received, lower, *arrived, density)


def to_owners(messages):
    one, two, three = messages
    return along_y(one, 1), along_y(two, 2), along_y(three, -1)


def body(
    b_vo, b_vv, amplitudes, pair_amps, coulomb_occ, eps_occ, eps_vir, c_index, a_index, b_index
):
    count_a, occupied, aux_all = b_vo.shape
    rows = count_a * occupied
    virtuals = b_vv.shape[1]
    pair_cols = amplitudes.shape[1]
    vo_rows = b_vo.reshape(rows, aux_all)
    tables = (a_index, b_index, c_index, eps_vir, eps_occ.reshape(1, occupied))
    late, pieces, sums, stack, terms, pair_rows, *amps = gather_pieces(
        b_vv[0], amplitudes, pair_amps.reshape(rows, occupied), vo_rows, tables
    )
    _, kept, sent = middle(late, pieces, vo_rows, sums, stack, terms, pair_rows, coulomb_occ, amps)
    mine, *messages, keep, send, density = first_sums(kept, swap_core(sent))
    arrived, received = together(to_owners(messages), swap_x_hi(send))
    upper, send, lower, *messages, density = second_sums(mine, arrived, keep, received, density)
    arrived, received = together(to_owners(messages), swap_x_hi(send))
    scale = lax.axis_size("ba") * occupied * occupied
    gamma, density = last_sums(scale, count_a, upper, received, lower, arrived, density)
    return gamma.reshape(count_a, occupied, gamma.shape[1]), density


def solution(mesh):
    placed = (
        P("aa", None, None),
        P("ba", None, "aa"),
        P("ba", None),
        P("aa", "ba", None),
        P(),
        P(),
        P(),
        P(),
        P("aa"),
        P("ba"),
    )
    return jax.shard_map(
        body,
        mesh=mesh,
        in_specs=placed,
        out_specs=(P("aa", None, "ba"), P("aa", None)),
        check_vma=False,
    )
```

time: 365 us -> 113 us (0.31)
  waiting for transfers between devices: 271 us -> 53.2 us
  starting transfers between devices: 0.11 us -> 35.6 us
  blocking collectives: 33.5 us -> 0 us
  matrix products: 33.4 us -> 0 us
  Pallas kernels: 0 us -> 13.5 us
  between operations: 15.1 us -> 2.06 us
  other arithmetic: 4.78 us -> 0 us
    all_gather x2 -> x0, waiting for transfers between devices: 204 us -> none  [the longest x1 154 us: body(): piece = lax.all_gather(b_vv, 'aa', axis=2, tiled=True)]
    reduce_scatter x1 -> x0, waiting for transfers between devices: 65.7 us -> none  [body(): gamma = lax.psum_scatter(gamma_terms, 'ba', scatter_dimension=1, tiled=True)]
    ppermute x0 -> x29, waiting for transfers between devices: none -> 53.2 us  [the longest x10 23.2 us: along_z(): return lax.ppermute(x, 'aa', shift_perm(2 * step))]
    ppermute x0 -> x29, starting transfers between devices: none -> 35.6 us  [the longest x10 12.3 us: along_z(): return lax.ppermute(x, 'aa', shift_perm(2 * step))]
    psum x1 -> x0, blocking collectives: 33.5 us -> none  [body(): density = lax.psum(partial_density, 'ba') / (total_b * occupied * occupied)]
    dot_general x4 -> x0, matrix products: 33.4 us -> none  [the longest x1 11.5 us: body(): jnp.dot(left, piece.reshape(count_b * virtuals, piece.shape[2]), preferre...]
    pallas_call x0 -> x11, Pallas kernels: none -> 13.5 us  [the longest x1 7.79 us: middle(): pl.pallas_call(functools.partial(middle_kernel, late), out_shape=(jax.Sha...]
    unnamed x6 -> x14, local copies, waits for them, and re-layouts: 0.02 us -> 5.81 us
  transfers between devices with their start and end apart: 3 -> 29, of which waited for: 3 -> 16; matrix products, arithmetic and copies ran while one was open for 4% -> 1% of each run, Pallas kernels for 0% -> 4%
where the time goes in v2:
time: 113 us; the launch traced here: 111 us
  waiting for transfers between devices  53.2 us (47%)
  starting transfers between devices  35.6 us (32%)
  Pallas kernels  13.5 us (12%)
  local copies, waits for them, and re-layouts  6.72 us (6%)
  between operations  2.06 us (2%)
    ppermute x10, waiting for transfers between devices, along_z(): return lax.ppermute(x, 'aa', shift_perm(2 * step))  23.2 us
    ppermute x10, starting transfers between devices, along_z(): return lax.ppermute(x, 'aa', shift_perm(2 * step))  12.3 us
    ppermute x9, starting transfers between devices, along_y(): return lax.ppermute(x, 'ba', shift_perm(4 * step))  12.1 us
    ppermute x9, waiting for transfers between devices, along_y(): return lax.ppermute(x, 'ba', shift_perm(4 * step))  9.45 us
    ppermute x3, waiting for transfers between devices, swap_x_hi(): return lax.ppermute(x, 'ba', swap_perm(2))  9.29 us
    pallas_call x1, Pallas kernels, middle(): pl.pallas_call(functools.partial(middle_kernel, late), out_shape=(jax.Sha...  7.79 us
    ppermute x5, waiting for transfers between devices, swap_x_lo(): return lax.ppermute(x, 'aa', swap_perm(1))  7.75 us
    ppermute x3, starting transfers between devices, swap_x_hi(): return lax.ppermute(x, 'ba', swap_perm(2))  6.57 us
  transfers between devices with their start and end apart: 29, of which 16 were waited for; matrix products, arithmetic and copies ran while one was open for 1% of the time, Pallas kernels for 4%

profile of v2, /device:TPU:96, one launch (start us, length us, event | category | flops | bytes accessed | tf_op | source)
XLA Modules:
  0.0 111.1 jit_solution(4827714298090141404)
XLA Ops:
  0.6 1.6 %collective-permute-start.2 = (bf16[768,256]{1,0:T(8,128)(2,1)}, bf16[768,256]{1,0:T(8,128)(2,1)S(1)}, u32[]{:S(2)}, u32[]{:S(2)}) collective-permute-start(bf16[768,256]{1,0:T(8,128)(2,1)} %bitcast.11), channel_id=1, source_target_pairs={{0,16},{16,0},{32,48},{48,32},{64,80},{80,64},{96,112},{112,96},{1... | collective-permute-start | bytes 1179656 | tf_op jit(solution)/shard_map/ppermute | solution.py:32
  2.3 3.1 %collective-permute-start = (bf16[768,256]{1,0:T(8,128)(2,1)}, bf16[768,256]{1,0:T(8,128)(2,1)S(1)}, u32[]{:S(2)}, u32[]{:S(2)}) collective-permute-start(bf16[768,256]{1,0:T(8,128)(2,1)} %bitcast.13), channel_id=1, source_target_pairs={{0,32},{16,48},{32,64},{48,80},{64,96},{80,112},{96,128},{112,144}... | collective-permute-start | bytes 1179656 | tf_op jit(solution)/shard_map/ppermute | solution.py:28
  5.4 2.7 %collective-permute-start.3 = (bf16[48,2304]{1,0:T(8,128)(2,1)}, bf16[48,2304]{1,0:T(8,128)(2,1)S(1)}, u32[]{:S(2)}, u32[]{:S(2)}) collective-permute-start(bf16[48,2304]{1,0:T(8,128)(2,1)} %refs_0_.1), channel_id=1, source_target_pairs={{0,2},{1,3},{2,0},{3,1},{4,6},{5,7},{6,4},{7,5},{8,10},{9,11},{10,... | collective-permute-start | bytes 663560 | tf_op jit(solution)/shard_map/ppermute | solution.py:40
  9.5 0.9 reshape.18.refs_6_
  10.4 0.7 copy-done.4
  11.1 0.7 copy-done.5
  11.7 0.7 copy-done.6
  12.4 0.9 shard_map.113
  13.3 5.4 %collective-permute-done.3.refs_1_ = bf16[48,2304]{1,0:T(8,128)(2,1)S(1)} collective-permute-done((bf16[48,2304]{1,0:T(8,128)(2,1)}, bf16[48,2304]{1,0:T(8,128)(2,1)S(1)}, u32[]{:S(2)}, u32[]{:S(2)}) %collective-permute-start.3) | collective-permute-done | bytes 221216 | tf_op jit(solution)/shard_map/ppermute | solution.py:40
  18.7 0.9 copy-done.2
  19.7 1.7 %collective-permute-start.8 = (bf16[2,48,2304]{2,1,0:T(8,128)(2,1)S(1)}, bf16[2,48,2304]{2,1,0:T(8,128)(2,1)S(1)}, u32[]{:S(2)}, u32[]{:S(2)}) collective-permute-start(bf16[2,48,2304]{2,1,0:T(8,128)(2,1)S(1)} %shard_map.115.refs_0_), channel_id=1, source_target_pairs={{0,4},{1,5},{2,6},{3,7},{4,8},{5,9},{6,10},{7,11},{8,12},{9,13},{1... | collective-permute-start | bytes 1327112 | tf_op jit(solution)/shard_map/ppermute | solution.py:36
  21.4 1.7 %collective-permute-start.7 = (bf16[2,48,2304]{2,1,0:T(8,128)(2,1)S(1)}, bf16[2,48,2304]{2,1,0:T(8,128)(2,1)S(1)}, u32[]{:S(2)}, u32[]{:S(2)}) collective-permute-start(bf16[2,48,2304]{2,1,0:T(8,128)(2,1)S(1)} %shard_map.115.refs_0_), channel_id=1, source_target_pairs={{0,12},{1,13},{2,14},{3,15},{4,0},{5,1},{6,2},{7,3},{8,4},{9,5},{1... | collective-permute-start | bytes 1327112 | tf_op jit(solution)/shard_map/ppermute | solution.py:36
  23.0 3.1 %collective-permute-start.4 = (bf16[768,256]{1,0:T(8,128)(2,1)S(1)}, bf16[768,256]{1,0:T(8,128)(2,1)S(1)}, u32[]{:S(2)}, u32[]{:S(2)}) collective-permute-start(bf16[768,256]{1,0:T(8,128)(2,1)S(1)} %collective-permute-done.refs_2_), channel_id=1, source_target_pairs={{0,32},{16,48},{32,64},{48,80},{64,96},{80,112},{96,128},{112,144}... | collective-permute-start | bytes 1179656 | tf_op jit(solution)/shard_map/ppermute | solution.py:28
  26.4 1.9 %copy-done = bf16[8,48,4096]{2,1,0:T(8,128)(2,1)S(1)} copy-done((bf16[8,48,4096]{2,1,0:T(8,128)(2,1)S(1)}, bf16[8,48,4096]{2,1,0:T(8,128)(2,1)}, u32[]{:S(2)}) %copy-start) | copy-done | bytes 3145752
  28.3 1.0 copy-done.1
  29.3 0.9 shard_map.114
  30.1 3.1 %collective-permute-done.4.refs_1_ = bf16[768,256]{1,0:T(8,128)(2,1)S(1)} collective-permute-done((bf16[768,256]{1,0:T(8,128)(2,1)S(1)}, bf16[768,256]{1,0:T(8,128)(2,1)S(1)}, u32[]{:S(2)}, u32[]{:S(2)}) %collective-permute-start.4) | collective-permute-done | bytes 393248 | tf_op jit(solution)/shard_map/ppermute | solution.py:28
  33.2 2.2 %collective-permute-done.6.refs_2_ = bf16[768,256]{1,0:T(8,128)(2,1)S(1)} collective-permute-done((bf16[768,256]{1,0:T(8,128)(2,1)S(1)}, bf16[768,256]{1,0:T(8,128)(2,1)S(1)}, u32[]{:S(2)}, u32[]{:S(2)}) %collective-permute-start.6) | collective-permute-done | bytes 393248 | tf_op jit(solution)/shard_map/ppermute | solution.py:32
  35.4 1.2 %collective-permute-done.5.refs_0_ = bf16[768,256]{1,0:T(8,128)(2,1)S(1)} collective-permute-done((bf16[768,256]{1,0:T(8,128)(2,1)S(1)}, bf16[768,256]{1,0:T(8,128)(2,1)S(1)}, u32[]{:S(2)}, u32[]{:S(2)}) %collective-permute-start.5) | collective-permute-done | bytes 393248 | tf_op jit(solution)/shard_map/ppermute | solution.py:28
  36.7 1.7 %collective-permute-start.12 = (bf16[2,48,2304]{2,1,0:T(8,128)(2,1)S(1)}, bf16[2,48,2304]{2,1,0:T(8,128)(2,1)S(1)}, u32[]{:S(2)}, u32[]{:S(2)}) collective-permute-start(bf16[2,48,2304]{2,1,0:T(8,128)(2,1)S(1)} %collective-permute-done.7.refs_1_), channel_id=1, source_target_pairs={{0,12},{1,13},{2,14},{3,15},{4,0},{5,1},{6,2},{7,3},{8,4},{9,5},{1... | collective-permute-start | bytes 1327112 | tf_op jit(solution)/shard_map/ppermute | solution.py:36
  38.3 1.7 %collective-permute-start.11 = (bf16[768,256]{1,0:T(8,128)(2,1)S(1)}, bf16[768,256]{1,0:T(8,128)(2,1)S(1)}, u32[]{:S(2)}, u32[]{:S(2)}) collective-permute-start(bf16[768,256]{1,0:T(8,128)(2,1)S(1)} %collective-permute-done.refs_2_), channel_id=1, source_target_pairs={{0,16},{16,0},{32,48},{48,32},{64,80},{80,64},{96,112},{112,96},{1... | collective-permute-start | bytes 1179656 | tf_op jit(solution)/shard_map/ppermute | solution.py:32
  40.1 2.0 %collective-permute-start.10 = (bf16[768,256]{1,0:T(8,128)(2,1)S(1)}, bf16[768,256]{1,0:T(8,128)(2,1)S(1)}, u32[]{:S(2)}, u32[]{:S(2)}) collective-permute-start(bf16[768,256]{1,0:T(8,128)(2,1)S(1)} %collective-permute-done.5.refs_0_), channel_id=1, source_target_pairs={{0,224},{16,240},{32,0},{48,16},{64,32},{80,48},{96,64},{112,80},{... | collective-permute-start | bytes 1179656 | tf_op jit(solution)/shard_map/ppermute | solution.py:28
  42.1 0.8 shard_map.116
  42.9 3.2 %collective-permute-done.11.refs_2_ = bf16[768,256]{1,0:T(8,128)(2,1)S(1)} collective-permute-done((bf16[768,256]{1,0:T(8,128)(2,1)S(1)}, bf16[768,256]{1,0:T(8,128)(2,1)S(1)}, u32[]{:S(2)}, u32[]{:S(2)}) %collective-permute-start.11) | collective-permute-done | bytes 393248 | tf_op jit(solution)/shard_map/ppermute | solution.py:32
  46.1 1.7 %collective-permute-done.9.refs_1_ = bf16[768,256]{1,0:T(8,128)(2,1)S(1)} collective-permute-done((bf16[768,256]{1,0:T(8,128)(2,1)S(1)}, bf16[768,256]{1,0:T(8,128)(2,1)S(1)}, u32[]{:S(2)}, u32[]{:S(2)}) %collective-permute-start.9) | collective-permute-done | bytes 393248 | tf_op jit(solution)/shard_map/ppermute | solution.py:28
  47.8 1.2 %collective-permute-done.10.refs_0_ = bf16[768,256]{1,0:T(8,128)(2,1)S(1)} collective-permute-done((bf16[768,256]{1,0:T(8,128)(2,1)S(1)}, bf16[768,256]{1,0:T(8,128)(2,1)S(1)}, u32[]{:S(2)}, u32[]{:S(2)}) %collective-permute-start.10) | collective-permute-done | bytes 393248 | tf_op jit(solution)/shard_map/ppermute | solution.py:28
  49.3 1.1 collective-permute-start.14
  50.6 2.8 %collective-permute-start.13 = (bf16[768,256]{1,0:T(8,128)(2,1)S(1)}, bf16[768,256]{1,0:T(8,128)(2,1)S(1)}, u32[]{:S(2)}, u32[]{:S(2)}) collective-permute-start(bf16[768,256]{1,0:T(8,128)(2,1)S(1)} %collective-permute-done.9.refs_1_), channel_id=1, source_target_pairs={{0,32},{16,48},{32,64},{48,80},{64,96},{80,112},{96,128},{112,144}... | collective-permute-start | bytes 1179656 | tf_op jit(solution)/shard_map/ppermute | solution.py:28
  53.5 0.8 shard_map.117
  54.3 7.7 %collective-permute-done.14.refs_1_ = bf16[768,256]{1,0:T(8,128)(2,1)S(1)} collective-permute-done((bf16[768,256]{1,0:T(8,128)(2,1)S(1)}, bf16[768,256]{1,0:T(8,128)(2,1)S(1)}, u32[]{:S(2)}, u32[]{:S(2)}) %collective-permute-start.14) | collective-permute-done | bytes 393248 | tf_op jit(solution)/shard_map/ppermute | solution.py:28
  62.0 0.6 collective-permute-start.18
  63.0 0.8 shard_map.119
  63.8 6.2 %collective-permute-done.19.refs_2_ = bf16[768,256]{1,0:T(8,128)(2,1)S(1)} collective-permute-done((bf16[768,256]{1,0:T(8,128)(2,1)S(1)}, bf16[768,256]{1,0:T(8,128)(2,1)S(1)}, u32[]{:S(2)}, u32[]{:S(2)}) %collective-permute-start.19) | collective-permute-done | bytes 393248 | tf_op jit(solution)/shard_map/ppermute | solution.py:28
  70.1 2.4 %collective-permute-done.18.refs_1_ = bf16[768,256]{1,0:T(8,128)(2,1)S(1)} collective-permute-done((bf16[768,256]{1,0:T(8,128)(2,1)S(1)}, bf16[768,256]{1,0:T(8,128)(2,1)S(1)}, u32[]{:S(2)}, u32[]{:S(2)}) %collective-permute-start.18) | collective-permute-done | bytes 393248 | tf_op jit(solution)/shard_map/ppermute | solution.py:32
  72.4 1.7 %collective-permute-done.17.refs_0_ = bf16[768,256]{1,0:T(8,128)(2,1)S(1)} collective-permute-done((bf16[768,256]{1,0:T(8,128)(2,1)S(1)}, bf16[768,256]{1,0:T(8,128)(2,1)S(1)}, u32[]{:S(2)}, u32[]{:S(2)}) %collective-permute-start.17) | collective-permute-done | bytes 393248 | tf_op jit(solution)/shard_map/ppermute | solution.py:28
  74.1 7.8 %shard_map.120 = (bf16[16,768,256]{2,1,0:T(8,128)(2,1)S(1)}, f32[3088,256]{1,0:T(8,128)S(1)}, bf16[3104,256]{1,0:T(8,128)(2,1)S(1)}) custom-call(bf16[384,4096]{1,0:T(8,128)(2,1)S(1)} %bitcast.10, bf16[768,256]{1,0:T(8,128)(2,1)S(1)} %collective-permute-done.17.refs_0_, ...), custom_call_target="tpu_custom_call", output_to_operand_aliasing={{0}: (11, {})} | custom-call | tf_op jit(solution)/shard_map/pallas_call | solution.py:287
  82.0 3.4 %collective-permute-done.20.recv_ref = bf16[3104,256]{1,0:T(8,128)(2,1)S(1)} collective-permute-done((bf16[3104,256]{1,0:T(8,128)(2,1)S(1)}, bf16[3104,256]{1,0:T(8,128)(2,1)S(1)}, u32[]{:S(2)}, u32[]{:S(2)}) %collective-permute-start.20) | collective-permute-done | bytes 1589280 | tf_op jit(solution)/shard_map/ppermute | solution.py:44
  85.4 0.4 shard_map.121
  85.8 1.6 %collective-permute-start.24 = (bf16[800,256]{1,0:T(8,128)(2,1)S(1)}, bf16[800,256]{1,0:T(8,128)(2,1)S(1)}, u32[]{:S(2)}, u32[]{:S(2)}) collective-permute-start(bf16[800,256]{1,0:T(8,128)(2,1)S(1)} %get-tuple-element.106), channel_id=1, source_target_pairs={{0,2},{1,3},{2,0},{3,1},{4,6},{5,7},{6,4},{7,5},{8,10},{9,11},{10,... | collective-permute-start | bytes 1228808 | tf_op jit(solution)/shard_map/ppermute | solution.py:40
  87.4 0.4 collective-permute-start.21
  87.8 1.8 %collective-permute-start.22 = (bf16[384,256]{1,0:T(8,128)(2,1)S(1)}, bf16[384,256]{1,0:T(8,128)(2,1)S(1)}, u32[]{:S(2)}, u32[]{:S(2)}) collective-permute-start(bf16[384,256]{1,0:T(8,128)(2,1)S(1)} %get-tuple-element.104), channel_id=1, source_target_pairs={{0,8},{1,9},{2,10},{3,11},{4,12},{5,13},{6,14},{7,15},{8,0},{9,1},... | collective-permute-start | bytes 589832 | tf_op jit(solution)/shard_map/ppermute | solution.py:36
  89.6 1.1 collective-permute-start.23
  90.7 8.8 %collective-permute-done.21.a_ref = bf16[384,256]{1,0:T(8,128)(2,1)S(1)} collective-permute-done((bf16[384,256]{1,0:T(8,128)(2,1)S(1)}, bf16[384,256]{1,0:T(8,128)(2,1)S(1)}, u32[]{:S(2)}, u32[]{:S(2)}) %collective-permute-start.21) | collective-permute-done | bytes 196640 | tf_op jit(solution)/shard_map/ppermute | solution.py:36
  99.5 0.6 collective-permute-done.23.c_ref
  100.6 3.6 %collective-permute-start.26 = (bf16[224,256]{1,0:T(8,128)(2,1)S(1)}, bf16[224,256]{1,0:T(8,128)(2,1)S(1)}, u32[]{:S(2)}, u32[]{:S(2)}) collective-permute-start(bf16[224,256]{1,0:T(8,128)(2,1)S(1)} %get-tuple-element.115), channel_id=1, source_target_pairs={{0,8},{1,9},{2,10},{3,11},{4,12},{5,13},{6,14},{7,15},{8,0},{9,1},... | collective-permute-start | bytes 344072 | tf_op jit(solution)/shard_map/ppermute | solution.py:36
  104.1 2.2 %collective-permute-start.28 = (bf16[192,256]{1,0:T(8,128)(2,1)S(1)}, bf16[192,256]{1,0:T(8,128)(2,1)S(1)}, u32[]{:S(2)}, u32[]{:S(2)}) collective-permute-start(bf16[192,256]{1,0:T(8,128)(2,1)S(1)} %get-tuple-element.117), channel_id=1, source_target_pairs={{0,2},{1,3},{2,0},{3,1},{4,6},{5,7},{6,4},{7,5},{8,10},{9,11},{10,... | collective-permute-start | bytes 294920 | tf_op jit(solution)/shard_map/ppermute | solution.py:40
  106.4 3.9 %collective-permute-done.28.recv_ref = bf16[192,256]{1,0:T(8,128)(2,1)S(1)} collective-permute-done((bf16[192,256]{1,0:T(8,128)(2,1)S(1)}, bf16[192,256]{1,0:T(8,128)(2,1)S(1)}, u32[]{:S(2)}, u32[]{:S(2)}) %collective-permute-start.28) | collective-permute-done | bytes 98336 | tf_op jit(solution)/shard_map/ppermute | solution.py:40
  110.3 0.8 shard_map.123
  (36 shorter events, 1.8 us)
Async XLA Ops:
  0.6 18.1 %collective-permute-start.2 = (bf16[768,256]{1,0:T(8,128)(2,1)}, bf16[768,256]{1,0:T(8,128)(2,1)S(1)}, u32[]{:S(2)}, u32[]{:S(2)}) collective-permute-start(bf16[768,256]{1,0:T(8,128)(2,1)} %bitcast.11), channel_id=1, source_target_pairs={{0,16},{16,0},{32,48},{48,32},{64,80},{80,64},{96,112},{112,96},{1... | collective-permute-start | bytes 1179656 | tf_op jit(solution)/shard_map/ppermute | solution.py:32
  2.2 16.5 %collective-permute-start.1 = (bf16[768,256]{1,0:T(8,128)(2,1)}, bf16[768,256]{1,0:T(8,128)(2,1)S(1)}, u32[]{:S(2)}, u32[]{:S(2)}) collective-permute-start(bf16[768,256]{1,0:T(8,128)(2,1)} %bitcast.12), channel_id=1, source_target_pairs={{0,224},{16,240},{32,0},{48,16},{64,32},{80,48},{96,64},{112,80},{... | collective-permute-start | bytes 1179656 | tf_op jit(solution)/shard_map/ppermute | solution.py:28
  2.3 16.4 %collective-permute-start = (bf16[768,256]{1,0:T(8,128)(2,1)}, bf16[768,256]{1,0:T(8,128)(2,1)S(1)}, u32[]{:S(2)}, u32[]{:S(2)}) collective-permute-start(bf16[768,256]{1,0:T(8,128)(2,1)} %bitcast.13), channel_id=1, source_target_pairs={{0,32},{16,48},{32,64},{48,80},{64,96},{80,112},{96,128},{112,144}... | collective-permute-start | bytes 1179656 | tf_op jit(solution)/shard_map/ppermute | solution.py:28
  5.4 13.3 %collective-permute-start.3 = (bf16[48,2304]{1,0:T(8,128)(2,1)}, bf16[48,2304]{1,0:T(8,128)(2,1)S(1)}, u32[]{:S(2)}, u32[]{:S(2)}) collective-permute-start(bf16[48,2304]{1,0:T(8,128)(2,1)} %refs_0_.1), channel_id=1, source_target_pairs={{0,2},{1,3},{2,0},{3,1},{4,6},{5,7},{6,4},{7,5},{8,10},{9,11},{10,... | collective-permute-start | bytes 663560 | tf_op jit(solution)/shard_map/ppermute | solution.py:40
  10.4 0.7 copy-start.4
  11.1 0.7 copy-start.5
  11.7 0.7 copy-start.6
  18.7 0.9 copy-start.2
  19.7 17.0 %collective-permute-start.8 = (bf16[2,48,2304]{2,1,0:T(8,128)(2,1)S(1)}, bf16[2,48,2304]{2,1,0:T(8,128)(2,1)S(1)}, u32[]{:S(2)}, u32[]{:S(2)}) collective-permute-start(bf16[2,48,2304]{2,1,0:T(8,128)(2,1)S(1)} %shard_map.115.refs_0_), channel_id=1, source_target_pairs={{0,4},{1,5},{2,6},{3,7},{4,8},{5,9},{6,10},{7,11},{8,12},{9,13},{1... | collective-permute-start | bytes 1327112 | tf_op jit(solution)/shard_map/ppermute | solution.py:36
  21.4 15.3 %collective-permute-start.7 = (bf16[2,48,2304]{2,1,0:T(8,128)(2,1)S(1)}, bf16[2,48,2304]{2,1,0:T(8,128)(2,1)S(1)}, u32[]{:S(2)}, u32[]{:S(2)}) collective-permute-start(bf16[2,48,2304]{2,1,0:T(8,128)(2,1)S(1)} %shard_map.115.refs_0_), channel_id=1, source_target_pairs={{0,12},{1,13},{2,14},{3,15},{4,0},{5,1},{6,2},{7,3},{8,4},{9,5},{1... | collective-permute-start | bytes 1327112 | tf_op jit(solution)/shard_map/ppermute | solution.py:36
  23.0 10.2 %collective-permute-start.4 = (bf16[768,256]{1,0:T(8,128)(2,1)S(1)}, bf16[768,256]{1,0:T(8,128)(2,1)S(1)}, u32[]{:S(2)}, u32[]{:S(2)}) collective-permute-start(bf16[768,256]{1,0:T(8,128)(2,1)S(1)} %collective-permute-done.refs_2_), channel_id=1, source_target_pairs={{0,32},{16,48},{32,64},{48,80},{64,96},{80,112},{96,128},{112,144}... | collective-permute-start | bytes 1179656 | tf_op jit(solution)/shard_map/ppermute | solution.py:28
  26.1 9.3 %collective-permute-start.6 = (bf16[768,256]{1,0:T(8,128)(2,1)S(1)}, bf16[768,256]{1,0:T(8,128)(2,1)S(1)}, u32[]{:S(2)}, u32[]{:S(2)}) collective-permute-start(bf16[768,256]{1,0:T(8,128)(2,1)S(1)} %collective-permute-done.1.refs_1_), channel_id=1, source_target_pairs={{0,16},{16,0},{32,48},{48,32},{64,80},{80,64},{96,112},{112,96},{1... | collective-permute-start | bytes 1179656 | tf_op jit(solution)/shard_map/ppermute | solution.py:32
  26.4 10.3 %collective-permute-start.5 = (bf16[768,256]{1,0:T(8,128)(2,1)S(1)}, bf16[768,256]{1,0:T(8,128)(2,1)S(1)}, u32[]{:S(2)}, u32[]{:S(2)}) collective-permute-start(bf16[768,256]{1,0:T(8,128)(2,1)S(1)} %collective-permute-done.1.refs_1_), channel_id=1, source_target_pairs={{0,224},{16,240},{32,0},{48,16},{64,32},{80,48},{96,64},{112,80},{... | collective-permute-start | bytes 1179656 | tf_op jit(solution)/shard_map/ppermute | solution.py:28
  26.4 1.9 %copy-start = (bf16[8,48,4096]{2,1,0:T(8,128)(2,1)S(1)}, bf16[8,48,4096]{2,1,0:T(8,128)(2,1)}, u32[]{:S(2)}) copy-start(bf16[8,48,4096]{2,1,0:T(8,128)(2,1)} %param.10) | copy-start | bytes 9437188
  28.3 1.0 copy-start.1
  36.7 12.4 %collective-permute-start.12 = (bf16[2,48,2304]{2,1,0:T(8,128)(2,1)S(1)}, bf16[2,48,2304]{2,1,0:T(8,128)(2,1)S(1)}, u32[]{:S(2)}, u32[]{:S(2)}) collective-permute-start(bf16[2,48,2304]{2,1,0:T(8,128)(2,1)S(1)} %collective-permute-done.7.refs_1_), channel_id=1, source_target_pairs={{0,12},{1,13},{2,14},{3,15},{4,0},{5,1},{6,2},{7,3},{8,4},{9,5},{1... | collective-permute-start | bytes 1327112 | tf_op jit(solution)/shard_map/ppermute | solution.py:36
  38.3 7.8 %collective-permute-start.11 = (bf16[768,256]{1,0:T(8,128)(2,1)S(1)}, bf16[768,256]{1,0:T(8,128)(2,1)S(1)}, u32[]{:S(2)}, u32[]{:S(2)}) collective-permute-start(bf16[768,256]{1,0:T(8,128)(2,1)S(1)} %collective-permute-done.refs_2_), channel_id=1, source_target_pairs={{0,16},{16,0},{32,48},{48,32},{64,80},{80,64},{96,112},{112,96},{1... | collective-permute-start | bytes 1179656 | tf_op jit(solution)/shard_map/ppermute | solution.py:32
  40.1 7.8 %collective-permute-start.9 = (bf16[768,256]{1,0:T(8,128)(2,1)S(1)}, bf16[768,256]{1,0:T(8,128)(2,1)S(1)}, u32[]{:S(2)}, u32[]{:S(2)}) collective-permute-start(bf16[768,256]{1,0:T(8,128)(2,1)S(1)} %collective-permute-done.4.refs_1_), channel_id=1, source_target_pairs={{0,32},{16,48},{32,64},{48,80},{64,96},{80,112},{96,128},{112,144}... | collective-permute-start | bytes 1179656 | tf_op jit(solution)/shard_map/ppermute | solution.py:28
  40.1 9.0 %collective-permute-start.10 = (bf16[768,256]{1,0:T(8,128)(2,1)S(1)}, bf16[768,256]{1,0:T(8,128)(2,1)S(1)}, u32[]{:S(2)}, u32[]{:S(2)}) collective-permute-start(bf16[768,256]{1,0:T(8,128)(2,1)S(1)} %collective-permute-done.5.refs_0_), channel_id=1, source_target_pairs={{0,224},{16,240},{32,0},{48,16},{64,32},{80,48},{96,64},{112,80},{... | collective-permute-start | bytes 1179656 | tf_op jit(solution)/shard_map/ppermute | solution.py:28
  49.2 13.8 %collective-permute-start.16 = (bf16[4,2,48,2304]{3,2,1,0:T(8,128)(2,1)S(1)}, bf16[4,2,48,2304]{3,2,1,0:T(8,128)(2,1)S(1)}, u32[]{:S(2)}, u32[]{:S(2)}) collective-permute-start(bf16[4,2,48,2304]{3,2,1,0:T(8,128)(2,1)S(1)} %shard_map.118.refs_8_), channel_id=1, source_target_pairs={{0,1},{1,0},{2,3},{3,2},{4,5},{5,4},{6,7},{7,6},{8,9},{9,8},{10,11... | collective-permute-start | bytes 5308424 | tf_op jit(solution)/shard_map/ppermute | solution.py:44
  49.3 12.7 %collective-permute-start.14 = (bf16[768,256]{1,0:T(8,128)(2,1)S(1)}, bf16[768,256]{1,0:T(8,128)(2,1)S(1)}, u32[]{:S(2)}, u32[]{:S(2)}) collective-permute-start(bf16[768,256]{1,0:T(8,128)(2,1)S(1)} %collective-permute-done.6.refs_2_), channel_id=1, source_target_pairs={{0,224},{16,240},{32,0},{48,16},{64,32},{80,48},{96,64},{112,80},{... | collective-permute-start | bytes 1179656 | tf_op jit(solution)/shard_map/ppermute | solution.py:28
  50.3 12.3 %collective-permute-start.15 = (bf16[768,256]{1,0:T(8,128)(2,1)S(1)}, bf16[768,256]{1,0:T(8,128)(2,1)S(1)}, u32[]{:S(2)}, u32[]{:S(2)}) collective-permute-start(bf16[768,256]{1,0:T(8,128)(2,1)S(1)} %collective-permute-done.10.refs_0_), channel_id=1, source_target_pairs={{0,16},{16,0},{32,48},{48,32},{64,80},{80,64},{96,112},{112,96},{1... | collective-permute-start | bytes 1179656 | tf_op jit(solution)/shard_map/ppermute | solution.py:32
  50.6 12.3 %collective-permute-start.13 = (bf16[768,256]{1,0:T(8,128)(2,1)S(1)}, bf16[768,256]{1,0:T(8,128)(2,1)S(1)}, u32[]{:S(2)}, u32[]{:S(2)}) collective-permute-start(bf16[768,256]{1,0:T(8,128)(2,1)S(1)} %collective-permute-done.9.refs_1_), channel_id=1, source_target_pairs={{0,32},{16,48},{32,64},{48,80},{64,96},{80,112},{96,128},{112,144}... | collective-permute-start | bytes 1179656 | tf_op jit(solution)/shard_map/ppermute | solution.py:28
  53.4 16.6 %collective-permute-start.19 = (bf16[768,256]{1,0:T(8,128)(2,1)S(1)}, bf16[768,256]{1,0:T(8,128)(2,1)S(1)}, u32[]{:S(2)}, u32[]{:S(2)}) collective-permute-start(bf16[768,256]{1,0:T(8,128)(2,1)S(1)} %collective-permute-done.11.refs_2_), channel_id=1, source_target_pairs={{0,32},{16,48},{32,64},{48,80},{64,96},{80,112},{96,128},{112,144}... | collective-permute-start | bytes 1179656 | tf_op jit(solution)/shard_map/ppermute | solution.py:28
  62.0 10.4 %collective-permute-start.18 = (bf16[768,256]{1,0:T(8,128)(2,1)S(1)}, bf16[768,256]{1,0:T(8,128)(2,1)S(1)}, u32[]{:S(2)}, u32[]{:S(2)}) collective-permute-start(bf16[768,256]{1,0:T(8,128)(2,1)S(1)} %collective-permute-done.9.refs_1_), channel_id=1, source_target_pairs={{0,16},{16,0},{32,48},{48,32},{64,80},{80,64},{96,112},{112,96},{1... | collective-permute-start | bytes 1179656 | tf_op jit(solution)/shard_map/ppermute | solution.py:32
  63.0 11.2 %copy-start.3 = (bf16[48,2304]{1,0:T(8,128)(2,1)S(1)}, bf16[48,2304]{1,0:T(8,128)(2,1)}, u32[]{:S(2)}) copy-start(bf16[48,2304]{1,0:T(8,128)(2,1)} %refs_7_.1) | copy-start | bytes 663556
  63.0 11.2 %collective-permute-start.17 = (bf16[768,256]{1,0:T(8,128)(2,1)S(1)}, bf16[768,256]{1,0:T(8,128)(2,1)S(1)}, u32[]{:S(2)}, u32[]{:S(2)}) collective-permute-start(bf16[768,256]{1,0:T(8,128)(2,1)S(1)} %collective-permute-done.15.refs_2_), channel_id=1, source_target_pairs={{0,224},{16,240},{32,0},{48,16},{64,32},{80,48},{96,64},{112,80},{... | collective-permute-start | bytes 1179656 | tf_op jit(solution)/shard_map/ppermute | solution.py:28
  81.9 3.5 %collective-permute-start.20 = (bf16[3104,256]{1,0:T(8,128)(2,1)S(1)}, bf16[3104,256]{1,0:T(8,128)(2,1)S(1)}, u32[]{:S(2)}, u32[]{:S(2)}) collective-permute-start(bf16[3104,256]{1,0:T(8,128)(2,1)S(1)} %get-tuple-element.101), channel_id=1, source_target_pairs={{0,1},{1,0},{2,3},{3,2},{4,5},{5,4},{6,7},{7,6},{8,9},{9,8},{10,11... | collective-permute-start | bytes 4767752 | tf_op jit(solution)/shard_map/ppermute | solution.py:44
  85.8 14.3 %collective-permute-start.24 = (bf16[800,256]{1,0:T(8,128)(2,1)S(1)}, bf16[800,256]{1,0:T(8,128)(2,1)S(1)}, u32[]{:S(2)}, u32[]{:S(2)}) collective-permute-start(bf16[800,256]{1,0:T(8,128)(2,1)S(1)} %get-tuple-element.106), channel_id=1, source_target_pairs={{0,2},{1,3},{2,0},{3,1},{4,6},{5,7},{6,4},{7,5},{8,10},{9,11},{10,... | collective-permute-start | bytes 1228808 | tf_op jit(solution)/shard_map/ppermute | solution.py:40
  87.4 12.1 %collective-permute-start.21 = (bf16[384,256]{1,0:T(8,128)(2,1)S(1)}, bf16[384,256]{1,0:T(8,128)(2,1)S(1)}, u32[]{:S(2)}, u32[]{:S(2)}) collective-permute-start(bf16[384,256]{1,0:T(8,128)(2,1)S(1)} %get-tuple-element.103), channel_id=1, source_target_pairs={{0,4},{1,5},{2,6},{3,7},{4,8},{5,9},{6,10},{7,11},{8,12},{9,13},{1... | collective-permute-start | bytes 589832 | tf_op jit(solution)/shard_map/ppermute | solution.py:36
  87.8 11.7 %collective-permute-start.22 = (bf16[384,256]{1,0:T(8,128)(2,1)S(1)}, bf16[384,256]{1,0:T(8,128)(2,1)S(1)}, u32[]{:S(2)}, u32[]{:S(2)}) collective-permute-start(bf16[384,256]{1,0:T(8,128)(2,1)S(1)} %get-tuple-element.104), channel_id=1, source_target_pairs={{0,8},{1,9},{2,10},{3,11},{4,12},{5,13},{6,14},{7,15},{8,0},{9,1},... | collective-permute-start | bytes 589832 | tf_op jit(solution)/shard_map/ppermute | solution.py:36
  89.6 10.5 %collective-permute-start.23 = (bf16[384,256]{1,0:T(8,128)(2,1)S(1)}, bf16[384,256]{1,0:T(8,128)(2,1)S(1)}, u32[]{:S(2)}, u32[]{:S(2)}) collective-permute-start(bf16[384,256]{1,0:T(8,128)(2,1)S(1)} %get-tuple-element.105), channel_id=1, source_target_pairs={{0,12},{1,13},{2,14},{3,15},{4,0},{5,1},{6,2},{7,3},{8,4},{9,5},{1... | collective-permute-start | bytes 589832 | tf_op jit(solution)/shard_map/ppermute | solution.py:36
  100.3 10.0 %collective-permute-start.25 = (bf16[224,256]{1,0:T(8,128)(2,1)S(1)}, bf16[224,256]{1,0:T(8,128)(2,1)S(1)}, u32[]{:S(2)}, u32[]{:S(2)}) collective-permute-start(bf16[224,256]{1,0:T(8,128)(2,1)S(1)} %get-tuple-element.114), channel_id=1, source_target_pairs={{0,4},{1,5},{2,6},{3,7},{4,8},{5,9},{6,10},{7,11},{8,12},{9,13},{1... | collective-permute-start | bytes 344072 | tf_op jit(solution)/shard_map/ppermute | solution.py:36
  100.6 9.7 %collective-permute-start.26 = (bf16[224,256]{1,0:T(8,128)(2,1)S(1)}, bf16[224,256]{1,0:T(8,128)(2,1)S(1)}, u32[]{:S(2)}, u32[]{:S(2)}) collective-permute-start(bf16[224,256]{1,0:T(8,128)(2,1)S(1)} %get-tuple-element.115), channel_id=1, source_target_pairs={{0,8},{1,9},{2,10},{3,11},{4,12},{5,13},{6,14},{7,15},{8,0},{9,1},... | collective-permute-start | bytes 344072 | tf_op jit(solution)/shard_map/ppermute | solution.py:36
  104.1 6.1 %collective-permute-start.27 = (bf16[224,256]{1,0:T(8,128)(2,1)S(1)}, bf16[224,256]{1,0:T(8,128)(2,1)S(1)}, u32[]{:S(2)}, u32[]{:S(2)}) collective-permute-start(bf16[224,256]{1,0:T(8,128)(2,1)S(1)} %get-tuple-element.116), channel_id=1, source_target_pairs={{0,12},{1,13},{2,14},{3,15},{4,0},{5,1},{6,2},{7,3},{8,4},{9,5},{1... | collective-permute-start | bytes 344072 | tf_op jit(solution)/shard_map/ppermute | solution.py:36
  104.1 6.1 %collective-permute-start.28 = (bf16[192,256]{1,0:T(8,128)(2,1)S(1)}, bf16[192,256]{1,0:T(8,128)(2,1)S(1)}, u32[]{:S(2)}, u32[]{:S(2)}) collective-permute-start(bf16[192,256]{1,0:T(8,128)(2,1)S(1)} %get-tuple-element.117), channel_id=1, source_target_pairs={{0,2},{1,3},{2,0},{3,1},{4,6},{5,7},{6,4},{7,5},{8,10},{9,11},{10,... | collective-permute-start | bytes 294920 | tf_op jit(solution)/shard_map/ppermute | solution.py:40

commit v3 on v2

--- a/solution.py
+++ b/solution.py
@@ -13,6 +13,7 @@
 VMEM_LIMIT = 24 * 1024 * 1024
 SMALL_LIMIT = 16 * 1024 * 1024
 TILE = 768
+UPPER = 160
 NT = (((1,), (1,)), ((), ()))
 
 
@@ -115,6 +116,28 @@
         out_specs=VMEM,
         compiler_params=pltpu.CompilerParams(vmem_limit_bytes=SMALL_LIMIT),
     )(*arrays)
+
+
+def whole_kernel(own_ref, other_ref, out_ref):
+    _, _, y, x_hi, core = where_am_i()
+    part = own_ref.shape[2]
+    for other_core, ref in enumerate((own_ref, other_ref)):
+        for n in range(NY):
+            for other_hi in range(2):
+                hi = 1 - x_hi if other_hi else x_hi
+                owner = ((y + n) % NY * 2 + hi) * 2 + (1 - core if other_core else core)
+                out_ref[pl.ds(pl.multiple_of(owner * part, part), part)] = ref[n, other_hi]
+
+
+def whole_amplitudes(own, other):
+    part, columns = own.shape[2:]
+    return pl.pallas_call(
+        whole_kernel,
+        out_shape=jax.ShapeDtypeStruct((RANKS * part, columns), own.dtype),
+        in_specs=[VMEM] * 2,
+        out_specs=VMEM,
+        compiler_params=pltpu.CompilerParams(vmem_limit_bytes=SMALL_LIMIT),
+    )(own, other)
 
 
 def add_kernel(places, first, a_ref, *refs):
@@ -164,39 +187,37 @@
     own, other = {0: piece}, {}
     get = lambda n: other[n - NZ] if n >= NZ else own[n]
     add = lambda places, **rest: add_products(places, [get(n) for n in places], a, **rest)
-    own[7], own[1], other[0], amp_hi, terms, pair_rows = together(
+    own[7], own[1], other[0], amp_hi, terms, pair_rows, sums = together(
         along_z(piece, 1),
         along_z(piece, -1),
         swap_x_lo(piece),
         swap_x_hi(amplitudes),
         energy_terms(tables),
         pair_rows,
+        add([0]),
     )
     amp = pack([amplitudes, amp_hi])
-    sums = add([0, 1, 7, NZ])
-    own[6], own[2], other[1], sums, amp_up, amp_down = together(
-        along_z(own[7], 1),
-        along_z(own[1], -1),
-        swap_x_lo(own[1]),
-        sums,
-        along_y(amp, -1),
-        along_y(amp, 1),
+    sums = add([1, 7, NZ], before=sums)
+    amp_up, amp_down = along_y(amp, -1), along_y(amp, 1)
+    own[6], own[2], other[1], sums = together(
+        along_z(own[7], 1), along_z(own[1], -1), swap_x_lo(own[1]), sums
     )
     sums = add([2, 6, NZ + 1], before=sums)
-    own[5], own[3], other[7], sums, amp_far = together(
-        along_z(own[6], 1), along_z(own[2], -1), swap_x_lo(own[7]), sums, along_y(amp_up, -1)
+    own[5], own[3], other[7], sums, amp_up, amp_down = together(
+        along_z(own[6], 1), along_z(own[2], -1), swap_x_lo(own[7]), sums, amp_up, amp_down
+    )
+    sums = add([3, 5, NZ + 7], before=sums)
+    own[4], other[2], other[3], sums, amp_far = together(
+        along_z(own[5], 1), along_z(other[1], -1), swap_x_lo(own[3]), sums, along_y(amp_up, -1)
     )
     amp_own = pack([amp, amp_up, amp_far, amp_down])
-    sums = add([3, 5, NZ + 7], before=sums)
-    own[4], other[2], other[3], sums, amp_other = together(
-        along_z(own[5], 1), along_z(other[1], -1), swap_x_lo(own[3]), sums, swap_core(amp_own)
-    )
+    amp_other = swap_core(amp_own)
     other[6], other[4], other[5] = (
         along_z(other[7], 1), along_z(other[3], -1), swap_x_lo(own[5])
     )
     sums, stack = add([4, NZ + 2, NZ + 3], before=sums)
     late = [NZ + 4, NZ + 5, NZ + 6]
-    return late, [get(n) for n in late], sums, stack, terms, pair_rows, amp_own, amp_other
+    return late, [get(n) for n in late], sums, stack, terms, pair_rows, whole_amplitudes(amp_own, amp_other)
 
 
 def gamma_dots(goes, left, stack_ref, out_ref):
@@ -215,8 +236,7 @@
     pieces, (before_ref, row_ref, col_ref, pair_ref, coulomb_ref), rest = (
         refs[:count], refs[count : count + 5], refs[count + 5 :]
     )
-    amp_refs, (_, stack_ref, keep_ref, sent_ref, *rest) = rest[:2], rest[2:]
-    left_ref, total, gram, amp_ref = rest
+    amp_ref, _, stack_ref, left_ref, sent_ref, density_ref, total, gram = rest
     products = before_ref[...]
     for place, piece in zip(late, pieces):
         stack_ref[place] = piece[...]
@@ -228,15 +248,6 @@
         )
     x = products.astype(jnp.bfloat16)
 
-    _, _, y, x_hi, core = where_am_i()
-    part = amp_refs[0].shape[2]
-    for other_core, ref in enumerate(amp_refs):
-        for n in range(NY):
-            for other_hi in range(2):
-                hi = 1 - x_hi if other_hi else x_hi
-                owner = ((y + n) % NY * 2 + hi) * 2 + (1 - core if other_core else core)
-                target = pl.ds(pl.multiple_of(owner * part, part), part)
-                amp_ref[target] = ref[n, other_hi]
     tiles = [slice(n, n + TILE) for n in range(0, amp_ref.shape[1], TILE)]
     for n, tile in enumerate(tiles):
         triples = jnp.dot(
@@ -254,10 +265,9 @@
     left_ref[...] = total[...].astype(left_ref.dtype)
 
     gamma_dots(1, left_ref[...], stack_ref, sent_ref)
-    gamma_dots(0, left_ref[...], stack_ref, keep_ref)
 
     rows, occupied = pair_ref.shape
-    width = keep_ref.shape[1]
+    width = sent_ref.shape[1]
     count = rows // occupied
     block = (occupied, rows)
     same = lax.broadcasted_iota(jnp.int32, block, 0) == lax.broadcasted_iota(jnp.int32, block, 1) % occupied
@@ -276,32 +286,51 @@
         preferred_element_type=jnp.float32,
     )
     density = jnp.concatenate([density, jnp.zeros((16 - count, width), jnp.float32)])
-    keep_ref[NZ * rows :] = density
+    density_ref[...] = density
     put_parts(sent_ref, NZ * rows, density)
 
 
-def middle(late, pieces, a, sums, stack, terms, pair_rows, coulomb, amps):
+def middle(late, pieces, a, sums, stack, terms, pair_rows, coulomb, amp):
     rows, virtuals = sums.shape
     width = pieces[0].shape[1]
-    pair_cols = coulomb.shape[1]
     return pl.pallas_call(
         functools.partial(middle_kernel, late),
         out_shape=(
             jax.ShapeDtypeStruct(stack.shape, stack.dtype),
-            jax.ShapeDtypeStruct((NZ * rows + 16, width), jnp.float32),
+            jax.ShapeDtypeStruct((rows, virtuals), jnp.bfloat16),
             jax.ShapeDtypeStruct((NZ * rows + 32, width), jnp.bfloat16),
-        ),
-        in_specs=[VMEM] * (7 + len(late) + len(amps)),
-        out_specs=(VMEM,) * 3,
-        input_output_aliases={6 + len(late) + len(amps): 0},
+            jax.ShapeDtypeStruct((16, width), jnp.float32),
+        ),
+        in_specs=[VMEM] * (8 + len(late)),
+        out_specs=(VMEM,) * 4,
         scratch_shapes=[
-            pltpu.VMEM((rows, virtuals), jnp.bfloat16),
             pltpu.VMEM((rows, virtuals), jnp.float32),
             pltpu.VMEM((rows, rows), jnp.float32),
-            pltpu.VMEM((virtuals, pair_cols), jnp.bfloat16),
         ],
+        input_output_aliases={7 + len(late): 0},
         compiler_params=pltpu.CompilerParams(vmem_limit_bytes=VMEM_LIMIT),
-    )(a, *pieces, sums, *terms, pair_rows, coulomb, *amps, stack)
+    )(a, *pieces, sums, *terms, pair_rows, coulomb, amp, stack)
+
+
+def kept_kernel(left_ref, stack_ref, out_ref):
+    gamma_dots(0, left_ref[...], stack_ref, out_ref)
+
+
+def gamma_kept(left, stack):
+    rows, virtuals = left.shape
+    width = stack.shape[2]
+    return pl.pallas_call(
+        kept_kernel,
+        out_shape=jax.ShapeDtypeStruct((NZ * rows, width), jnp.float32),
+        in_specs=[VMEM, VMEM],
+        out_specs=VMEM,
+        compiler_params=pltpu.CompilerParams(vmem_limit_bytes=SMALL_LIMIT),
+        cost_estimate=pl.CostEstimate(
+            flops=2 * rows * virtuals * width * NZ,
+            bytes_accessed=2 * virtuals * width * NZ,
+            transcendentals=0,
+        ),
+    )(left, stack)
 
 
 def put_parts(ref, first, values):
@@ -318,72 +347,80 @@
     return wide(ref, first, 16) + wide(ref, first + 16, 16)
 
 
-def first_kernel(kept_ref, recv_ref, mine_ref, one_ref, two_ref, three_ref, keep_ref, send_ref, out_ref):
-    half = mine_ref.shape[0] // 2
-    rows = 2 * half
+def first_kernel(kept_ref, own_ref, recv_ref, mine_ref, one_ref, two_ref, three_ref, keep_ref, send_ref, out_ref):
+    upper, lower = mine_ref.shape[0] // 2, keep_ref.shape[0] // NY
+    rows = upper + lower
     for hi in range(2):
         for n, ref in enumerate((mine_ref, one_ref, two_ref, three_ref)):
             first = (hi * NY + n) * rows
-            upper = kept_ref[first : first + half] + wide(recv_ref, first, half)
-            ref[hi * half : (hi + 1) * half] = upper.astype(ref.dtype)
-            lower = kept_ref[first + half : first + rows] + wide(recv_ref, first + half, half)
+            total = kept_ref[first : first + upper] + wide(recv_ref, first, upper)
+            ref[hi * upper : (hi + 1) * upper] = total.astype(ref.dtype)
+            first += upper
+            total = kept_ref[first : first + lower] + wide(recv_ref, first, lower)
             ref = send_ref if hi else keep_ref
-            ref[n * half : (n + 1) * half] = lower.astype(ref.dtype)
-    density = kept_ref[NZ * rows :] + got_parts(recv_ref, NZ * rows)
+            ref[n * lower : (n + 1) * lower] = total.astype(ref.dtype)
+    density = own_ref[...] + got_parts(recv_ref, NZ * rows)
     out_ref[...] = density
-    put_parts(send_ref, NY * half, density)
-
-
-def first_sums(kept, received):
-    rows, width = (kept.shape[0] - 16) // NZ, kept.shape[1]
+    put_parts(send_ref, NY * lower, density)
+
+
+def first_sums(kept, density, received):
+    rows, width = kept.shape[0] // NZ, kept.shape[1]
+    upper, lower = UPPER, rows - UPPER
     shape = lambda n, kind: jax.ShapeDtypeStruct((n, width), kind)
-    message = shape(rows, jnp.bfloat16)
+    message = shape(2 * upper, jnp.bfloat16)
     return pl.pallas_call(
         first_kernel,
         out_shape=(
-            shape(rows, jnp.float32),
+            shape(2 * upper, jnp.float32),
             message,
             message,
             message,
-            shape(NY * rows // 2, jnp.float32),
-            shape(NY * rows // 2 + 32, jnp.bfloat16),
+            shape(NY * lower, jnp.float32),
+            shape(NY * lower + 32, jnp.bfloat16),
             shape(16, jnp.float32),
         ),
-        in_specs=[VMEM] * 2,
+        in_specs=[VMEM] * 3,
         out_specs=(VMEM,) * 7,
         compiler_params=pltpu.CompilerParams(vmem_limit_bytes=SMALL_LIMIT),
-    )(kept, received)
+    )(kept, density, received)
+
+
+def to_owners(messages):
+    one, two, three = messages
+    two = along_y(two, 2)
+    return along_y(one, 1), two, along_y(three, -1)
 
 
 def second_kernel(
     mine_ref, a_ref, b_ref, c_ref, keep_ref, recv_ref, density_ref,
     upper_ref, send_ref, lower_ref, one_ref, two_ref, three_ref, out_ref,
 ):
-    half = upper_ref.shape[0]
+    upper, lower = upper_ref.shape[0], lower_ref.shape[0]
     for hi, ref in enumerate((upper_ref, send_ref)):
-        first = hi * half
-        arrived = sum(wide(other, first, half) for other in (a_ref, b_ref, c_ref))
-        ref[...] = (mine_ref[first : first + half] + arrived).astype(ref.dtype)
-    density = density_ref[...] + got_parts(recv_ref, NY * half)
+        first = hi * upper
+        arrived = sum(wide(other, first, upper) for other in (a_ref, b_ref, c_ref))
+        ref[...] = (mine_ref[first : first + upper] + arrived).astype(ref.dtype)
+    density = density_ref[...] + got_parts(recv_ref, NY * lower)
     out_ref[...] = density
     for n, ref in enumerate((lower_ref, one_ref, two_ref, three_ref)):
-        first = n * half
-        total = keep_ref[first : first + half] + wide(recv_ref, first, half)
-        ref[:half] = total.astype(ref.dtype)
+        first = n * lower
+        total = keep_ref[first : first + lower] + wide(recv_ref, first, lower)
+        ref[:lower] = total.astype(ref.dtype)
         if n:
-            put_parts(ref, half, density)
+            put_parts(ref, lower, density)
 
 
 def second_sums(mine, arrived, keep, received, density):
-    half, width = mine.shape[0] // 2, mine.shape[1]
+    upper, lower, width = mine.shape[0] // 2, keep.shape[0] // NY, mine.shape[1]
     shape = lambda n, kind: jax.ShapeDtypeStruct((n, width), kind)
-    message = shape(half + 32, jnp.bfloat16)
+    message = shape(lower + 32, jnp.bfloat16)
     return pl.pallas_call(
         second_kernel,
         out_shape=(
-            shape(half, jnp.float32),
-            shape(half, jnp.bfloat16),
-            shape(half, jnp.float32),
+            shape(upper, jnp.float32),
+            shape(upper, jnp.bfloat16),
+            shape(lower, jnp.float32),
             message,
             message,
             message,
@@ -398,32 +435,27 @@
 def last_kernel(
     scale, upper_ref, recv_ref, lower_ref, a_ref, b_ref, c_ref, density_ref, gamma_ref, out_ref
 ):
-    half = upper_ref.shape[0]
-    gamma_ref[:half] = upper_ref[...] + wide(recv_ref, 0, half)
+    upper, lower = upper_ref.shape[0], lower_ref.shape[0]
+    gamma_ref[:upper] = upper_ref[...] + wide(recv_ref, 0, upper)
     arrived = (a_ref, b_ref, c_ref)
-    gamma_ref[half:] = lower_ref[...] + sum(wide(ref, 0, half) for ref in arrived)
-    density = density_ref[...] + sum(got_parts(ref, half) for ref in arrived)
+    gamma_ref[upper:] = lower_ref[...] + sum(wide(ref, 0, lower) for ref in arrived)
+    density = density_ref[...] + sum(got_parts(ref, lower) for ref in arrived)
     count = out_ref.shape[0]
     out_ref[...] = density[:count, :count] / scale
 
 
 def last_sums(scale, count, upper, received, lower, arrived, density):
-    half, width = upper.shape
+    rows, width = upper.shape[0] + lower.shape[0], upper.shape[1]
     return pl.pallas_call(
         functools.partial(last_kernel, scale),
         out_shape=(
-            jax.ShapeDtypeStruct((2 * half, width), jnp.float32),
+            jax.ShapeDtypeStruct((rows, width), jnp.float32),
             jax.ShapeDtypeStruct((count, count), jnp.float32),
         ),
         in_specs=[VMEM] * 7,
         out_specs=(VMEM, VMEM),
         compiler_params=pltpu.CompilerParams(vmem_limit_bytes=SMALL_LIMIT),
     )(upper, received, lower, *arrived, density)
-
-
-def to_owners(messages):
-    one, two, three = messages
-    return along_y(one, 1), along_y(two, 2), along_y(three, -1)
 
 
 def body(
@@ -435,11 +467,15 @@
     pair_cols = amplitudes.shape[1]
     vo_rows = b_vo.reshape(rows, aux_all)
     tables = (a_index, b_index, c_index, eps_vir, eps_occ.reshape(1, occupied))
-    late, pieces, sums, stack, terms, pair_rows, *amps = gather_pieces(
+    late, pieces, sums, stack, terms, pair_rows, amp = gather_pieces(
         b_vv[0], amplitudes, pair_amps.reshape(rows, occupied), vo_rows, tables
     )
-    _, kept, sent = middle(late, pieces, vo_rows, sums, stack, terms, pair_rows, coulomb_occ, amps)
-    mine, *messages, keep, send, density = first_sums(kept, swap_core(sent))
+    stack, left, sent, density = middle(
+        late, pieces, vo_rows, sums, stack, terms, pair_rows, coulomb_occ, amp
+    )
+    received = swap_core(sent)
+    kept = gamma_kept(left, stack)
+    mine, *messages, keep, send, density = first_sums(kept, density, received)
     arrived, received = together(to_owners(messages), swap_x_hi(send))
     upper, send, lower, *messages, density = second_sums(mine, arrived, keep, received, density)
     arrived, received = together(to_owners(messages), swap_x_hi(send))

time: 113 us -> 109 us (0.965); the launches traced: 111 us -> 108 us
  waiting for transfers between devices: 53.2 us -> 47.4 us
  starting transfers between devices: 35.6 us -> 38.8 us
    ppermute x10, waiting for transfers between devices: 23.2 us -> 19.5 us  [along_z(): return lax.ppermute(x, 'aa', shift_perm(2 * step))]
    ppermute x10, starting transfers between devices: 12.3 us -> 15.5 us  [along_z(): return lax.ppermute(x, 'aa', shift_perm(2 * step))]
    ppermute x5, waiting for transfers between devices: 7.75 us -> 9.74 us  [swap_x_lo(): return lax.ppermute(x, 'aa', swap_perm(1))]
    pallas_call x2 -> x4, Pallas kernels: 0.51 us -> 2.09 us  [the longest x1 1.42 us: gamma_kept(): pl.pallas_call(kept_kernel, out_shape=jax.ShapeDtypeStruct((NZ * rows, wi...]
    ppermute x2, waiting for transfers between devices: 3.42 us -> 2 us  [swap_core(): return lax.ppermute(x, 'ba', swap_perm(1))]
    pallas_call x1, Pallas kernels: 7.79 us -> 6.48 us  [middle(): pl.pallas_call(functools.partial(middle_kernel, late), out_shape=(jax.Sha...]
    ppermute x9, waiting for transfers between devices: 9.45 us -> 8.2 us  [along_y(): return lax.ppermute(x, 'ba', shift_perm(4 * step))]
    ppermute x3, waiting for transfers between devices: 9.29 us -> 8.06 us  [swap_x_hi(): return lax.ppermute(x, 'ba', swap_perm(2))]
  transfers between devices with their start and end apart: 29 -> 29, of which waited for: 16 -> 17; matrix products, arithmetic and copies ran while one was open for 1% -> 1% of each run, Pallas kernels for 4% -> 6%
where the time goes in v3:
time: 109 us; the launch traced here: 108 us
  waiting for transfers between devices  47.4 us (43%)
  starting transfers between devices  38.8 us (36%)
  Pallas kernels  14.1 us (13%)
  local copies, waits for them, and re-layouts  5.79 us (5%)
  between operations  2.1 us (2%)
    ppermute x10, waiting for transfers between devices, along_z(): return lax.ppermute(x, 'aa', shift_perm(2 * step))  19.5 us
    ppermute x10, starting transfers between devices, along_z(): return lax.ppermute(x, 'aa', shift_perm(2 * step))  15.5 us
    ppermute x9, starting transfers between devices, along_y(): return lax.ppermute(x, 'ba', shift_perm(4 * step))  12.9 us
    ppermute x5, waiting for transfers between devices, swap_x_lo(): return lax.ppermute(x, 'aa', swap_perm(1))  9.74 us
    ppermute x9, waiting for transfers between devices, along_y(): return lax.ppermute(x, 'ba', shift_perm(4 * step))  8.2 us
    ppermute x3, waiting for transfers between devices, swap_x_hi(): return lax.ppermute(x, 'ba', swap_perm(2))  8.06 us
    pallas_call x1, Pallas kernels, middle(): pl.pallas_call(functools.partial(middle_kernel, late), out_shape=(jax.Sha...  6.48 us
    ppermute x3, starting transfers between devices, swap_x_hi(): return lax.ppermute(x, 'ba', swap_perm(2))  5.96 us
  transfers between devices with their start and end apart: 29, of which 17 were waited for; matrix products, arithmetic and copies ran while one was open for 1% of the time, Pallas kernels for 6%

profile of v3, /device:TPU:96, one launch (start us, length us, event | category | flops | bytes accessed | tf_op | source)
XLA Modules:
  0.0 108.3 jit_solution(16789091263681938054)
XLA Ops:
  0.6 1.6 %collective-permute-start.2 = (bf16[768,256]{1,0:T(8,128)(2,1)}, bf16[768,256]{1,0:T(8,128)(2,1)S(1)}, u32[]{:S(2)}, u32[]{:S(2)}) collective-permute-start(bf16[768,256]{1,0:T(8,128)(2,1)} %bitcast.12), channel_id=1, source_target_pairs={{0,16},{16,0},{32,48},{48,32},{64,80},{80,64},{96,112},{112,96},{1... | collective-permute-start | bytes 1179656 | tf_op jit(solution)/shard_map/ppermute | solution.py:33
  2.3 3.1 %collective-permute-start = (bf16[768,256]{1,0:T(8,128)(2,1)}, bf16[768,256]{1,0:T(8,128)(2,1)S(1)}, u32[]{:S(2)}, u32[]{:S(2)}) collective-permute-start(bf16[768,256]{1,0:T(8,128)(2,1)} %bitcast.14), channel_id=1, source_target_pairs={{0,32},{16,48},{32,64},{48,80},{64,96},{80,112},{96,128},{112,144}... | collective-permute-start | bytes 1179656 | tf_op jit(solution)/shard_map/ppermute | solution.py:29
  5.4 2.7 %collective-permute-start.3 = (bf16[48,2304]{1,0:T(8,128)(2,1)}, bf16[48,2304]{1,0:T(8,128)(2,1)S(1)}, u32[]{:S(2)}, u32[]{:S(2)}) collective-permute-start(bf16[48,2304]{1,0:T(8,128)(2,1)} %refs_0_.1), channel_id=1, source_target_pairs={{0,2},{1,3},{2,0},{3,1},{4,6},{5,7},{6,4},{7,5},{8,10},{9,11},{10,... | collective-permute-start | bytes 663560 | tf_op jit(solution)/shard_map/ppermute | solution.py:41
  9.5 0.9 reshape.18.refs_6_
  10.4 0.7 copy-done.4
  11.1 0.7 copy-done.5
  11.7 0.7 copy-done.6
  12.4 0.9 shard_map.113
  13.3 1.9 %copy-done = bf16[8,48,4096]{2,1,0:T(8,128)(2,1)S(1)} copy-done((bf16[8,48,4096]{2,1,0:T(8,128)(2,1)S(1)}, bf16[8,48,4096]{2,1,0:T(8,128)(2,1)}, u32[]{:S(2)}) %copy-start) | copy-done | bytes 3145752
  15.2 1.0 copy-done.1
  16.2 0.4 shard_map.114
  16.6 2.2 %collective-permute-done.3.refs_1_ = bf16[48,2304]{1,0:T(8,128)(2,1)S(1)} collective-permute-done((bf16[48,2304]{1,0:T(8,128)(2,1)}, bf16[48,2304]{1,0:T(8,128)(2,1)S(1)}, u32[]{:S(2)}, u32[]{:S(2)}) %collective-permute-start.3) | collective-permute-done | bytes 221216 | tf_op jit(solution)/shard_map/ppermute | solution.py:41
  18.7 3.2 %collective-permute-start.4 = (bf16[768,256]{1,0:T(8,128)(2,1)S(1)}, bf16[768,256]{1,0:T(8,128)(2,1)S(1)}, u32[]{:S(2)}, u32[]{:S(2)}) collective-permute-start(bf16[768,256]{1,0:T(8,128)(2,1)S(1)} %collective-permute-done.refs_1_), channel_id=1, source_target_pairs={{0,32},{16,48},{32,64},{48,80},{64,96},{80,112},{96,128},{112,144}... | collective-permute-start | bytes 1179656 | tf_op jit(solution)/shard_map/ppermute | solution.py:29
  22.2 1.7 %collective-permute-start.11 = (bf16[2,48,2304]{2,1,0:T(8,128)(2,1)S(1)}, bf16[2,48,2304]{2,1,0:T(8,128)(2,1)S(1)}, u32[]{:S(2)}, u32[]{:S(2)}) collective-permute-start(bf16[2,48,2304]{2,1,0:T(8,128)(2,1)S(1)} %shard_map.117.refs_0_), channel_id=1, source_target_pairs={{0,4},{1,5},{2,6},{3,7},{4,8},{5,9},{6,10},{7,11},{8,12},{9,13},{1... | collective-permute-start | bytes 1327112 | tf_op jit(solution)/shard_map/ppermute | solution.py:37
  23.9 1.7 %collective-permute-start.10 = (bf16[2,48,2304]{2,1,0:T(8,128)(2,1)S(1)}, bf16[2,48,2304]{2,1,0:T(8,128)(2,1)S(1)}, u32[]{:S(2)}, u32[]{:S(2)}) collective-permute-start(bf16[2,48,2304]{2,1,0:T(8,128)(2,1)S(1)} %shard_map.117.refs_0_), channel_id=1, source_target_pairs={{0,12},{1,13},{2,14},{3,15},{4,0},{5,1},{6,2},{7,3},{8,4},{9,5},{1... | collective-permute-start | bytes 1327112 | tf_op jit(solution)/shard_map/ppermute | solution.py:37
  25.5 0.8 shard_map.115
  26.4 3.1 %collective-permute-done.4.refs_1_ = bf16[768,256]{1,0:T(8,128)(2,1)S(1)} collective-permute-done((bf16[768,256]{1,0:T(8,128)(2,1)S(1)}, bf16[768,256]{1,0:T(8,128)(2,1)S(1)}, u32[]{:S(2)}, u32[]{:S(2)}) %collective-permute-start.4) | collective-permute-done | bytes 393248 | tf_op jit(solution)/shard_map/ppermute | solution.py:29
  29.7 3.5 %collective-permute-done.6.refs_2_ = bf16[768,256]{1,0:T(8,128)(2,1)S(1)} collective-permute-done((bf16[768,256]{1,0:T(8,128)(2,1)S(1)}, bf16[768,256]{1,0:T(8,128)(2,1)S(1)}, u32[]{:S(2)}, u32[]{:S(2)}) %collective-permute-start.6) | collective-permute-done | bytes 393248 | tf_op jit(solution)/shard_map/ppermute | solution.py:33
  33.4 1.8 %collective-permute-start.8 = (bf16[768,256]{1,0:T(8,128)(2,1)S(1)}, bf16[768,256]{1,0:T(8,128)(2,1)S(1)}, u32[]{:S(2)}, u32[]{:S(2)}) collective-permute-start(bf16[768,256]{1,0:T(8,128)(2,1)S(1)} %collective-permute-done.5.refs_0_), channel_id=1, source_target_pairs={{0,224},{16,240},{32,0},{48,16},{64,32},{80,48},{96,64},{112,80},{... | collective-permute-start | bytes 1179656 | tf_op jit(solution)/shard_map/ppermute | solution.py:29
  35.2 0.8 shard_map.116
  36.0 4.1 %collective-permute-done.9.refs_2_ = bf16[768,256]{1,0:T(8,128)(2,1)S(1)} collective-permute-done((bf16[768,256]{1,0:T(8,128)(2,1)S(1)}, bf16[768,256]{1,0:T(8,128)(2,1)S(1)}, u32[]{:S(2)}, u32[]{:S(2)}) %collective-permute-start.9) | collective-permute-done | bytes 393248 | tf_op jit(solution)/shard_map/ppermute | solution.py:33
  40.1 1.3 %collective-permute-done.7.refs_1_ = bf16[768,256]{1,0:T(8,128)(2,1)S(1)} collective-permute-done((bf16[768,256]{1,0:T(8,128)(2,1)S(1)}, bf16[768,256]{1,0:T(8,128)(2,1)S(1)}, u32[]{:S(2)}, u32[]{:S(2)}) %collective-permute-start.7) | collective-permute-done | bytes 393248 | tf_op jit(solution)/shard_map/ppermute | solution.py:29
  41.4 1.8 %collective-permute-done.8.refs_0_ = bf16[768,256]{1,0:T(8,128)(2,1)S(1)} collective-permute-done((bf16[768,256]{1,0:T(8,128)(2,1)S(1)}, bf16[768,256]{1,0:T(8,128)(2,1)S(1)}, u32[]{:S(2)}, u32[]{:S(2)}) %collective-permute-start.8) | collective-permute-done | bytes 393248 | tf_op jit(solution)/shard_map/ppermute | solution.py:29
  43.2 3.0 %collective-permute-start.15 = (bf16[2,48,2304]{2,1,0:T(8,128)(2,1)S(1)}, bf16[2,48,2304]{2,1,0:T(8,128)(2,1)S(1)}, u32[]{:S(2)}, u32[]{:S(2)}) collective-permute-start(bf16[2,48,2304]{2,1,0:T(8,128)(2,1)S(1)} %collective-permute-done.10.refs_1_), channel_id=1, source_target_pairs={{0,12},{1,13},{2,14},{3,15},{4,0},{5,1},{6,2},{7,3},{8,4},{9,5},{1... | collective-permute-start | bytes 1327112 | tf_op jit(solution)/shard_map/ppermute | solution.py:37
  46.2 1.7 %collective-permute-start.14 = (bf16[768,256]{1,0:T(8,128)(2,1)S(1)}, bf16[768,256]{1,0:T(8,128)(2,1)S(1)}, u32[]{:S(2)}, u32[]{:S(2)}) collective-permute-start(bf16[768,256]{1,0:T(8,128)(2,1)S(1)} %collective-permute-done.8.refs_0_), channel_id=1, source_target_pairs={{0,16},{16,0},{32,48},{48,32},{64,80},{80,64},{96,112},{112,96},{1... | collective-permute-start | bytes 1179656 | tf_op jit(solution)/shard_map/ppermute | solution.py:33
  47.9 3.2 %collective-permute-start.12 = (bf16[768,256]{1,0:T(8,128)(2,1)S(1)}, bf16[768,256]{1,0:T(8,128)(2,1)S(1)}, u32[]{:S(2)}, u32[]{:S(2)}) collective-permute-start(bf16[768,256]{1,0:T(8,128)(2,1)S(1)} %collective-permute-done.7.refs_1_), channel_id=1, source_target_pairs={{0,32},{16,48},{32,64},{48,80},{64,96},{80,112},{96,128},{112,144}... | collective-permute-start | bytes 1179656 | tf_op jit(solution)/shard_map/ppermute | solution.py:29
  51.1 0.8 shard_map.118
  52.0 3.2 %collective-permute-done.13.refs_1_ = bf16[768,256]{1,0:T(8,128)(2,1)S(1)} collective-permute-done((bf16[768,256]{1,0:T(8,128)(2,1)S(1)}, bf16[768,256]{1,0:T(8,128)(2,1)S(1)}, u32[]{:S(2)}, u32[]{:S(2)}) %collective-permute-start.13) | collective-permute-done | bytes 393248 | tf_op jit(solution)/shard_map/ppermute | solution.py:29
  55.2 1.2 %collective-permute-done.12.refs_0_ = bf16[768,256]{1,0:T(8,128)(2,1)S(1)} collective-permute-done((bf16[768,256]{1,0:T(8,128)(2,1)S(1)}, bf16[768,256]{1,0:T(8,128)(2,1)S(1)}, u32[]{:S(2)}, u32[]{:S(2)}) %collective-permute-start.12) | collective-permute-done | bytes 393248 | tf_op jit(solution)/shard_map/ppermute | solution.py:29
  56.6 3.8 %collective-permute-start.18 = (bf16[768,256]{1,0:T(8,128)(2,1)S(1)}, bf16[768,256]{1,0:T(8,128)(2,1)S(1)}, u32[]{:S(2)}, u32[]{:S(2)}) collective-permute-start(bf16[768,256]{1,0:T(8,128)(2,1)S(1)} %collective-permute-done.9.refs_2_), channel_id=1, source_target_pairs={{0,32},{16,48},{32,64},{48,80},{64,96},{80,112},{96,128},{112,144}... | collective-permute-start | bytes 1179656 | tf_op jit(solution)/shard_map/ppermute | solution.py:29
  60.8 0.8 shard_map.119
  61.9 7.5 %collective-permute-done.18.refs_2_ = bf16[768,256]{1,0:T(8,128)(2,1)S(1)} collective-permute-done((bf16[768,256]{1,0:T(8,128)(2,1)S(1)}, bf16[768,256]{1,0:T(8,128)(2,1)S(1)}, u32[]{:S(2)}, u32[]{:S(2)}) %collective-permute-start.18) | collective-permute-done | bytes 393248 | tf_op jit(solution)/shard_map/ppermute | solution.py:29
  69.4 2.2 %collective-permute-done.17.refs_1_ = bf16[768,256]{1,0:T(8,128)(2,1)S(1)} collective-permute-done((bf16[768,256]{1,0:T(8,128)(2,1)S(1)}, bf16[768,256]{1,0:T(8,128)(2,1)S(1)}, u32[]{:S(2)}, u32[]{:S(2)}) %collective-permute-start.17) | collective-permute-done | bytes 393248 | tf_op jit(solution)/shard_map/ppermute | solution.py:33
  71.6 1.3 %collective-permute-done.16.refs_0_ = bf16[768,256]{1,0:T(8,128)(2,1)S(1)} collective-permute-done((bf16[768,256]{1,0:T(8,128)(2,1)S(1)}, bf16[768,256]{1,0:T(8,128)(2,1)S(1)}, u32[]{:S(2)}, u32[]{:S(2)}) %collective-permute-start.16) | collective-permute-done | bytes 393248 | tf_op jit(solution)/shard_map/ppermute | solution.py:29
  72.9 6.5 %shard_map.122 = (bf16[16,768,256]{2,1,0:T(8,128)(2,1)S(1)}, bf16[384,768]{1,0:T(8,128)(2,1)S(1)}, bf16[3104,256]{1,0:T(8,128)(2,1)S(1)}, f32[16,256]{1,0:T(8,128)S(1)}) custom-call(bf16[384,4096]{1,0:T(8,128)(2,1)S(1)} %bitcast.11, bf16[768,256]{1,0:T(8,128)(2,1)S(1)} %collective-permute-done.16.refs_0_, ...), custom_call_target="tpu_custom_call", output_to_operand_aliasing={{0}: (10, {})} | custom-call | tf_op jit(solution)/shard_map/pallas_call | solution.py:296
  79.7 1.4 %shard_map.123.kept_ref = f32[3072,256]{1,0:T(8,128)S(1)} custom-call(bf16[384,768]{1,0:T(8,128)(2,1)S(1)} %get-tuple-element.108.left_ref, bf16[16,768,256]{2,1,0:T(8,128)(2,1)S(1)} %get-tuple-element.109.stack_ref), custom_call_target="tpu_custom_call" | custom-call | flops 1207959552 | bytes 3145728 | tf_op jit(solution)/shard_map/pallas_call | solution.py:322
  81.1 2.0 %collective-permute-done.20.recv_ref = bf16[3104,256]{1,0:T(8,128)(2,1)S(1)} collective-permute-done((bf16[3104,256]{1,0:T(8,128)(2,1)S(1)}, bf16[3104,256]{1,0:T(8,128)(2,1)S(1)}, u32[]{:S(2)}, u32[]{:S(2)}) %collective-permute-start.20) | collective-permute-done | bytes 1589280 | tf_op jit(solution)/shard_map/ppermute | solution.py:45
  83.4 1.7 %collective-permute-start.24 = (bf16[928,256]{1,0:T(8,128)(2,1)S(1)}, bf16[928,256]{1,0:T(8,128)(2,1)S(1)}, u32[]{:S(2)}, u32[]{:S(2)}) collective-permute-start(bf16[928,256]{1,0:T(8,128)(2,1)S(1)} %get-tuple-element.116), channel_id=1, source_target_pairs={{0,2},{1,3},{2,0},{3,1},{4,6},{5,7},{6,4},{7,5},{8,10},{9,11},{10,... | collective-permute-start | bytes 1425416 | tf_op jit(solution)/shard_map/ppermute | solution.py:41
  85.0 2.2 %collective-permute-start.22 = (bf16[320,256]{1,0:T(8,128)(2,1)S(1)}, bf16[320,256]{1,0:T(8,128)(2,1)S(1)}, u32[]{:S(2)}, u32[]{:S(2)}) collective-permute-start(bf16[320,256]{1,0:T(8,128)(2,1)S(1)} %get-tuple-element.114), channel_id=1, source_target_pairs={{0,8},{1,9},{2,10},{3,11},{4,12},{5,13},{6,14},{7,15},{8,0},{9,1},... | collective-permute-start | bytes 491528 | tf_op jit(solution)/shard_map/ppermute | solution.py:37
  87.3 1.0 collective-permute-start.23
  88.3 7.4 %collective-permute-done.21.a_ref = bf16[320,256]{1,0:T(8,128)(2,1)S(1)} collective-permute-done((bf16[320,256]{1,0:T(8,128)(2,1)S(1)}, bf16[320,256]{1,0:T(8,128)(2,1)S(1)}, u32[]{:S(2)}, u32[]{:S(2)}) %collective-permute-start.21) | collective-permute-done | bytes 163872 | tf_op jit(solution)/shard_map/ppermute | solution.py:37
  95.7 0.6 collective-permute-done.23.c_ref
  96.4 1.5 %collective-permute-done.24.recv_ref = bf16[928,256]{1,0:T(8,128)(2,1)S(1)} collective-permute-done((bf16[928,256]{1,0:T(8,128)(2,1)S(1)}, bf16[928,256]{1,0:T(8,128)(2,1)S(1)}, u32[]{:S(2)}, u32[]{:S(2)}) %collective-permute-start.24) | collective-permute-done | bytes 475168 | tf_op jit(solution)/shard_map/ppermute | solution.py:41
  98.1 2.3 %collective-permute-start.26 = (bf16[256,256]{1,0:T(8,128)(2,1)S(1)}, bf16[256,256]{1,0:T(8,128)(2,1)S(1)}, u32[]{:S(2)}, u32[]{:S(2)}) collective-permute-start(bf16[256,256]{1,0:T(8,128)(2,1)S(1)} %get-tuple-element.125), channel_id=1, source_target_pairs={{0,8},{1,9},{2,10},{3,11},{4,12},{5,13},{6,14},{7,15},{8,0},{9,1},... | collective-permute-start | bytes 393224 | tf_op jit(solution)/shard_map/ppermute | solution.py:37
  100.4 1.0 collective-permute-start.27
  101.4 1.6 %collective-permute-start.28 = (bf16[160,256]{1,0:T(8,128)(2,1)S(1)}, bf16[160,256]{1,0:T(8,128)(2,1)S(1)}, u32[]{:S(2)}, u32[]{:S(2)}) collective-permute-start(bf16[160,256]{1,0:T(8,128)(2,1)S(1)} %get-tuple-element.127), channel_id=1, source_target_pairs={{0,2},{1,3},{2,0},{3,1},{4,6},{5,7},{6,4},{7,5},{8,10},{9,11},{10,... | collective-permute-start | bytes 245768 | tf_op jit(solution)/shard_map/ppermute | solution.py:41
  102.9 4.4 %collective-permute-done.28.recv_ref = bf16[160,256]{1,0:T(8,128)(2,1)S(1)} collective-permute-done((bf16[160,256]{1,0:T(8,128)(2,1)S(1)}, bf16[160,256]{1,0:T(8,128)(2,1)S(1)}, u32[]{:S(2)}, u32[]{:S(2)}) %collective-permute-start.28) | collective-permute-done | bytes 81952 | tf_op jit(solution)/shard_map/ppermute | solution.py:41
  107.5 0.8 shard_map.126
  (39 shorter events, 2.6 us)
Async XLA Ops:
  0.6 18.1 %collective-permute-start.2 = (bf16[768,256]{1,0:T(8,128)(2,1)}, bf16[768,256]{1,0:T(8,128)(2,1)S(1)}, u32[]{:S(2)}, u32[]{:S(2)}) collective-permute-start(bf16[768,256]{1,0:T(8,128)(2,1)} %bitcast.12), channel_id=1, source_target_pairs={{0,16},{16,0},{32,48},{48,32},{64,80},{80,64},{96,112},{112,96},{1... | collective-permute-start | bytes 1179656 | tf_op jit(solution)/shard_map/ppermute | solution.py:33
  2.2 16.5 %collective-permute-start.1 = (bf16[768,256]{1,0:T(8,128)(2,1)}, bf16[768,256]{1,0:T(8,128)(2,1)S(1)}, u32[]{:S(2)}, u32[]{:S(2)}) collective-permute-start(bf16[768,256]{1,0:T(8,128)(2,1)} %bitcast.13), channel_id=1, source_target_pairs={{0,224},{16,240},{32,0},{48,16},{64,32},{80,48},{96,64},{112,80},{... | collective-permute-start | bytes 1179656 | tf_op jit(solution)/shard_map/ppermute | solution.py:29
  2.3 16.4 %collective-permute-start = (bf16[768,256]{1,0:T(8,128)(2,1)}, bf16[768,256]{1,0:T(8,128)(2,1)S(1)}, u32[]{:S(2)}, u32[]{:S(2)}) collective-permute-start(bf16[768,256]{1,0:T(8,128)(2,1)} %bitcast.14), channel_id=1, source_target_pairs={{0,32},{16,48},{32,64},{48,80},{64,96},{80,112},{96,128},{112,144}... | collective-permute-start | bytes 1179656 | tf_op jit(solution)/shard_map/ppermute | solution.py:29
  5.4 13.3 %collective-permute-start.3 = (bf16[48,2304]{1,0:T(8,128)(2,1)}, bf16[48,2304]{1,0:T(8,128)(2,1)S(1)}, u32[]{:S(2)}, u32[]{:S(2)}) collective-permute-start(bf16[48,2304]{1,0:T(8,128)(2,1)} %refs_0_.1), channel_id=1, source_target_pairs={{0,2},{1,3},{2,0},{3,1},{4,6},{5,7},{6,4},{7,5},{8,10},{9,11},{10,... | collective-permute-start | bytes 663560 | tf_op jit(solution)/shard_map/ppermute | solution.py:41
  10.4 0.7 copy-start.4
  11.1 0.7 copy-start.5
  11.7 0.7 copy-start.6
  13.3 1.9 %copy-start = (bf16[8,48,4096]{2,1,0:T(8,128)(2,1)S(1)}, bf16[8,48,4096]{2,1,0:T(8,128)(2,1)}, u32[]{:S(2)}) copy-start(bf16[8,48,4096]{2,1,0:T(8,128)(2,1)} %param.10) | copy-start | bytes 9437188
  15.2 1.0 copy-start.1
  16.2 6.0 %copy-start.2 = (bf16[48,2304]{1,0:T(8,128)(2,1)S(1)}, bf16[48,2304]{1,0:T(8,128)(2,1)}, u32[]{:S(2)}) copy-start(bf16[48,2304]{1,0:T(8,128)(2,1)} %refs_0_.1) | copy-start | bytes 663556
  18.7 10.7 %collective-permute-start.4 = (bf16[768,256]{1,0:T(8,128)(2,1)S(1)}, bf16[768,256]{1,0:T(8,128)(2,1)S(1)}, u32[]{:S(2)}, u32[]{:S(2)}) collective-permute-start(bf16[768,256]{1,0:T(8,128)(2,1)S(1)} %collective-permute-done.refs_1_), channel_id=1, source_target_pairs={{0,32},{16,48},{32,64},{48,80},{64,96},{80,112},{96,128},{112,144}... | collective-permute-start | bytes 1179656 | tf_op jit(solution)/shard_map/ppermute | solution.py:29
  21.9 11.2 %collective-permute-start.6 = (bf16[768,256]{1,0:T(8,128)(2,1)S(1)}, bf16[768,256]{1,0:T(8,128)(2,1)S(1)}, u32[]{:S(2)}, u32[]{:S(2)}) collective-permute-start(bf16[768,256]{1,0:T(8,128)(2,1)S(1)} %collective-permute-done.1.refs_0_), channel_id=1, source_target_pairs={{0,16},{16,0},{32,48},{48,32},{64,80},{80,64},{96,112},{112,96},{1... | collective-permute-start | bytes 1179656 | tf_op jit(solution)/shard_map/ppermute | solution.py:33
  22.2 11.0 %collective-permute-start.5 = (bf16[768,256]{1,0:T(8,128)(2,1)S(1)}, bf16[768,256]{1,0:T(8,128)(2,1)S(1)}, u32[]{:S(2)}, u32[]{:S(2)}) collective-permute-start(bf16[768,256]{1,0:T(8,128)(2,1)S(1)} %collective-permute-done.1.refs_0_), channel_id=1, source_target_pairs={{0,224},{16,240},{32,0},{48,16},{64,32},{80,48},{96,64},{112,80},{... | collective-permute-start | bytes 1179656 | tf_op jit(solution)/shard_map/ppermute | solution.py:29
  22.2 17.9 %collective-permute-start.11 = (bf16[2,48,2304]{2,1,0:T(8,128)(2,1)S(1)}, bf16[2,48,2304]{2,1,0:T(8,128)(2,1)S(1)}, u32[]{:S(2)}, u32[]{:S(2)}) collective-permute-start(bf16[2,48,2304]{2,1,0:T(8,128)(2,1)S(1)} %shard_map.117.refs_0_), channel_id=1, source_target_pairs={{0,4},{1,5},{2,6},{3,7},{4,8},{5,9},{6,10},{7,11},{8,12},{9,13},{1... | collective-permute-start | bytes 1327112 | tf_op jit(solution)/shard_map/ppermute | solution.py:37
  23.9 16.2 %collective-permute-start.10 = (bf16[2,48,2304]{2,1,0:T(8,128)(2,1)S(1)}, bf16[2,48,2304]{2,1,0:T(8,128)(2,1)S(1)}, u32[]{:S(2)}, u32[]{:S(2)}) collective-permute-start(bf16[2,48,2304]{2,1,0:T(8,128)(2,1)S(1)} %shard_map.117.refs_0_), channel_id=1, source_target_pairs={{0,12},{1,13},{2,14},{3,15},{4,0},{5,1},{6,2},{7,3},{8,4},{9,5},{1... | collective-permute-start | bytes 1327112 | tf_op jit(solution)/shard_map/ppermute | solution.py:37
  29.4 10.6 %collective-permute-start.9 = (bf16[768,256]{1,0:T(8,128)(2,1)S(1)}, bf16[768,256]{1,0:T(8,128)(2,1)S(1)}, u32[]{:S(2)}, u32[]{:S(2)}) collective-permute-start(bf16[768,256]{1,0:T(8,128)(2,1)S(1)} %collective-permute-done.refs_1_), channel_id=1, source_target_pairs={{0,16},{16,0},{32,48},{48,32},{64,80},{80,64},{96,112},{112,96},{1... | collective-permute-start | bytes 1179656 | tf_op jit(solution)/shard_map/ppermute | solution.py:33
  33.1 8.3 %collective-permute-start.7 = (bf16[768,256]{1,0:T(8,128)(2,1)S(1)}, bf16[768,256]{1,0:T(8,128)(2,1)S(1)}, u32[]{:S(2)}, u32[]{:S(2)}) collective-permute-start(bf16[768,256]{1,0:T(8,128)(2,1)S(1)} %collective-permute-done.4.refs_1_), channel_id=1, source_target_pairs={{0,32},{16,48},{32,64},{48,80},{64,96},{80,112},{96,128},{112,144}... | collective-permute-start | bytes 1179656 | tf_op jit(solution)/shard_map/ppermute | solution.py:29
  33.4 9.9 %collective-permute-start.8 = (bf16[768,256]{1,0:T(8,128)(2,1)S(1)}, bf16[768,256]{1,0:T(8,128)(2,1)S(1)}, u32[]{:S(2)}, u32[]{:S(2)}) collective-permute-start(bf16[768,256]{1,0:T(8,128)(2,1)S(1)} %collective-permute-done.5.refs_0_), channel_id=1, source_target_pairs={{0,224},{16,240},{32,0},{48,16},{64,32},{80,48},{96,64},{112,80},{... | collective-permute-start | bytes 1179656 | tf_op jit(solution)/shard_map/ppermute | solution.py:29
  43.2 13.2 %collective-permute-start.15 = (bf16[2,48,2304]{2,1,0:T(8,128)(2,1)S(1)}, bf16[2,48,2304]{2,1,0:T(8,128)(2,1)S(1)}, u32[]{:S(2)}, u32[]{:S(2)}) collective-permute-start(bf16[2,48,2304]{2,1,0:T(8,128)(2,1)S(1)} %collective-permute-done.10.refs_1_), channel_id=1, source_target_pairs={{0,12},{1,13},{2,14},{3,15},{4,0},{5,1},{6,2},{7,3},{8,4},{9,5},{1... | collective-permute-start | bytes 1327112 | tf_op jit(solution)/shard_map/ppermute | solution.py:37
  46.2 9.0 %collective-permute-start.13 = (bf16[768,256]{1,0:T(8,128)(2,1)S(1)}, bf16[768,256]{1,0:T(8,128)(2,1)S(1)}, u32[]{:S(2)}, u32[]{:S(2)}) collective-permute-start(bf16[768,256]{1,0:T(8,128)(2,1)S(1)} %collective-permute-done.6.refs_2_), channel_id=1, source_target_pairs={{0,224},{16,240},{32,0},{48,16},{64,32},{80,48},{96,64},{112,80},{... | collective-permute-start | bytes 1179656 | tf_op jit(solution)/shard_map/ppermute | solution.py:29
  46.2 9.0 %collective-permute-start.14 = (bf16[768,256]{1,0:T(8,128)(2,1)S(1)}, bf16[768,256]{1,0:T(8,128)(2,1)S(1)}, u32[]{:S(2)}, u32[]{:S(2)}) collective-permute-start(bf16[768,256]{1,0:T(8,128)(2,1)S(1)} %collective-permute-done.8.refs_0_), channel_id=1, source_target_pairs={{0,16},{16,0},{32,48},{48,32},{64,80},{80,64},{96,112},{112,96},{1... | collective-permute-start | bytes 1179656 | tf_op jit(solution)/shard_map/ppermute | solution.py:33
  47.9 8.5 %collective-permute-start.12 = (bf16[768,256]{1,0:T(8,128)(2,1)S(1)}, bf16[768,256]{1,0:T(8,128)(2,1)S(1)}, u32[]{:S(2)}, u32[]{:S(2)}) collective-permute-start(bf16[768,256]{1,0:T(8,128)(2,1)S(1)} %collective-permute-done.7.refs_1_), channel_id=1, source_target_pairs={{0,32},{16,48},{32,64},{48,80},{64,96},{80,112},{96,128},{112,144}... | collective-permute-start | bytes 1179656 | tf_op jit(solution)/shard_map/ppermute | solution.py:29
  56.5 5.1 %collective-permute-start.19 = (bf16[4,2,48,2304]{3,2,1,0:T(8,128)(2,1)S(1)}, bf16[4,2,48,2304]{3,2,1,0:T(8,128)(2,1)S(1)}, u32[]{:S(2)}, u32[]{:S(2)}) collective-permute-start(bf16[4,2,48,2304]{3,2,1,0:T(8,128)(2,1)S(1)} %shard_map.120.own_ref), channel_id=1, source_target_pairs={{0,1},{1,0},{2,3},{3,2},{4,5},{5,4},{6,7},{7,6},{8,9},{9,8},{10,11... | collective-permute-start | bytes 5308424 | tf_op jit(solution)/shard_map/ppermute | solution.py:45
  56.6 12.7 %collective-permute-start.18 = (bf16[768,256]{1,0:T(8,128)(2,1)S(1)}, bf16[768,256]{1,0:T(8,128)(2,1)S(1)}, u32[]{:S(2)}, u32[]{:S(2)}) collective-permute-start(bf16[768,256]{1,0:T(8,128)(2,1)S(1)} %collective-permute-done.9.refs_2_), channel_id=1, source_target_pairs={{0,32},{16,48},{32,64},{48,80},{64,96},{80,112},{96,128},{112,144}... | collective-permute-start | bytes 1179656 | tf_op jit(solution)/shard_map/ppermute | solution.py:29
  60.4 11.2 %collective-permute-start.17 = (bf16[768,256]{1,0:T(8,128)(2,1)S(1)}, bf16[768,256]{1,0:T(8,128)(2,1)S(1)}, u32[]{:S(2)}, u32[]{:S(2)}) collective-permute-start(bf16[768,256]{1,0:T(8,128)(2,1)S(1)} %collective-permute-done.7.refs_1_), channel_id=1, source_target_pairs={{0,16},{16,0},{32,48},{48,32},{64,80},{80,64},{96,112},{112,96},{1... | collective-permute-start | bytes 1179656 | tf_op jit(solution)/shard_map/ppermute | solution.py:33
  60.8 12.1 %collective-permute-start.16 = (bf16[768,256]{1,0:T(8,128)(2,1)S(1)}, bf16[768,256]{1,0:T(8,128)(2,1)S(1)}, u32[]{:S(2)}, u32[]{:S(2)}) collective-permute-start(bf16[768,256]{1,0:T(8,128)(2,1)S(1)} %collective-permute-done.14.refs_2_), channel_id=1, source_target_pairs={{0,224},{16,240},{32,0},{48,16},{64,32},{80,48},{96,64},{112,80},{... | collective-permute-start | bytes 1179656 | tf_op jit(solution)/shard_map/ppermute | solution.py:29
  61.6 11.3 %copy-start.3 = (bf16[48,2304]{1,0:T(8,128)(2,1)S(1)}, bf16[48,2304]{1,0:T(8,128)(2,1)}, u32[]{:S(2)}) copy-start(bf16[48,2304]{1,0:T(8,128)(2,1)} %refs_7_.1) | copy-start | bytes 663556
  79.4 3.7 %collective-permute-start.20 = (bf16[3104,256]{1,0:T(8,128)(2,1)S(1)}, bf16[3104,256]{1,0:T(8,128)(2,1)S(1)}, u32[]{:S(2)}, u32[]{:S(2)}) collective-permute-start(bf16[3104,256]{1,0:T(8,128)(2,1)S(1)} %get-tuple-element.111), channel_id=1, source_target_pairs={{0,1},{1,0},{2,3},{3,2},{4,5},{5,4},{6,7},{7,6},{8,9},{9,8},{10,11... | collective-permute-start | bytes 4767752 | tf_op jit(solution)/shard_map/ppermute | solution.py:45
  83.4 14.5 %collective-permute-start.24 = (bf16[928,256]{1,0:T(8,128)(2,1)S(1)}, bf16[928,256]{1,0:T(8,128)(2,1)S(1)}, u32[]{:S(2)}, u32[]{:S(2)}) collective-permute-start(bf16[928,256]{1,0:T(8,128)(2,1)S(1)} %get-tuple-element.116), channel_id=1, source_target_pairs={{0,2},{1,3},{2,0},{3,1},{4,6},{5,7},{6,4},{7,5},{8,10},{9,11},{10,... | collective-permute-start | bytes 1425416 | tf_op jit(solution)/shard_map/ppermute | solution.py:41
  85.0 10.7 %collective-permute-start.21 = (bf16[320,256]{1,0:T(8,128)(2,1)S(1)}, bf16[320,256]{1,0:T(8,128)(2,1)S(1)}, u32[]{:S(2)}, u32[]{:S(2)}) collective-permute-start(bf16[320,256]{1,0:T(8,128)(2,1)S(1)} %get-tuple-element.113), channel_id=1, source_target_pairs={{0,4},{1,5},{2,6},{3,7},{4,8},{5,9},{6,10},{7,11},{8,12},{9,13},{1... | collective-permute-start | bytes 491528 | tf_op jit(solution)/shard_map/ppermute | solution.py:37
  85.0 10.7 %collective-permute-start.22 = (bf16[320,256]{1,0:T(8,128)(2,1)S(1)}, bf16[320,256]{1,0:T(8,128)(2,1)S(1)}, u32[]{:S(2)}, u32[]{:S(2)}) collective-permute-start(bf16[320,256]{1,0:T(8,128)(2,1)S(1)} %get-tuple-element.114), channel_id=1, source_target_pairs={{0,8},{1,9},{2,10},{3,11},{4,12},{5,13},{6,14},{7,15},{8,0},{9,1},... | collective-permute-start | bytes 491528 | tf_op jit(solution)/shard_map/ppermute | solution.py:37
  87.3 9.1 %collective-permute-start.23 = (bf16[320,256]{1,0:T(8,128)(2,1)S(1)}, bf16[320,256]{1,0:T(8,128)(2,1)S(1)}, u32[]{:S(2)}, u32[]{:S(2)}) collective-permute-start(bf16[320,256]{1,0:T(8,128)(2,1)S(1)} %get-tuple-element.115), channel_id=1, source_target_pairs={{0,12},{1,13},{2,14},{3,15},{4,0},{5,1},{6,2},{7,3},{8,4},{9,5},{1... | collective-permute-start | bytes 491528 | tf_op jit(solution)/shard_map/ppermute | solution.py:37
  98.0 9.3 %collective-permute-start.25 = (bf16[256,256]{1,0:T(8,128)(2,1)S(1)}, bf16[256,256]{1,0:T(8,128)(2,1)S(1)}, u32[]{:S(2)}, u32[]{:S(2)}) collective-permute-start(bf16[256,256]{1,0:T(8,128)(2,1)S(1)} %get-tuple-element.124), channel_id=1, source_target_pairs={{0,4},{1,5},{2,6},{3,7},{4,8},{5,9},{6,10},{7,11},{8,12},{9,13},{1... | collective-permute-start | bytes 393224 | tf_op jit(solution)/shard_map/ppermute | solution.py:37
  98.1 9.2 %collective-permute-start.26 = (bf16[256,256]{1,0:T(8,128)(2,1)S(1)}, bf16[256,256]{1,0:T(8,128)(2,1)S(1)}, u32[]{:S(2)}, u32[]{:S(2)}) collective-permute-start(bf16[256,256]{1,0:T(8,128)(2,1)S(1)} %get-tuple-element.125), channel_id=1, source_target_pairs={{0,8},{1,9},{2,10},{3,11},{4,12},{5,13},{6,14},{7,15},{8,0},{9,1},... | collective-permute-start | bytes 393224 | tf_op jit(solution)/shard_map/ppermute | solution.py:37
  100.4 7.1 %collective-permute-start.27 = (bf16[256,256]{1,0:T(8,128)(2,1)S(1)}, bf16[256,256]{1,0:T(8,128)(2,1)S(1)}, u32[]{:S(2)}, u32[]{:S(2)}) collective-permute-start(bf16[256,256]{1,0:T(8,128)(2,1)S(1)} %get-tuple-element.126), channel_id=1, source_target_pairs={{0,12},{1,13},{2,14},{3,15},{4,0},{5,1},{6,2},{7,3},{8,4},{9,5},{1... | collective-permute-start | bytes 393224 | tf_op jit(solution)/shard_map/ppermute | solution.py:37
  101.4 5.9 %collective-permute-start.28 = (bf16[160,256]{1,0:T(8,128)(2,1)S(1)}, bf16[160,256]{1,0:T(8,128)(2,1)S(1)}, u32[]{:S(2)}, u32[]{:S(2)}) collective-permute-start(bf16[160,256]{1,0:T(8,128)(2,1)S(1)} %get-tuple-element.127), channel_id=1, source_target_pairs={{0,2},{1,3},{2,0},{3,1},{4,6},{5,7},{6,4},{7,5},{8,10},{9,11},{10,... | collective-permute-start | bytes 245768 | tf_op jit(solution)/shard_map/ppermute | solution.py:41

commit v4 on v3

--- a/solution.py
+++ b/solution.py
@@ -277,14 +277,13 @@
             for n in range(count)
         ]
     )
-    owner = lax.broadcasted_iota(jnp.int32, (rows, width), 0) // occupied
-    place = lax.broadcasted_iota(jnp.int32, (rows, width), 1)
-    density = jnp.dot(
-        picked,
-        jnp.where(owner == place, 1.0, 0.0),
-        precision=lax.Precision.HIGHEST,
-        preferred_element_type=jnp.float32,
-    )
+    lane = lax.broadcasted_iota(jnp.int32, (count, rows), 1)
+    place = lax.broadcasted_iota(jnp.int32, (count, width), 1)
+    density = jnp.zeros((count, width), jnp.float32)
+    for n in range(count):
+        inside = jnp.logical_and(lane >= n * occupied, lane < (n + 1) * occupied)
+        total_n = jnp.sum(jnp.where(inside, picked, 0.0), axis=1, keepdims=True)
+        density = jnp.where(place == n, total_n, density)
     density = jnp.concatenate([density, jnp.zeros((16 - count, width), jnp.float32)])
     density_ref[...] = density
     put_parts(sent_ref, NZ * rows, density)

time: 109 us -> 109 us (level)
  no operation moved by 1% of the time
where the time goes in v4:
time: 109 us; the launch traced here: 108 us
  waiting for transfers between devices  47.4 us (43%)
  starting transfers between devices  38.8 us (36%)
  Pallas kernels  14.3 us (13%)
  local copies, waits for them, and re-layouts  5.79 us (5%)
  between operations  2.11 us (2%)
    ppermute x10, waiting for transfers between devices, along_z(): return lax.ppermute(x, 'aa', shift_perm(2 * step))  19.5 us
    ppermute x10, starting transfers between devices, along_z(): return lax.ppermute(x, 'aa', shift_perm(2 * step))  15.5 us
    ppermute x9, starting transfers between devices, along_y(): return lax.ppermute(x, 'ba', shift_perm(4 * step))  12.9 us
    ppermute x5, waiting for transfers between devices, swap_x_lo(): return lax.ppermute(x, 'aa', swap_perm(1))  9.74 us
    ppermute x9, waiting for transfers between devices, along_y(): return lax.ppermute(x, 'ba', shift_perm(4 * step))  8.21 us
    ppermute x3, waiting for transfers between devices, swap_x_hi(): return lax.ppermute(x, 'ba', swap_perm(2))  8.05 us
    pallas_call x1, Pallas kernels, middle(): pl.pallas_call(functools.partial(middle_kernel, late), out_shape=(jax.Sha...  6.63 us
    ppermute x3, starting transfers between devices, swap_x_hi(): return lax.ppermute(x, 'ba', swap_perm(2))  5.98 us
  transfers between devices with their start and end apart: 29, of which 17 were waited for; matrix products, arithmetic and copies ran while one was open for 1% of the time, Pallas kernels for 6%

profile of v4, /device:TPU:96, one launch (start us, length us, event | category | flops | bytes accessed | tf_op | source)
XLA Modules:
  0.0 108.4 jit_solution(10452985065453923132)
XLA Ops:
  0.6 1.6 %collective-permute-start.2 = (bf16[768,256]{1,0:T(8,128)(2,1)}, bf16[768,256]{1,0:T(8,128)(2,1)S(1)}, u32[]{:S(2)}, u32[]{:S(2)}) collective-permute-start(bf16[768,256]{1,0:T(8,128)(2,1)} %bitcast.12), channel_id=1, source_target_pairs={{0,16},{16,0},{32,48},{48,32},{64,80},{80,64},{96,112},{112,96},{1... | collective-permute-start | bytes 1179656 | tf_op jit(solution)/shard_map/ppermute | solution.py:33
  2.3 3.1 %collective-permute-start = (bf16[768,256]{1,0:T(8,128)(2,1)}, bf16[768,256]{1,0:T(8,128)(2,1)S(1)}, u32[]{:S(2)}, u32[]{:S(2)}) collective-permute-start(bf16[768,256]{1,0:T(8,128)(2,1)} %bitcast.14), channel_id=1, source_target_pairs={{0,32},{16,48},{32,64},{48,80},{64,96},{80,112},{96,128},{112,144}... | collective-permute-start | bytes 1179656 | tf_op jit(solution)/shard_map/ppermute | solution.py:29
  5.4 2.7 %collective-permute-start.3 = (bf16[48,2304]{1,0:T(8,128)(2,1)}, bf16[48,2304]{1,0:T(8,128)(2,1)S(1)}, u32[]{:S(2)}, u32[]{:S(2)}) collective-permute-start(bf16[48,2304]{1,0:T(8,128)(2,1)} %refs_0_.1), channel_id=1, source_target_pairs={{0,2},{1,3},{2,0},{3,1},{4,6},{5,7},{6,4},{7,5},{8,10},{9,11},{10,... | collective-permute-start | bytes 663560 | tf_op jit(solution)/shard_map/ppermute | solution.py:41
  9.5 0.9 reshape.18.refs_6_
  10.4 0.7 copy-done.4
  11.1 0.7 copy-done.5
  11.7 0.7 copy-done.6
  12.4 0.9 shard_map.113
  13.3 1.9 %copy-done = bf16[8,48,4096]{2,1,0:T(8,128)(2,1)S(1)} copy-done((bf16[8,48,4096]{2,1,0:T(8,128)(2,1)S(1)}, bf16[8,48,4096]{2,1,0:T(8,128)(2,1)}, u32[]{:S(2)}) %copy-start) | copy-done | bytes 3145752
  15.2 1.0 copy-done.1
  16.2 0.4 shard_map.114
  16.6 2.2 %collective-permute-done.3.refs_1_ = bf16[48,2304]{1,0:T(8,128)(2,1)S(1)} collective-permute-done((bf16[48,2304]{1,0:T(8,128)(2,1)}, bf16[48,2304]{1,0:T(8,128)(2,1)S(1)}, u32[]{:S(2)}, u32[]{:S(2)}) %collective-permute-start.3) | collective-permute-done | bytes 221216 | tf_op jit(solution)/shard_map/ppermute | solution.py:41
  18.7 3.2 %collective-permute-start.4 = (bf16[768,256]{1,0:T(8,128)(2,1)S(1)}, bf16[768,256]{1,0:T(8,128)(2,1)S(1)}, u32[]{:S(2)}, u32[]{:S(2)}) collective-permute-start(bf16[768,256]{1,0:T(8,128)(2,1)S(1)} %collective-permute-done.refs_1_), channel_id=1, source_target_pairs={{0,32},{16,48},{32,64},{48,80},{64,96},{80,112},{96,128},{112,144}... | collective-permute-start | bytes 1179656 | tf_op jit(solution)/shard_map/ppermute | solution.py:29
  22.2 1.7 %collective-permute-start.11 = (bf16[2,48,2304]{2,1,0:T(8,128)(2,1)S(1)}, bf16[2,48,2304]{2,1,0:T(8,128)(2,1)S(1)}, u32[]{:S(2)}, u32[]{:S(2)}) collective-permute-start(bf16[2,48,2304]{2,1,0:T(8,128)(2,1)S(1)} %shard_map.117.refs_0_), channel_id=1, source_target_pairs={{0,4},{1,5},{2,6},{3,7},{4,8},{5,9},{6,10},{7,11},{8,12},{9,13},{1... | collective-permute-start | bytes 1327112 | tf_op jit(solution)/shard_map/ppermute | solution.py:37
  23.9 1.7 %collective-permute-start.10 = (bf16[2,48,2304]{2,1,0:T(8,128)(2,1)S(1)}, bf16[2,48,2304]{2,1,0:T(8,128)(2,1)S(1)}, u32[]{:S(2)}, u32[]{:S(2)}) collective-permute-start(bf16[2,48,2304]{2,1,0:T(8,128)(2,1)S(1)} %shard_map.117.refs_0_), channel_id=1, source_target_pairs={{0,12},{1,13},{2,14},{3,15},{4,0},{5,1},{6,2},{7,3},{8,4},{9,5},{1... | collective-permute-start | bytes 1327112 | tf_op jit(solution)/shard_map/ppermute | solution.py:37
  25.5 0.8 shard_map.115
  26.4 3.1 %collective-permute-done.4.refs_1_ = bf16[768,256]{1,0:T(8,128)(2,1)S(1)} collective-permute-done((bf16[768,256]{1,0:T(8,128)(2,1)S(1)}, bf16[768,256]{1,0:T(8,128)(2,1)S(1)}, u32[]{:S(2)}, u32[]{:S(2)}) %collective-permute-start.4) | collective-permute-done | bytes 393248 | tf_op jit(solution)/shard_map/ppermute | solution.py:29
  29.7 3.5 %collective-permute-done.6.refs_2_ = bf16[768,256]{1,0:T(8,128)(2,1)S(1)} collective-permute-done((bf16[768,256]{1,0:T(8,128)(2,1)S(1)}, bf16[768,256]{1,0:T(8,128)(2,1)S(1)}, u32[]{:S(2)}, u32[]{:S(2)}) %collective-permute-start.6) | collective-permute-done | bytes 393248 | tf_op jit(solution)/shard_map/ppermute | solution.py:33
  33.4 1.8 %collective-permute-start.8 = (bf16[768,256]{1,0:T(8,128)(2,1)S(1)}, bf16[768,256]{1,0:T(8,128)(2,1)S(1)}, u32[]{:S(2)}, u32[]{:S(2)}) collective-permute-start(bf16[768,256]{1,0:T(8,128)(2,1)S(1)} %collective-permute-done.5.refs_0_), channel_id=1, source_target_pairs={{0,224},{16,240},{32,0},{48,16},{64,32},{80,48},{96,64},{112,80},{... | collective-permute-start | bytes 1179656 | tf_op jit(solution)/shard_map/ppermute | solution.py:29
  35.2 0.8 shard_map.116
  36.0 4.1 %collective-permute-done.9.refs_2_ = bf16[768,256]{1,0:T(8,128)(2,1)S(1)} collective-permute-done((bf16[768,256]{1,0:T(8,128)(2,1)S(1)}, bf16[768,256]{1,0:T(8,128)(2,1)S(1)}, u32[]{:S(2)}, u32[]{:S(2)}) %collective-permute-start.9) | collective-permute-done | bytes 393248 | tf_op jit(solution)/shard_map/ppermute | solution.py:33
  40.1 1.3 %collective-permute-done.7.refs_1_ = bf16[768,256]{1,0:T(8,128)(2,1)S(1)} collective-permute-done((bf16[768,256]{1,0:T(8,128)(2,1)S(1)}, bf16[768,256]{1,0:T(8,128)(2,1)S(1)}, u32[]{:S(2)}, u32[]{:S(2)}) %collective-permute-start.7) | collective-permute-done | bytes 393248 | tf_op jit(solution)/shard_map/ppermute | solution.py:29
  41.4 1.8 %collective-permute-done.8.refs_0_ = bf16[768,256]{1,0:T(8,128)(2,1)S(1)} collective-permute-done((bf16[768,256]{1,0:T(8,128)(2,1)S(1)}, bf16[768,256]{1,0:T(8,128)(2,1)S(1)}, u32[]{:S(2)}, u32[]{:S(2)}) %collective-permute-start.8) | collective-permute-done | bytes 393248 | tf_op jit(solution)/shard_map/ppermute | solution.py:29
  43.2 3.0 %collective-permute-start.15 = (bf16[2,48,2304]{2,1,0:T(8,128)(2,1)S(1)}, bf16[2,48,2304]{2,1,0:T(8,128)(2,1)S(1)}, u32[]{:S(2)}, u32[]{:S(2)}) collective-permute-start(bf16[2,48,2304]{2,1,0:T(8,128)(2,1)S(1)} %collective-permute-done.10.refs_1_), channel_id=1, source_target_pairs={{0,12},{1,13},{2,14},{3,15},{4,0},{5,1},{6,2},{7,3},{8,4},{9,5},{1... | collective-permute-start | bytes 1327112 | tf_op jit(solution)/shard_map/ppermute | solution.py:37
  46.2 1.7 %collective-permute-start.14 = (bf16[768,256]{1,0:T(8,128)(2,1)S(1)}, bf16[768,256]{1,0:T(8,128)(2,1)S(1)}, u32[]{:S(2)}, u32[]{:S(2)}) collective-permute-start(bf16[768,256]{1,0:T(8,128)(2,1)S(1)} %collective-permute-done.8.refs_0_), channel_id=1, source_target_pairs={{0,16},{16,0},{32,48},{48,32},{64,80},{80,64},{96,112},{112,96},{1... | collective-permute-start | bytes 1179656 | tf_op jit(solution)/shard_map/ppermute | solution.py:33
  47.9 3.2 %collective-permute-start.12 = (bf16[768,256]{1,0:T(8,128)(2,1)S(1)}, bf16[768,256]{1,0:T(8,128)(2,1)S(1)}, u32[]{:S(2)}, u32[]{:S(2)}) collective-permute-start(bf16[768,256]{1,0:T(8,128)(2,1)S(1)} %collective-permute-done.7.refs_1_), channel_id=1, source_target_pairs={{0,32},{16,48},{32,64},{48,80},{64,96},{80,112},{96,128},{112,144}... | collective-permute-start | bytes 1179656 | tf_op jit(solution)/shard_map/ppermute | solution.py:29
  51.1 0.8 shard_map.118
  52.0 3.2 %collective-permute-done.13.refs_1_ = bf16[768,256]{1,0:T(8,128)(2,1)S(1)} collective-permute-done((bf16[768,256]{1,0:T(8,128)(2,1)S(1)}, bf16[768,256]{1,0:T(8,128)(2,1)S(1)}, u32[]{:S(2)}, u32[]{:S(2)}) %collective-permute-start.13) | collective-permute-done | bytes 393248 | tf_op jit(solution)/shard_map/ppermute | solution.py:29
  55.2 1.2 %collective-permute-done.12.refs_0_ = bf16[768,256]{1,0:T(8,128)(2,1)S(1)} collective-permute-done((bf16[768,256]{1,0:T(8,128)(2,1)S(1)}, bf16[768,256]{1,0:T(8,128)(2,1)S(1)}, u32[]{:S(2)}, u32[]{:S(2)}) %collective-permute-start.12) | collective-permute-done | bytes 393248 | tf_op jit(solution)/shard_map/ppermute | solution.py:29
  56.6 3.8 %collective-permute-start.18 = (bf16[768,256]{1,0:T(8,128)(2,1)S(1)}, bf16[768,256]{1,0:T(8,128)(2,1)S(1)}, u32[]{:S(2)}, u32[]{:S(2)}) collective-permute-start(bf16[768,256]{1,0:T(8,128)(2,1)S(1)} %collective-permute-done.9.refs_2_), channel_id=1, source_target_pairs={{0,32},{16,48},{32,64},{48,80},{64,96},{80,112},{96,128},{112,144}... | collective-permute-start | bytes 1179656 | tf_op jit(solution)/shard_map/ppermute | solution.py:29
  60.8 0.8 shard_map.119
  61.9 7.5 %collective-permute-done.18.refs_2_ = bf16[768,256]{1,0:T(8,128)(2,1)S(1)} collective-permute-done((bf16[768,256]{1,0:T(8,128)(2,1)S(1)}, bf16[768,256]{1,0:T(8,128)(2,1)S(1)}, u32[]{:S(2)}, u32[]{:S(2)}) %collective-permute-start.18) | collective-permute-done | bytes 393248 | tf_op jit(solution)/shard_map/ppermute | solution.py:29
  69.4 2.2 %collective-permute-done.17.refs_1_ = bf16[768,256]{1,0:T(8,128)(2,1)S(1)} collective-permute-done((bf16[768,256]{1,0:T(8,128)(2,1)S(1)}, bf16[768,256]{1,0:T(8,128)(2,1)S(1)}, u32[]{:S(2)}, u32[]{:S(2)}) %collective-permute-start.17) | collective-permute-done | bytes 393248 | tf_op jit(solution)/shard_map/ppermute | solution.py:33
  71.6 1.3 %collective-permute-done.16.refs_0_ = bf16[768,256]{1,0:T(8,128)(2,1)S(1)} collective-permute-done((bf16[768,256]{1,0:T(8,128)(2,1)S(1)}, bf16[768,256]{1,0:T(8,128)(2,1)S(1)}, u32[]{:S(2)}, u32[]{:S(2)}) %collective-permute-start.16) | collective-permute-done | bytes 393248 | tf_op jit(solution)/shard_map/ppermute | solution.py:29
  72.9 6.6 %shard_map.122 = (bf16[16,768,256]{2,1,0:T(8,128)(2,1)S(1)}, bf16[384,768]{1,0:T(8,128)(2,1)S(1)}, bf16[3104,256]{1,0:T(8,128)(2,1)S(1)}, f32[16,256]{1,0:T(8,128)S(1)}) custom-call(bf16[384,4096]{1,0:T(8,128)(2,1)S(1)} %bitcast.11, bf16[768,256]{1,0:T(8,128)(2,1)S(1)} %collective-permute-done.16.refs_0_, ...), custom_call_target="tpu_custom_call", output_to_operand_aliasing={{0}: (10, {})} | custom-call | tf_op jit(solution)/shard_map/pallas_call | solution.py:295
  79.8 1.4 %shard_map.123.kept_ref = f32[3072,256]{1,0:T(8,128)S(1)} custom-call(bf16[384,768]{1,0:T(8,128)(2,1)S(1)} %get-tuple-element.108.left_ref, bf16[16,768,256]{2,1,0:T(8,128)(2,1)S(1)} %get-tuple-element.109.stack_ref), custom_call_target="tpu_custom_call" | custom-call | flops 1207959552 | bytes 3145728 | tf_op jit(solution)/shard_map/pallas_call | solution.py:321
  81.3 2.0 %collective-permute-done.20.recv_ref = bf16[3104,256]{1,0:T(8,128)(2,1)S(1)} collective-permute-done((bf16[3104,256]{1,0:T(8,128)(2,1)S(1)}, bf16[3104,256]{1,0:T(8,128)(2,1)S(1)}, u32[]{:S(2)}, u32[]{:S(2)}) %collective-permute-start.20) | collective-permute-done | bytes 1589280 | tf_op jit(solution)/shard_map/ppermute | solution.py:45
  83.5 1.7 %collective-permute-start.24 = (bf16[928,256]{1,0:T(8,128)(2,1)S(1)}, bf16[928,256]{1,0:T(8,128)(2,1)S(1)}, u32[]{:S(2)}, u32[]{:S(2)}) collective-permute-start(bf16[928,256]{1,0:T(8,128)(2,1)S(1)} %get-tuple-element.116), channel_id=1, source_target_pairs={{0,2},{1,3},{2,0},{3,1},{4,6},{5,7},{6,4},{7,5},{8,10},{9,11},{10,... | collective-permute-start | bytes 1425416 | tf_op jit(solution)/shard_map/ppermute | solution.py:41
  85.2 2.2 %collective-permute-start.22 = (bf16[320,256]{1,0:T(8,128)(2,1)S(1)}, bf16[320,256]{1,0:T(8,128)(2,1)S(1)}, u32[]{:S(2)}, u32[]{:S(2)}) collective-permute-start(bf16[320,256]{1,0:T(8,128)(2,1)S(1)} %get-tuple-element.114), channel_id=1, source_target_pairs={{0,8},{1,9},{2,10},{3,11},{4,12},{5,13},{6,14},{7,15},{8,0},{9,1},... | collective-permute-start | bytes 491528 | tf_op jit(solution)/shard_map/ppermute | solution.py:37
  87.4 1.0 collective-permute-start.23
  88.4 7.4 %collective-permute-done.21.a_ref = bf16[320,256]{1,0:T(8,128)(2,1)S(1)} collective-permute-done((bf16[320,256]{1,0:T(8,128)(2,1)S(1)}, bf16[320,256]{1,0:T(8,128)(2,1)S(1)}, u32[]{:S(2)}, u32[]{:S(2)}) %collective-permute-start.21) | collective-permute-done | bytes 163872 | tf_op jit(solution)/shard_map/ppermute | solution.py:37
  95.9 0.6 collective-permute-done.23.c_ref
  96.5 1.5 %collective-permute-done.24.recv_ref = bf16[928,256]{1,0:T(8,128)(2,1)S(1)} collective-permute-done((bf16[928,256]{1,0:T(8,128)(2,1)S(1)}, bf16[928,256]{1,0:T(8,128)(2,1)S(1)}, u32[]{:S(2)}, u32[]{:S(2)}) %collective-permute-start.24) | collective-permute-done | bytes 475168 | tf_op jit(solution)/shard_map/ppermute | solution.py:41
  98.3 2.3 %collective-permute-start.26 = (bf16[256,256]{1,0:T(8,128)(2,1)S(1)}, bf16[256,256]{1,0:T(8,128)(2,1)S(1)}, u32[]{:S(2)}, u32[]{:S(2)}) collective-permute-start(bf16[256,256]{1,0:T(8,128)(2,1)S(1)} %get-tuple-element.125), channel_id=1, source_target_pairs={{0,8},{1,9},{2,10},{3,11},{4,12},{5,13},{6,14},{7,15},{8,0},{9,1},... | collective-permute-start | bytes 393224 | tf_op jit(solution)/shard_map/ppermute | solution.py:37
  100.5 1.0 collective-permute-start.27
  101.5 1.6 %collective-permute-start.28 = (bf16[160,256]{1,0:T(8,128)(2,1)S(1)}, bf16[160,256]{1,0:T(8,128)(2,1)S(1)}, u32[]{:S(2)}, u32[]{:S(2)}) collective-permute-start(bf16[160,256]{1,0:T(8,128)(2,1)S(1)} %get-tuple-element.127), channel_id=1, source_target_pairs={{0,2},{1,3},{2,0},{3,1},{4,6},{5,7},{6,4},{7,5},{8,10},{9,11},{10,... | collective-permute-start | bytes 245768 | tf_op jit(solution)/shard_map/ppermute | solution.py:41
  103.1 4.4 %collective-permute-done.28.recv_ref = bf16[160,256]{1,0:T(8,128)(2,1)S(1)} collective-permute-done((bf16[160,256]{1,0:T(8,128)(2,1)S(1)}, bf16[160,256]{1,0:T(8,128)(2,1)S(1)}, u32[]{:S(2)}, u32[]{:S(2)}) %collective-permute-start.28) | collective-permute-done | bytes 81952 | tf_op jit(solution)/shard_map/ppermute | solution.py:41
  107.6 0.8 shard_map.126
  (39 shorter events, 2.6 us)
Async XLA Ops:
  0.6 18.1 %collective-permute-start.2 = (bf16[768,256]{1,0:T(8,128)(2,1)}, bf16[768,256]{1,0:T(8,128)(2,1)S(1)}, u32[]{:S(2)}, u32[]{:S(2)}) collective-permute-start(bf16[768,256]{1,0:T(8,128)(2,1)} %bitcast.12), channel_id=1, source_target_pairs={{0,16},{16,0},{32,48},{48,32},{64,80},{80,64},{96,112},{112,96},{1... | collective-permute-start | bytes 1179656 | tf_op jit(solution)/shard_map/ppermute | solution.py:33
  2.2 16.5 %collective-permute-start.1 = (bf16[768,256]{1,0:T(8,128)(2,1)}, bf16[768,256]{1,0:T(8,128)(2,1)S(1)}, u32[]{:S(2)}, u32[]{:S(2)}) collective-permute-start(bf16[768,256]{1,0:T(8,128)(2,1)} %bitcast.13), channel_id=1, source_target_pairs={{0,224},{16,240},{32,0},{48,16},{64,32},{80,48},{96,64},{112,80},{... | collective-permute-start | bytes 1179656 | tf_op jit(solution)/shard_map/ppermute | solution.py:29
  2.3 16.4 %collective-permute-start = (bf16[768,256]{1,0:T(8,128)(2,1)}, bf16[768,256]{1,0:T(8,128)(2,1)S(1)}, u32[]{:S(2)}, u32[]{:S(2)}) collective-permute-start(bf16[768,256]{1,0:T(8,128)(2,1)} %bitcast.14), channel_id=1, source_target_pairs={{0,32},{16,48},{32,64},{48,80},{64,96},{80,112},{96,128},{112,144}... | collective-permute-start | bytes 1179656 | tf_op jit(solution)/shard_map/ppermute | solution.py:29
  5.4 13.3 %collective-permute-start.3 = (bf16[48,2304]{1,0:T(8,128)(2,1)}, bf16[48,2304]{1,0:T(8,128)(2,1)S(1)}, u32[]{:S(2)}, u32[]{:S(2)}) collective-permute-start(bf16[48,2304]{1,0:T(8,128)(2,1)} %refs_0_.1), channel_id=1, source_target_pairs={{0,2},{1,3},{2,0},{3,1},{4,6},{5,7},{6,4},{7,5},{8,10},{9,11},{10,... | collective-permute-start | bytes 663560 | tf_op jit(solution)/shard_map/ppermute | solution.py:41
  10.4 0.7 copy-start.4
  11.1 0.7 copy-start.5
  11.7 0.7 copy-start.6
  13.3 1.9 %copy-start = (bf16[8,48,4096]{2,1,0:T(8,128)(2,1)S(1)}, bf16[8,48,4096]{2,1,0:T(8,128)(2,1)}, u32[]{:S(2)}) copy-start(bf16[8,48,4096]{2,1,0:T(8,128)(2,1)} %param.10) | copy-start | bytes 9437188
  15.2 1.0 copy-start.1
  16.2 6.0 %copy-start.2 = (bf16[48,2304]{1,0:T(8,128)(2,1)S(1)}, bf16[48,2304]{1,0:T(8,128)(2,1)}, u32[]{:S(2)}) copy-start(bf16[48,2304]{1,0:T(8,128)(2,1)} %refs_0_.1) | copy-start | bytes 663556
  18.7 10.7 %collective-permute-start.4 = (bf16[768,256]{1,0:T(8,128)(2,1)S(1)}, bf16[768,256]{1,0:T(8,128)(2,1)S(1)}, u32[]{:S(2)}, u32[]{:S(2)}) collective-permute-start(bf16[768,256]{1,0:T(8,128)(2,1)S(1)} %collective-permute-done.refs_1_), channel_id=1, source_target_pairs={{0,32},{16,48},{32,64},{48,80},{64,96},{80,112},{96,128},{112,144}... | collective-permute-start | bytes 1179656 | tf_op jit(solution)/shard_map/ppermute | solution.py:29
  21.9 11.2 %collective-permute-start.6 = (bf16[768,256]{1,0:T(8,128)(2,1)S(1)}, bf16[768,256]{1,0:T(8,128)(2,1)S(1)}, u32[]{:S(2)}, u32[]{:S(2)}) collective-permute-start(bf16[768,256]{1,0:T(8,128)(2,1)S(1)} %collective-permute-done.1.refs_0_), channel_id=1, source_target_pairs={{0,16},{16,0},{32,48},{48,32},{64,80},{80,64},{96,112},{112,96},{1... | collective-permute-start | bytes 1179656 | tf_op jit(solution)/shard_map/ppermute | solution.py:33
  22.2 11.0 %collective-permute-start.5 = (bf16[768,256]{1,0:T(8,128)(2,1)S(1)}, bf16[768,256]{1,0:T(8,128)(2,1)S(1)}, u32[]{:S(2)}, u32[]{:S(2)}) collective-permute-start(bf16[768,256]{1,0:T(8,128)(2,1)S(1)} %collective-permute-done.1.refs_0_), channel_id=1, source_target_pairs={{0,224},{16,240},{32,0},{48,16},{64,32},{80,48},{96,64},{112,80},{... | collective-permute-start | bytes 1179656 | tf_op jit(solution)/shard_map/ppermute | solution.py:29
  22.2 17.9 %collective-permute-start.11 = (bf16[2,48,2304]{2,1,0:T(8,128)(2,1)S(1)}, bf16[2,48,2304]{2,1,0:T(8,128)(2,1)S(1)}, u32[]{:S(2)}, u32[]{:S(2)}) collective-permute-start(bf16[2,48,2304]{2,1,0:T(8,128)(2,1)S(1)} %shard_map.117.refs_0_), channel_id=1, source_target_pairs={{0,4},{1,5},{2,6},{3,7},{4,8},{5,9},{6,10},{7,11},{8,12},{9,13},{1... | collective-permute-start | bytes 1327112 | tf_op jit(solution)/shard_map/ppermute | solution.py:37
  23.9 16.2 %collective-permute-start.10 = (bf16[2,48,2304]{2,1,0:T(8,128)(2,1)S(1)}, bf16[2,48,2304]{2,1,0:T(8,128)(2,1)S(1)}, u32[]{:S(2)}, u32[]{:S(2)}) collective-permute-start(bf16[2,48,2304]{2,1,0:T(8,128)(2,1)S(1)} %shard_map.117.refs_0_), channel_id=1, source_target_pairs={{0,12},{1,13},{2,14},{3,15},{4,0},{5,1},{6,2},{7,3},{8,4},{9,5},{1... | collective-permute-start | bytes 1327112 | tf_op jit(solution)/shard_map/ppermute | solution.py:37
  29.4 10.6 %collective-permute-start.9 = (bf16[768,256]{1,0:T(8,128)(2,1)S(1)}, bf16[768,256]{1,0:T(8,128)(2,1)S(1)}, u32[]{:S(2)}, u32[]{:S(2)}) collective-permute-start(bf16[768,256]{1,0:T(8,128)(2,1)S(1)} %collective-permute-done.refs_1_), channel_id=1, source_target_pairs={{0,16},{16,0},{32,48},{48,32},{64,80},{80,64},{96,112},{112,96},{1... | collective-permute-start | bytes 1179656 | tf_op jit(solution)/shard_map/ppermute | solution.py:33
  33.1 8.3 %collective-permute-start.7 = (bf16[768,256]{1,0:T(8,128)(2,1)S(1)}, bf16[768,256]{1,0:T(8,128)(2,1)S(1)}, u32[]{:S(2)}, u32[]{:S(2)}) collective-permute-start(bf16[768,256]{1,0:T(8,128)(2,1)S(1)} %collective-permute-done.4.refs_1_), channel_id=1, source_target_pairs={{0,32},{16,48},{32,64},{48,80},{64,96},{80,112},{96,128},{112,144}... | collective-permute-start | bytes 1179656 | tf_op jit(solution)/shard_map/ppermute | solution.py:29
  33.4 9.9 %collective-permute-start.8 = (bf16[768,256]{1,0:T(8,128)(2,1)S(1)}, bf16[768,256]{1,0:T(8,128)(2,1)S(1)}, u32[]{:S(2)}, u32[]{:S(2)}) collective-permute-start(bf16[768,256]{1,0:T(8,128)(2,1)S(1)} %collective-permute-done.5.refs_0_), channel_id=1, source_target_pairs={{0,224},{16,240},{32,0},{48,16},{64,32},{80,48},{96,64},{112,80},{... | collective-permute-start | bytes 1179656 | tf_op jit(solution)/shard_map/ppermute | solution.py:29
  43.2 13.2 %collective-permute-start.15 = (bf16[2,48,2304]{2,1,0:T(8,128)(2,1)S(1)}, bf16[2,48,2304]{2,1,0:T(8,128)(2,1)S(1)}, u32[]{:S(2)}, u32[]{:S(2)}) collective-permute-start(bf16[2,48,2304]{2,1,0:T(8,128)(2,1)S(1)} %collective-permute-done.10.refs_1_), channel_id=1, source_target_pairs={{0,12},{1,13},{2,14},{3,15},{4,0},{5,1},{6,2},{7,3},{8,4},{9,5},{1... | collective-permute-start | bytes 1327112 | tf_op jit(solution)/shard_map/ppermute | solution.py:37
  46.2 9.0 %collective-permute-start.13 = (bf16[768,256]{1,0:T(8,128)(2,1)S(1)}, bf16[768,256]{1,0:T(8,128)(2,1)S(1)}, u32[]{:S(2)}, u32[]{:S(2)}) collective-permute-start(bf16[768,256]{1,0:T(8,128)(2,1)S(1)} %collective-permute-done.6.refs_2_), channel_id=1, source_target_pairs={{0,224},{16,240},{32,0},{48,16},{64,32},{80,48},{96,64},{112,80},{... | collective-permute-start | bytes 1179656 | tf_op jit(solution)/shard_map/ppermute | solution.py:29
  46.2 9.0 %collective-permute-start.14 = (bf16[768,256]{1,0:T(8,128)(2,1)S(1)}, bf16[768,256]{1,0:T(8,128)(2,1)S(1)}, u32[]{:S(2)}, u32[]{:S(2)}) collective-permute-start(bf16[768,256]{1,0:T(8,128)(2,1)S(1)} %collective-permute-done.8.refs_0_), channel_id=1, source_target_pairs={{0,16},{16,0},{32,48},{48,32},{64,80},{80,64},{96,112},{112,96},{1... | collective-permute-start | bytes 1179656 | tf_op jit(solution)/shard_map/ppermute | solution.py:33
  47.9 8.5 %collective-permute-start.12 = (bf16[768,256]{1,0:T(8,128)(2,1)S(1)}, bf16[768,256]{1,0:T(8,128)(2,1)S(1)}, u32[]{:S(2)}, u32[]{:S(2)}) collective-permute-start(bf16[768,256]{1,0:T(8,128)(2,1)S(1)} %collective-permute-done.7.refs_1_), channel_id=1, source_target_pairs={{0,32},{16,48},{32,64},{48,80},{64,96},{80,112},{96,128},{112,144}... | collective-permute-start | bytes 1179656 | tf_op jit(solution)/shard_map/ppermute | solution.py:29
  56.5 5.1 %collective-permute-start.19 = (bf16[4,2,48,2304]{3,2,1,0:T(8,128)(2,1)S(1)}, bf16[4,2,48,2304]{3,2,1,0:T(8,128)(2,1)S(1)}, u32[]{:S(2)}, u32[]{:S(2)}) collective-permute-start(bf16[4,2,48,2304]{3,2,1,0:T(8,128)(2,1)S(1)} %shard_map.120.own_ref), channel_id=1, source_target_pairs={{0,1},{1,0},{2,3},{3,2},{4,5},{5,4},{6,7},{7,6},{8,9},{9,8},{10,11... | collective-permute-start | bytes 5308424 | tf_op jit(solution)/shard_map/ppermute | solution.py:45
  56.6 12.7 %collective-permute-start.18 = (bf16[768,256]{1,0:T(8,128)(2,1)S(1)}, bf16[768,256]{1,0:T(8,128)(2,1)S(1)}, u32[]{:S(2)}, u32[]{:S(2)}) collective-permute-start(bf16[768,256]{1,0:T(8,128)(2,1)S(1)} %collective-permute-done.9.refs_2_), channel_id=1, source_target_pairs={{0,32},{16,48},{32,64},{48,80},{64,96},{80,112},{96,128},{112,144}... | collective-permute-start | bytes 1179656 | tf_op jit(solution)/shard_map/ppermute | solution.py:29
  60.4 11.2 %collective-permute-start.17 = (bf16[768,256]{1,0:T(8,128)(2,1)S(1)}, bf16[768,256]{1,0:T(8,128)(2,1)S(1)}, u32[]{:S(2)}, u32[]{:S(2)}) collective-permute-start(bf16[768,256]{1,0:T(8,128)(2,1)S(1)} %collective-permute-done.7.refs_1_), channel_id=1, source_target_pairs={{0,16},{16,0},{32,48},{48,32},{64,80},{80,64},{96,112},{112,96},{1... | collective-permute-start | bytes 1179656 | tf_op jit(solution)/shard_map/ppermute | solution.py:33
  60.8 12.1 %collective-permute-start.16 = (bf16[768,256]{1,0:T(8,128)(2,1)S(1)}, bf16[768,256]{1,0:T(8,128)(2,1)S(1)}, u32[]{:S(2)}, u32[]{:S(2)}) collective-permute-start(bf16[768,256]{1,0:T(8,128)(2,1)S(1)} %collective-permute-done.14.refs_2_), channel_id=1, source_target_pairs={{0,224},{16,240},{32,0},{48,16},{64,32},{80,48},{96,64},{112,80},{... | collective-permute-start | bytes 1179656 | tf_op jit(solution)/shard_map/ppermute | solution.py:29
  61.6 11.3 %copy-start.3 = (bf16[48,2304]{1,0:T(8,128)(2,1)S(1)}, bf16[48,2304]{1,0:T(8,128)(2,1)}, u32[]{:S(2)}) copy-start(bf16[48,2304]{1,0:T(8,128)(2,1)} %refs_7_.1) | copy-start | bytes 663556
  79.5 3.7 %collective-permute-start.20 = (bf16[3104,256]{1,0:T(8,128)(2,1)S(1)}, bf16[3104,256]{1,0:T(8,128)(2,1)S(1)}, u32[]{:S(2)}, u32[]{:S(2)}) collective-permute-start(bf16[3104,256]{1,0:T(8,128)(2,1)S(1)} %get-tuple-element.111), channel_id=1, source_target_pairs={{0,1},{1,0},{2,3},{3,2},{4,5},{5,4},{6,7},{7,6},{8,9},{9,8},{10,11... | collective-permute-start | bytes 4767752 | tf_op jit(solution)/shard_map/ppermute | solution.py:45
  83.5 14.5 %collective-permute-start.24 = (bf16[928,256]{1,0:T(8,128)(2,1)S(1)}, bf16[928,256]{1,0:T(8,128)(2,1)S(1)}, u32[]{:S(2)}, u32[]{:S(2)}) collective-permute-start(bf16[928,256]{1,0:T(8,128)(2,1)S(1)} %get-tuple-element.116), channel_id=1, source_target_pairs={{0,2},{1,3},{2,0},{3,1},{4,6},{5,7},{6,4},{7,5},{8,10},{9,11},{10,... | collective-permute-start | bytes 1425416 | tf_op jit(solution)/shard_map/ppermute | solution.py:41
  85.2 10.7 %collective-permute-start.21 = (bf16[320,256]{1,0:T(8,128)(2,1)S(1)}, bf16[320,256]{1,0:T(8,128)(2,1)S(1)}, u32[]{:S(2)}, u32[]{:S(2)}) collective-permute-start(bf16[320,256]{1,0:T(8,128)(2,1)S(1)} %get-tuple-element.113), channel_id=1, source_target_pairs={{0,4},{1,5},{2,6},{3,7},{4,8},{5,9},{6,10},{7,11},{8,12},{9,13},{1... | collective-permute-start | bytes 491528 | tf_op jit(solution)/shard_map/ppermute | solution.py:37
  85.2 10.7 %collective-permute-start.22 = (bf16[320,256]{1,0:T(8,128)(2,1)S(1)}, bf16[320,256]{1,0:T(8,128)(2,1)S(1)}, u32[]{:S(2)}, u32[]{:S(2)}) collective-permute-start(bf16[320,256]{1,0:T(8,128)(2,1)S(1)} %get-tuple-element.114), channel_id=1, source_target_pairs={{0,8},{1,9},{2,10},{3,11},{4,12},{5,13},{6,14},{7,15},{8,0},{9,1},... | collective-permute-start | bytes 491528 | tf_op jit(solution)/shard_map/ppermute | solution.py:37
  87.4 9.1 %collective-permute-start.23 = (bf16[320,256]{1,0:T(8,128)(2,1)S(1)}, bf16[320,256]{1,0:T(8,128)(2,1)S(1)}, u32[]{:S(2)}, u32[]{:S(2)}) collective-permute-start(bf16[320,256]{1,0:T(8,128)(2,1)S(1)} %get-tuple-element.115), channel_id=1, source_target_pairs={{0,12},{1,13},{2,14},{3,15},{4,0},{5,1},{6,2},{7,3},{8,4},{9,5},{1... | collective-permute-start | bytes 491528 | tf_op jit(solution)/shard_map/ppermute | solution.py:37
  98.2 9.3 %collective-permute-start.25 = (bf16[256,256]{1,0:T(8,128)(2,1)S(1)}, bf16[256,256]{1,0:T(8,128)(2,1)S(1)}, u32[]{:S(2)}, u32[]{:S(2)}) collective-permute-start(bf16[256,256]{1,0:T(8,128)(2,1)S(1)} %get-tuple-element.124), channel_id=1, source_target_pairs={{0,4},{1,5},{2,6},{3,7},{4,8},{5,9},{6,10},{7,11},{8,12},{9,13},{1... | collective-permute-start | bytes 393224 | tf_op jit(solution)/shard_map/ppermute | solution.py:37
  98.3 9.2 %collective-permute-start.26 = (bf16[256,256]{1,0:T(8,128)(2,1)S(1)}, bf16[256,256]{1,0:T(8,128)(2,1)S(1)}, u32[]{:S(2)}, u32[]{:S(2)}) collective-permute-start(bf16[256,256]{1,0:T(8,128)(2,1)S(1)} %get-tuple-element.125), channel_id=1, source_target_pairs={{0,8},{1,9},{2,10},{3,11},{4,12},{5,13},{6,14},{7,15},{8,0},{9,1},... | collective-permute-start | bytes 393224 | tf_op jit(solution)/shard_map/ppermute | solution.py:37
  100.5 7.1 %collective-permute-start.27 = (bf16[256,256]{1,0:T(8,128)(2,1)S(1)}, bf16[256,256]{1,0:T(8,128)(2,1)S(1)}, u32[]{:S(2)}, u32[]{:S(2)}) collective-permute-start(bf16[256,256]{1,0:T(8,128)(2,1)S(1)} %get-tuple-element.126), channel_id=1, source_target_pairs={{0,12},{1,13},{2,14},{3,15},{4,0},{5,1},{6,2},{7,3},{8,4},{9,5},{1... | collective-permute-start | bytes 393224 | tf_op jit(solution)/shard_map/ppermute | solution.py:37
  101.5 5.9 %collective-permute-start.28 = (bf16[160,256]{1,0:T(8,128)(2,1)S(1)}, bf16[160,256]{1,0:T(8,128)(2,1)S(1)}, u32[]{:S(2)}, u32[]{:S(2)}) collective-permute-start(bf16[160,256]{1,0:T(8,128)(2,1)S(1)} %get-tuple-element.127), channel_id=1, source_target_pairs={{0,2},{1,3},{2,0},{3,1},{4,6},{5,7},{6,4},{7,5},{8,10},{9,11},{10,... | collective-permute-start | bytes 245768 | tf_op jit(solution)/shard_map/ppermute | solution.py:41

commit v5 on v4

--- a/solution.py
+++ b/solution.py
@@ -10,6 +10,7 @@
 NZ = 8
 NY = 4
 RANKS = 16
+LANES = 128
 VMEM_LIMIT = 24 * 1024 * 1024
 SMALL_LIMIT = 16 * 1024 * 1024
 TILE = 768
@@ -118,7 +119,11 @@
     )(*arrays)
 
 
-def whole_kernel(own_ref, other_ref, out_ref):
+def whole_kernel(own_ref, other_ref, coulomb_ref, out_ref):
+    occupied, columns = coulomb_ref.shape
+    first = out_ref.shape[0] - LANES
+    out_ref[first : first + occupied] = coulomb_ref[...]
+    out_ref[first + occupied :] = jnp.zeros((LANES - occupied, columns), out_ref.dtype)
     _, _, y, x_hi, core = where_am_i()
     part = own_ref.shape[2]
     for other_core, ref in enumerate((own_ref, other_ref)):
@@ -129,15 +134,15 @@
                 out_ref[pl.ds(pl.multiple_of(owner * part, part), part)] = ref[n, other_hi]
 
 
-def whole_amplitudes(own, other):
+def whole_amplitudes(own, other, coulomb):
     part, columns = own.shape[2:]
     return pl.pallas_call(
         whole_kernel,
-        out_shape=jax.ShapeDtypeStruct((RANKS * part, columns), own.dtype),
-        in_specs=[VMEM] * 2,
+        out_shape=jax.ShapeDtypeStruct((RANKS * part + LANES, columns), own.dtype),
+        in_specs=[VMEM] * 3,
         out_specs=VMEM,
         compiler_params=pltpu.CompilerParams(vmem_limit_bytes=SMALL_LIMIT),
-    )(own, other)
+    )(own, other, coulomb)
 
 
 def add_kernel(places, first, a_ref, *refs):
@@ -183,7 +188,7 @@
     )(a, *pieces, *before)
 
 
-def gather_pieces(piece, amplitudes, pair_rows, a, tables):
+def gather_pieces(piece, amplitudes, pair_rows, coulomb, a, tables):
     own, other = {0: piece}, {}
     get = lambda n: other[n - NZ] if n >= NZ else own[n]
     add = lambda places, **rest: add_products(places, [get(n) for n in places], a, **rest)
@@ -217,7 +222,7 @@
     )
     sums, stack = add([4, NZ + 2, NZ + 3], before=sums)
     late = [NZ + 4, NZ + 5, NZ + 6]
-    return late, [get(n) for n in late], sums, stack, terms, pair_rows, whole_amplitudes(amp_own, amp_other)
+    return late, [get(n) for n in late], sums, stack, terms, pair_rows, whole_amplitudes(amp_own, amp_other, coulomb)
 
 
 def gamma_dots(goes, left, stack_ref, out_ref):
@@ -233,10 +238,10 @@
 
 def middle_kernel(late, a_ref, *refs):
     count = len(late)
-    pieces, (before_ref, row_ref, col_ref, pair_ref, coulomb_ref), rest = (
-        refs[:count], refs[count : count + 5], refs[count + 5 :]
-    )
-    amp_ref, _, stack_ref, left_ref, sent_ref, density_ref, total, gram = rest
+    pieces, (before_ref, row_ref, col_ref, pair_ref), rest = (
+        refs[:count], refs[count : count + 4], refs[count + 4 :]
+    )
+    amp_ref, _, stack_ref, left_ref, sent_ref, density_ref, x_ref, total, gram = rest
     products = before_ref[...]
     for place, piece in zip(late, pieces):
         stack_ref[place] = piece[...]
@@ -246,15 +251,16 @@
             NT,
             preferred_element_type=jnp.float32,
         )
-    x = products.astype(jnp.bfloat16)
+    virtuals = products.shape[1]
+    x_ref[:, :virtuals] = products.astype(jnp.bfloat16)
+    x_ref[:, virtuals:] = jnp.zeros((x_ref.shape[0], LANES), jnp.bfloat16)
+    x_ref[:, virtuals : virtuals + pair_ref.shape[1]] = -pair_ref[...]
 
     tiles = [slice(n, n + TILE) for n in range(0, amp_ref.shape[1], TILE)]
     for n, tile in enumerate(tiles):
-        triples = jnp.dot(
-            x, amp_ref[:, tile], preferred_element_type=jnp.float32
-        ) - jnp.dot(pair_ref[...], coulomb_ref[:, tile], preferred_element_type=jnp.float32)
+        triples = jnp.dot(x_ref[...], amp_ref[:, tile], preferred_element_type=jnp.float32)
         ratio = (triples / (row_ref[...] + col_ref[:, tile])).astype(jnp.bfloat16)
-        terms = lax.dot_general(ratio, amp_ref[:, tile], NT, preferred_element_type=jnp.float32)
+        terms = lax.dot_general(ratio, amp_ref[:virtuals, tile], NT, preferred_element_type=jnp.float32)
         pairs = lax.dot_general(ratio, ratio, NT, preferred_element_type=jnp.float32)
         if n == 0:
             total[...] = terms
@@ -289,7 +295,7 @@
     put_parts(sent_ref, NZ * rows, density)
 
 
-def middle(late, pieces, a, sums, stack, terms, pair_rows, coulomb, amp):
+def middle(late, pieces, a, sums, stack, terms, pair_rows, amp):
     rows, virtuals = sums.shape
     width = pieces[0].shape[1]
     return pl.pallas_call(
@@ -300,15 +306,16 @@
             jax.ShapeDtypeStruct((NZ * rows + 32, width), jnp.bfloat16),
             jax.ShapeDtypeStruct((16, width), jnp.float32),
         ),
-        in_specs=[VMEM] * (8 + len(late)),
+        in_specs=[VMEM] * (7 + len(late)),
         out_specs=(VMEM,) * 4,
         scratch_shapes=[
+            pltpu.VMEM((rows, virtuals + LANES), jnp.bfloat16),
             pltpu.VMEM((rows, virtuals), jnp.float32),
             pltpu.VMEM((rows, rows), jnp.float32),
         ],
-        input_output_aliases={7 + len(late): 0},
+        input_output_aliases={6 + len(late): 0},
         compiler_params=pltpu.CompilerParams(vmem_limit_bytes=VMEM_LIMIT),
-    )(a, *pieces, sums, *terms, pair_rows, coulomb, amp, stack)
+    )(a, *pieces, sums, *terms, pair_rows, amp, stack)
 
 
 def kept_kernel(left_ref, stack_ref, out_ref):
@@ -467,10 +474,10 @@
     vo_rows = b_vo.reshape(rows, aux_all)
     tables = (a_index, b_index, c_index, eps_vir, eps_occ.reshape(1, occupied))
     late, pieces, sums, stack, terms, pair_rows, amp = gather_pieces(
-        b_vv[0], amplitudes, pair_amps.reshape(rows, occupied), vo_rows, tables
+        b_vv[0], amplitudes, pair_amps.reshape(rows, occupied), coulomb_occ, vo_rows, tables
     )
     stack, left, sent, density = middle(
-        late, pieces, vo_rows, sums, stack, terms, pair_rows, coulomb_occ, amp
+        late, pieces, vo_rows, sums, stack, terms, pair_rows, amp
     )
     received = swap_core(sent)
     kept = gamma_kept(left, stack)

time: 109 us -> 109 us (level)
  no operation moved by 1% of the time
where the time goes in v5:
time: 109 us; the launch traced here: 108 us
  waiting for transfers between devices  47.4 us (43%)
  starting transfers between devices  38.8 us (36%)
  Pallas kernels  14.1 us (13%)
  local copies, waits for them, and re-layouts  5.79 us (5%)
  between operations  2.11 us (2%)
    ppermute x10, waiting for transfers between devices, along_z(): return lax.ppermute(x, 'aa', shift_perm(2 * step))  19.4 us
    ppermute x10, starting transfers between devices, along_z(): return lax.ppermute(x, 'aa', shift_perm(2 * step))  15.5 us
    ppermute x9, starting transfers between devices, along_y(): return lax.ppermute(x, 'ba', shift_perm(4 * step))  12.9 us
    ppermute x5, waiting for transfers between devices, swap_x_lo(): return lax.ppermute(x, 'aa', swap_perm(1))  9.74 us
    ppermute x9, waiting for transfers between devices, along_y(): return lax.ppermute(x, 'ba', shift_perm(4 * step))  8.18 us
    ppermute x3, waiting for transfers between devices, swap_x_hi(): return lax.ppermute(x, 'ba', swap_perm(2))  8.05 us
    pallas_call x1, Pallas kernels, middle(): pl.pallas_call(functools.partial(middle_kernel, late), out_shape=(jax.Sha...  6.5 us
    ppermute x3, starting transfers between devices, swap_x_hi(): return lax.ppermute(x, 'ba', swap_perm(2))  5.97 us
  transfers between devices with their start and end apart: 29, of which 17 were waited for; matrix products, arithmetic and copies ran while one was open for 1% of the time, Pallas kernels for 6%

profile of v5, /device:TPU:96, one launch (start us, length us, event | category | flops | bytes accessed | tf_op | source)
XLA Modules:
  0.0 108.3 jit_solution(7436280683519343156)
XLA Ops:
  0.6 1.6 %collective-permute-start.2 = (bf16[768,256]{1,0:T(8,128)(2,1)}, bf16[768,256]{1,0:T(8,128)(2,1)S(1)}, u32[]{:S(2)}, u32[]{:S(2)}) collective-permute-start(bf16[768,256]{1,0:T(8,128)(2,1)} %bitcast.12), channel_id=1, source_target_pairs={{0,16},{16,0},{32,48},{48,32},{64,80},{80,64},{96,112},{112,96},{1... | collective-permute-start | bytes 1179656 | tf_op jit(solution)/shard_map/ppermute | solution.py:34
  2.3 3.1 %collective-permute-start = (bf16[768,256]{1,0:T(8,128)(2,1)}, bf16[768,256]{1,0:T(8,128)(2,1)S(1)}, u32[]{:S(2)}, u32[]{:S(2)}) collective-permute-start(bf16[768,256]{1,0:T(8,128)(2,1)} %bitcast.14), channel_id=1, source_target_pairs={{0,32},{16,48},{32,64},{48,80},{64,96},{80,112},{96,128},{112,144}... | collective-permute-start | bytes 1179656 | tf_op jit(solution)/shard_map/ppermute | solution.py:30
  5.4 2.7 %collective-permute-start.3 = (bf16[48,2304]{1,0:T(8,128)(2,1)}, bf16[48,2304]{1,0:T(8,128)(2,1)S(1)}, u32[]{:S(2)}, u32[]{:S(2)}) collective-permute-start(bf16[48,2304]{1,0:T(8,128)(2,1)} %refs_0_.1), channel_id=1, source_target_pairs={{0,2},{1,3},{2,0},{3,1},{4,6},{5,7},{6,4},{7,5},{8,10},{9,11},{10,... | collective-permute-start | bytes 663560 | tf_op jit(solution)/shard_map/ppermute | solution.py:42
  9.5 0.9 reshape.18.refs_6_
  10.4 0.7 copy-done.4
  11.1 0.7 copy-done.5
  11.7 0.7 copy-done.6
  12.4 0.9 shard_map.113
  13.3 1.9 %copy-done = bf16[8,48,4096]{2,1,0:T(8,128)(2,1)S(1)} copy-done((bf16[8,48,4096]{2,1,0:T(8,128)(2,1)S(1)}, bf16[8,48,4096]{2,1,0:T(8,128)(2,1)}, u32[]{:S(2)}) %copy-start) | copy-done | bytes 3145752
  15.2 1.0 copy-done.1
  16.2 0.4 shard_map.114
  16.6 2.2 %collective-permute-done.3.refs_1_ = bf16[48,2304]{1,0:T(8,128)(2,1)S(1)} collective-permute-done((bf16[48,2304]{1,0:T(8,128)(2,1)}, bf16[48,2304]{1,0:T(8,128)(2,1)S(1)}, u32[]{:S(2)}, u32[]{:S(2)}) %collective-permute-start.3) | collective-permute-done | bytes 221216 | tf_op jit(solution)/shard_map/ppermute | solution.py:42
  18.7 3.2 %collective-permute-start.4 = (bf16[768,256]{1,0:T(8,128)(2,1)S(1)}, bf16[768,256]{1,0:T(8,128)(2,1)S(1)}, u32[]{:S(2)}, u32[]{:S(2)}) collective-permute-start(bf16[768,256]{1,0:T(8,128)(2,1)S(1)} %collective-permute-done.refs_1_), channel_id=1, source_target_pairs={{0,32},{16,48},{32,64},{48,80},{64,96},{80,112},{96,128},{112,144}... | collective-permute-start | bytes 1179656 | tf_op jit(solution)/shard_map/ppermute | solution.py:30
  22.2 1.7 %collective-permute-start.11 = (bf16[2,48,2304]{2,1,0:T(8,128)(2,1)S(1)}, bf16[2,48,2304]{2,1,0:T(8,128)(2,1)S(1)}, u32[]{:S(2)}, u32[]{:S(2)}) collective-permute-start(bf16[2,48,2304]{2,1,0:T(8,128)(2,1)S(1)} %shard_map.117.refs_0_), channel_id=1, source_target_pairs={{0,4},{1,5},{2,6},{3,7},{4,8},{5,9},{6,10},{7,11},{8,12},{9,13},{1... | collective-permute-start | bytes 1327112 | tf_op jit(solution)/shard_map/ppermute | solution.py:38
  23.9 1.7 %collective-permute-start.10 = (bf16[2,48,2304]{2,1,0:T(8,128)(2,1)S(1)}, bf16[2,48,2304]{2,1,0:T(8,128)(2,1)S(1)}, u32[]{:S(2)}, u32[]{:S(2)}) collective-permute-start(bf16[2,48,2304]{2,1,0:T(8,128)(2,1)S(1)} %shard_map.117.refs_0_), channel_id=1, source_target_pairs={{0,12},{1,13},{2,14},{3,15},{4,0},{5,1},{6,2},{7,3},{8,4},{9,5},{1... | collective-permute-start | bytes 1327112 | tf_op jit(solution)/shard_map/ppermute | solution.py:38
  25.5 0.8 shard_map.115
  26.4 3.1 %collective-permute-done.4.refs_1_ = bf16[768,256]{1,0:T(8,128)(2,1)S(1)} collective-permute-done((bf16[768,256]{1,0:T(8,128)(2,1)S(1)}, bf16[768,256]{1,0:T(8,128)(2,1)S(1)}, u32[]{:S(2)}, u32[]{:S(2)}) %collective-permute-start.4) | collective-permute-done | bytes 393248 | tf_op jit(solution)/shard_map/ppermute | solution.py:30
  29.7 3.5 %collective-permute-done.6.refs_2_ = bf16[768,256]{1,0:T(8,128)(2,1)S(1)} collective-permute-done((bf16[768,256]{1,0:T(8,128)(2,1)S(1)}, bf16[768,256]{1,0:T(8,128)(2,1)S(1)}, u32[]{:S(2)}, u32[]{:S(2)}) %collective-permute-start.6) | collective-permute-done | bytes 393248 | tf_op jit(solution)/shard_map/ppermute | solution.py:34
  33.4 1.8 %collective-permute-start.8 = (bf16[768,256]{1,0:T(8,128)(2,1)S(1)}, bf16[768,256]{1,0:T(8,128)(2,1)S(1)}, u32[]{:S(2)}, u32[]{:S(2)}) collective-permute-start(bf16[768,256]{1,0:T(8,128)(2,1)S(1)} %collective-permute-done.5.refs_0_), channel_id=1, source_target_pairs={{0,224},{16,240},{32,0},{48,16},{64,32},{80,48},{96,64},{112,80},{... | collective-permute-start | bytes 1179656 | tf_op jit(solution)/shard_map/ppermute | solution.py:30
  35.2 0.8 shard_map.116
  36.0 4.1 %collective-permute-done.9.refs_2_ = bf16[768,256]{1,0:T(8,128)(2,1)S(1)} collective-permute-done((bf16[768,256]{1,0:T(8,128)(2,1)S(1)}, bf16[768,256]{1,0:T(8,128)(2,1)S(1)}, u32[]{:S(2)}, u32[]{:S(2)}) %collective-permute-start.9) | collective-permute-done | bytes 393248 | tf_op jit(solution)/shard_map/ppermute | solution.py:34
  40.1 1.3 %collective-permute-done.7.refs_1_ = bf16[768,256]{1,0:T(8,128)(2,1)S(1)} collective-permute-done((bf16[768,256]{1,0:T(8,128)(2,1)S(1)}, bf16[768,256]{1,0:T(8,128)(2,1)S(1)}, u32[]{:S(2)}, u32[]{:S(2)}) %collective-permute-start.7) | collective-permute-done | bytes 393248 | tf_op jit(solution)/shard_map/ppermute | solution.py:30
  41.4 1.8 %collective-permute-done.8.refs_0_ = bf16[768,256]{1,0:T(8,128)(2,1)S(1)} collective-permute-done((bf16[768,256]{1,0:T(8,128)(2,1)S(1)}, bf16[768,256]{1,0:T(8,128)(2,1)S(1)}, u32[]{:S(2)}, u32[]{:S(2)}) %collective-permute-start.8) | collective-permute-done | bytes 393248 | tf_op jit(solution)/shard_map/ppermute | solution.py:30
  43.2 3.0 %collective-permute-start.15 = (bf16[2,48,2304]{2,1,0:T(8,128)(2,1)S(1)}, bf16[2,48,2304]{2,1,0:T(8,128)(2,1)S(1)}, u32[]{:S(2)}, u32[]{:S(2)}) collective-permute-start(bf16[2,48,2304]{2,1,0:T(8,128)(2,1)S(1)} %collective-permute-done.10.refs_1_), channel_id=1, source_target_pairs={{0,12},{1,13},{2,14},{3,15},{4,0},{5,1},{6,2},{7,3},{8,4},{9,5},{1... | collective-permute-start | bytes 1327112 | tf_op jit(solution)/shard_map/ppermute | solution.py:38
  46.2 1.7 %collective-permute-start.14 = (bf16[768,256]{1,0:T(8,128)(2,1)S(1)}, bf16[768,256]{1,0:T(8,128)(2,1)S(1)}, u32[]{:S(2)}, u32[]{:S(2)}) collective-permute-start(bf16[768,256]{1,0:T(8,128)(2,1)S(1)} %collective-permute-done.8.refs_0_), channel_id=1, source_target_pairs={{0,16},{16,0},{32,48},{48,32},{64,80},{80,64},{96,112},{112,96},{1... | collective-permute-start | bytes 1179656 | tf_op jit(solution)/shard_map/ppermute | solution.py:34
  47.9 3.2 %collective-permute-start.12 = (bf16[768,256]{1,0:T(8,128)(2,1)S(1)}, bf16[768,256]{1,0:T(8,128)(2,1)S(1)}, u32[]{:S(2)}, u32[]{:S(2)}) collective-permute-start(bf16[768,256]{1,0:T(8,128)(2,1)S(1)} %collective-permute-done.7.refs_1_), channel_id=1, source_target_pairs={{0,32},{16,48},{32,64},{48,80},{64,96},{80,112},{96,128},{112,144}... | collective-permute-start | bytes 1179656 | tf_op jit(solution)/shard_map/ppermute | solution.py:30
  51.1 0.8 shard_map.118
  52.0 3.2 %collective-permute-done.13.refs_1_ = bf16[768,256]{1,0:T(8,128)(2,1)S(1)} collective-permute-done((bf16[768,256]{1,0:T(8,128)(2,1)S(1)}, bf16[768,256]{1,0:T(8,128)(2,1)S(1)}, u32[]{:S(2)}, u32[]{:S(2)}) %collective-permute-start.13) | collective-permute-done | bytes 393248 | tf_op jit(solution)/shard_map/ppermute | solution.py:30
  55.2 1.2 %collective-permute-done.12.refs_0_ = bf16[768,256]{1,0:T(8,128)(2,1)S(1)} collective-permute-done((bf16[768,256]{1,0:T(8,128)(2,1)S(1)}, bf16[768,256]{1,0:T(8,128)(2,1)S(1)}, u32[]{:S(2)}, u32[]{:S(2)}) %collective-permute-start.12) | collective-permute-done | bytes 393248 | tf_op jit(solution)/shard_map/ppermute | solution.py:30
  56.7 3.8 %collective-permute-start.18 = (bf16[768,256]{1,0:T(8,128)(2,1)S(1)}, bf16[768,256]{1,0:T(8,128)(2,1)S(1)}, u32[]{:S(2)}, u32[]{:S(2)}) collective-permute-start(bf16[768,256]{1,0:T(8,128)(2,1)S(1)} %collective-permute-done.9.refs_2_), channel_id=1, source_target_pairs={{0,32},{16,48},{32,64},{48,80},{64,96},{80,112},{96,128},{112,144}... | collective-permute-start | bytes 1179656 | tf_op jit(solution)/shard_map/ppermute | solution.py:30
  60.8 0.8 shard_map.119
  61.9 7.5 %collective-permute-done.18.refs_2_ = bf16[768,256]{1,0:T(8,128)(2,1)S(1)} collective-permute-done((bf16[768,256]{1,0:T(8,128)(2,1)S(1)}, bf16[768,256]{1,0:T(8,128)(2,1)S(1)}, u32[]{:S(2)}, u32[]{:S(2)}) %collective-permute-start.18) | collective-permute-done | bytes 393248 | tf_op jit(solution)/shard_map/ppermute | solution.py:30
  69.4 2.2 %collective-permute-done.17.refs_1_ = bf16[768,256]{1,0:T(8,128)(2,1)S(1)} collective-permute-done((bf16[768,256]{1,0:T(8,128)(2,1)S(1)}, bf16[768,256]{1,0:T(8,128)(2,1)S(1)}, u32[]{:S(2)}, u32[]{:S(2)}) %collective-permute-start.17) | collective-permute-done | bytes 393248 | tf_op jit(solution)/shard_map/ppermute | solution.py:34
  71.6 1.3 %collective-permute-done.16.refs_0_ = bf16[768,256]{1,0:T(8,128)(2,1)S(1)} collective-permute-done((bf16[768,256]{1,0:T(8,128)(2,1)S(1)}, bf16[768,256]{1,0:T(8,128)(2,1)S(1)}, u32[]{:S(2)}, u32[]{:S(2)}) %collective-permute-start.16) | collective-permute-done | bytes 393248 | tf_op jit(solution)/shard_map/ppermute | solution.py:30
  72.9 6.5 %shard_map.122 = (bf16[16,768,256]{2,1,0:T(8,128)(2,1)S(1)}, bf16[384,768]{1,0:T(8,128)(2,1)S(1)}, bf16[3104,256]{1,0:T(8,128)(2,1)S(1)}, f32[16,256]{1,0:T(8,128)S(1)}) custom-call(bf16[384,4096]{1,0:T(8,128)(2,1)S(1)} %bitcast.11, bf16[768,256]{1,0:T(8,128)(2,1)S(1)} %collective-permute-done.16.refs_0_, ...), custom_call_target="tpu_custom_call", output_to_operand_aliasing={{0}: (9, {})} | custom-call | tf_op jit(solution)/shard_map/pallas_call | solution.py:301
  79.7 1.4 %shard_map.123.kept_ref = f32[3072,256]{1,0:T(8,128)S(1)} custom-call(bf16[384,768]{1,0:T(8,128)(2,1)S(1)} %get-tuple-element.108.left_ref, bf16[16,768,256]{2,1,0:T(8,128)(2,1)S(1)} %get-tuple-element.109.stack_ref), custom_call_target="tpu_custom_call" | custom-call | flops 1207959552 | bytes 3145728 | tf_op jit(solution)/shard_map/pallas_call | solution.py:328
  81.2 2.0 %collective-permute-done.20.recv_ref = bf16[3104,256]{1,0:T(8,128)(2,1)S(1)} collective-permute-done((bf16[3104,256]{1,0:T(8,128)(2,1)S(1)}, bf16[3104,256]{1,0:T(8,128)(2,1)S(1)}, u32[]{:S(2)}, u32[]{:S(2)}) %collective-permute-start.20) | collective-permute-done | bytes 1589280 | tf_op jit(solution)/shard_map/ppermute | solution.py:46
  83.4 1.7 %collective-permute-start.24 = (bf16[928,256]{1,0:T(8,128)(2,1)S(1)}, bf16[928,256]{1,0:T(8,128)(2,1)S(1)}, u32[]{:S(2)}, u32[]{:S(2)}) collective-permute-start(bf16[928,256]{1,0:T(8,128)(2,1)S(1)} %get-tuple-element.116), channel_id=1, source_target_pairs={{0,2},{1,3},{2,0},{3,1},{4,6},{5,7},{6,4},{7,5},{8,10},{9,11},{10,... | collective-permute-start | bytes 1425416 | tf_op jit(solution)/shard_map/ppermute | solution.py:42
  85.1 2.2 %collective-permute-start.22 = (bf16[320,256]{1,0:T(8,128)(2,1)S(1)}, bf16[320,256]{1,0:T(8,128)(2,1)S(1)}, u32[]{:S(2)}, u32[]{:S(2)}) collective-permute-start(bf16[320,256]{1,0:T(8,128)(2,1)S(1)} %get-tuple-element.114), channel_id=1, source_target_pairs={{0,8},{1,9},{2,10},{3,11},{4,12},{5,13},{6,14},{7,15},{8,0},{9,1},... | collective-permute-start | bytes 491528 | tf_op jit(solution)/shard_map/ppermute | solution.py:38
  87.3 1.1 collective-permute-start.23
  88.3 7.4 %collective-permute-done.21.a_ref = bf16[320,256]{1,0:T(8,128)(2,1)S(1)} collective-permute-done((bf16[320,256]{1,0:T(8,128)(2,1)S(1)}, bf16[320,256]{1,0:T(8,128)(2,1)S(1)}, u32[]{:S(2)}, u32[]{:S(2)}) %collective-permute-start.21) | collective-permute-done | bytes 163872 | tf_op jit(solution)/shard_map/ppermute | solution.py:38
  95.8 0.6 collective-permute-done.23.c_ref
  96.4 1.5 %collective-permute-done.24.recv_ref = bf16[928,256]{1,0:T(8,128)(2,1)S(1)} collective-permute-done((bf16[928,256]{1,0:T(8,128)(2,1)S(1)}, bf16[928,256]{1,0:T(8,128)(2,1)S(1)}, u32[]{:S(2)}, u32[]{:S(2)}) %collective-permute-start.24) | collective-permute-done | bytes 475168 | tf_op jit(solution)/shard_map/ppermute | solution.py:42
  98.1 2.3 %collective-permute-start.26 = (bf16[256,256]{1,0:T(8,128)(2,1)S(1)}, bf16[256,256]{1,0:T(8,128)(2,1)S(1)}, u32[]{:S(2)}, u32[]{:S(2)}) collective-permute-start(bf16[256,256]{1,0:T(8,128)(2,1)S(1)} %get-tuple-element.125), channel_id=1, source_target_pairs={{0,8},{1,9},{2,10},{3,11},{4,12},{5,13},{6,14},{7,15},{8,0},{9,1},... | collective-permute-start | bytes 393224 | tf_op jit(solution)/shard_map/ppermute | solution.py:38
  100.4 1.0 collective-permute-start.27
  101.4 1.6 %collective-permute-start.28 = (bf16[160,256]{1,0:T(8,128)(2,1)S(1)}, bf16[160,256]{1,0:T(8,128)(2,1)S(1)}, u32[]{:S(2)}, u32[]{:S(2)}) collective-permute-start(bf16[160,256]{1,0:T(8,128)(2,1)S(1)} %get-tuple-element.127), channel_id=1, source_target_pairs={{0,2},{1,3},{2,0},{3,1},{4,6},{5,7},{6,4},{7,5},{8,10},{9,11},{10,... | collective-permute-start | bytes 245768 | tf_op jit(solution)/shard_map/ppermute | solution.py:42
  103.0 4.4 %collective-permute-done.28.recv_ref = bf16[160,256]{1,0:T(8,128)(2,1)S(1)} collective-permute-done((bf16[160,256]{1,0:T(8,128)(2,1)S(1)}, bf16[160,256]{1,0:T(8,128)(2,1)S(1)}, u32[]{:S(2)}, u32[]{:S(2)}) %collective-permute-start.28) | collective-permute-done | bytes 81952 | tf_op jit(solution)/shard_map/ppermute | solution.py:42
  107.5 0.8 shard_map.126
  (39 shorter events, 2.6 us)
Async XLA Ops:
  0.6 18.1 %collective-permute-start.2 = (bf16[768,256]{1,0:T(8,128)(2,1)}, bf16[768,256]{1,0:T(8,128)(2,1)S(1)}, u32[]{:S(2)}, u32[]{:S(2)}) collective-permute-start(bf16[768,256]{1,0:T(8,128)(2,1)} %bitcast.12), channel_id=1, source_target_pairs={{0,16},{16,0},{32,48},{48,32},{64,80},{80,64},{96,112},{112,96},{1... | collective-permute-start | bytes 1179656 | tf_op jit(solution)/shard_map/ppermute | solution.py:34
  2.2 16.5 %collective-permute-start.1 = (bf16[768,256]{1,0:T(8,128)(2,1)}, bf16[768,256]{1,0:T(8,128)(2,1)S(1)}, u32[]{:S(2)}, u32[]{:S(2)}) collective-permute-start(bf16[768,256]{1,0:T(8,128)(2,1)} %bitcast.13), channel_id=1, source_target_pairs={{0,224},{16,240},{32,0},{48,16},{64,32},{80,48},{96,64},{112,80},{... | collective-permute-start | bytes 1179656 | tf_op jit(solution)/shard_map/ppermute | solution.py:30
  2.3 16.4 %collective-permute-start = (bf16[768,256]{1,0:T(8,128)(2,1)}, bf16[768,256]{1,0:T(8,128)(2,1)S(1)}, u32[]{:S(2)}, u32[]{:S(2)}) collective-permute-start(bf16[768,256]{1,0:T(8,128)(2,1)} %bitcast.14), channel_id=1, source_target_pairs={{0,32},{16,48},{32,64},{48,80},{64,96},{80,112},{96,128},{112,144}... | collective-permute-start | bytes 1179656 | tf_op jit(solution)/shard_map/ppermute | solution.py:30
  5.4 13.3 %collective-permute-start.3 = (bf16[48,2304]{1,0:T(8,128)(2,1)}, bf16[48,2304]{1,0:T(8,128)(2,1)S(1)}, u32[]{:S(2)}, u32[]{:S(2)}) collective-permute-start(bf16[48,2304]{1,0:T(8,128)(2,1)} %refs_0_.1), channel_id=1, source_target_pairs={{0,2},{1,3},{2,0},{3,1},{4,6},{5,7},{6,4},{7,5},{8,10},{9,11},{10,... | collective-permute-start | bytes 663560 | tf_op jit(solution)/shard_map/ppermute | solution.py:42
  10.4 0.7 copy-start.4
  11.1 0.7 copy-start.5
  11.7 0.7 copy-start.6
  13.3 1.9 %copy-start = (bf16[8,48,4096]{2,1,0:T(8,128)(2,1)S(1)}, bf16[8,48,4096]{2,1,0:T(8,128)(2,1)}, u32[]{:S(2)}) copy-start(bf16[8,48,4096]{2,1,0:T(8,128)(2,1)} %param.10) | copy-start | bytes 9437188
  15.2 1.0 copy-start.1
  16.2 6.0 %copy-start.3 = (bf16[48,2304]{1,0:T(8,128)(2,1)S(1)}, bf16[48,2304]{1,0:T(8,128)(2,1)}, u32[]{:S(2)}) copy-start(bf16[48,2304]{1,0:T(8,128)(2,1)} %refs_0_.1) | copy-start | bytes 663556
  18.7 10.7 %collective-permute-start.4 = (bf16[768,256]{1,0:T(8,128)(2,1)S(1)}, bf16[768,256]{1,0:T(8,128)(2,1)S(1)}, u32[]{:S(2)}, u32[]{:S(2)}) collective-permute-start(bf16[768,256]{1,0:T(8,128)(2,1)S(1)} %collective-permute-done.refs_1_), channel_id=1, source_target_pairs={{0,32},{16,48},{32,64},{48,80},{64,96},{80,112},{96,128},{112,144}... | collective-permute-start | bytes 1179656 | tf_op jit(solution)/shard_map/ppermute | solution.py:30
  21.9 11.2 %collective-permute-start.6 = (bf16[768,256]{1,0:T(8,128)(2,1)S(1)}, bf16[768,256]{1,0:T(8,128)(2,1)S(1)}, u32[]{:S(2)}, u32[]{:S(2)}) collective-permute-start(bf16[768,256]{1,0:T(8,128)(2,1)S(1)} %collective-permute-done.1.refs_0_), channel_id=1, source_target_pairs={{0,16},{16,0},{32,48},{48,32},{64,80},{80,64},{96,112},{112,96},{1... | collective-permute-start | bytes 1179656 | tf_op jit(solution)/shard_map/ppermute | solution.py:34
  22.2 11.0 %collective-permute-start.5 = (bf16[768,256]{1,0:T(8,128)(2,1)S(1)}, bf16[768,256]{1,0:T(8,128)(2,1)S(1)}, u32[]{:S(2)}, u32[]{:S(2)}) collective-permute-start(bf16[768,256]{1,0:T(8,128)(2,1)S(1)} %collective-permute-done.1.refs_0_), channel_id=1, source_target_pairs={{0,224},{16,240},{32,0},{48,16},{64,32},{80,48},{96,64},{112,80},{... | collective-permute-start | bytes 1179656 | tf_op jit(solution)/shard_map/ppermute | solution.py:30
  22.2 17.9 %collective-permute-start.11 = (bf16[2,48,2304]{2,1,0:T(8,128)(2,1)S(1)}, bf16[2,48,2304]{2,1,0:T(8,128)(2,1)S(1)}, u32[]{:S(2)}, u32[]{:S(2)}) collective-permute-start(bf16[2,48,2304]{2,1,0:T(8,128)(2,1)S(1)} %shard_map.117.refs_0_), channel_id=1, source_target_pairs={{0,4},{1,5},{2,6},{3,7},{4,8},{5,9},{6,10},{7,11},{8,12},{9,13},{1... | collective-permute-start | bytes 1327112 | tf_op jit(solution)/shard_map/ppermute | solution.py:38
  23.9 16.2 %collective-permute-start.10 = (bf16[2,48,2304]{2,1,0:T(8,128)(2,1)S(1)}, bf16[2,48,2304]{2,1,0:T(8,128)(2,1)S(1)}, u32[]{:S(2)}, u32[]{:S(2)}) collective-permute-start(bf16[2,48,2304]{2,1,0:T(8,128)(2,1)S(1)} %shard_map.117.refs_0_), channel_id=1, source_target_pairs={{0,12},{1,13},{2,14},{3,15},{4,0},{5,1},{6,2},{7,3},{8,4},{9,5},{1... | collective-permute-start | bytes 1327112 | tf_op jit(solution)/shard_map/ppermute | solution.py:38
  29.4 10.6 %collective-permute-start.9 = (bf16[768,256]{1,0:T(8,128)(2,1)S(1)}, bf16[768,256]{1,0:T(8,128)(2,1)S(1)}, u32[]{:S(2)}, u32[]{:S(2)}) collective-permute-start(bf16[768,256]{1,0:T(8,128)(2,1)S(1)} %collective-permute-done.refs_1_), channel_id=1, source_target_pairs={{0,16},{16,0},{32,48},{48,32},{64,80},{80,64},{96,112},{112,96},{1... | collective-permute-start | bytes 1179656 | tf_op jit(solution)/shard_map/ppermute | solution.py:34
  33.1 8.3 %collective-permute-start.7 = (bf16[768,256]{1,0:T(8,128)(2,1)S(1)}, bf16[768,256]{1,0:T(8,128)(2,1)S(1)}, u32[]{:S(2)}, u32[]{:S(2)}) collective-permute-start(bf16[768,256]{1,0:T(8,128)(2,1)S(1)} %collective-permute-done.4.refs_1_), channel_id=1, source_target_pairs={{0,32},{16,48},{32,64},{48,80},{64,96},{80,112},{96,128},{112,144}... | collective-permute-start | bytes 1179656 | tf_op jit(solution)/shard_map/ppermute | solution.py:30
  33.4 9.9 %collective-permute-start.8 = (bf16[768,256]{1,0:T(8,128)(2,1)S(1)}, bf16[768,256]{1,0:T(8,128)(2,1)S(1)}, u32[]{:S(2)}, u32[]{:S(2)}) collective-permute-start(bf16[768,256]{1,0:T(8,128)(2,1)S(1)} %collective-permute-done.5.refs_0_), channel_id=1, source_target_pairs={{0,224},{16,240},{32,0},{48,16},{64,32},{80,48},{96,64},{112,80},{... | collective-permute-start | bytes 1179656 | tf_op jit(solution)/shard_map/ppermute | solution.py:30
  43.2 13.2 %collective-permute-start.15 = (bf16[2,48,2304]{2,1,0:T(8,128)(2,1)S(1)}, bf16[2,48,2304]{2,1,0:T(8,128)(2,1)S(1)}, u32[]{:S(2)}, u32[]{:S(2)}) collective-permute-start(bf16[2,48,2304]{2,1,0:T(8,128)(2,1)S(1)} %collective-permute-done.10.refs_1_), channel_id=1, source_target_pairs={{0,12},{1,13},{2,14},{3,15},{4,0},{5,1},{6,2},{7,3},{8,4},{9,5},{1... | collective-permute-start | bytes 1327112 | tf_op jit(solution)/shard_map/ppermute | solution.py:38
  46.2 9.0 %collective-permute-start.13 = (bf16[768,256]{1,0:T(8,128)(2,1)S(1)}, bf16[768,256]{1,0:T(8,128)(2,1)S(1)}, u32[]{:S(2)}, u32[]{:S(2)}) collective-permute-start(bf16[768,256]{1,0:T(8,128)(2,1)S(1)} %collective-permute-done.6.refs_2_), channel_id=1, source_target_pairs={{0,224},{16,240},{32,0},{48,16},{64,32},{80,48},{96,64},{112,80},{... | collective-permute-start | bytes 1179656 | tf_op jit(solution)/shard_map/ppermute | solution.py:30
  46.2 9.0 %collective-permute-start.14 = (bf16[768,256]{1,0:T(8,128)(2,1)S(1)}, bf16[768,256]{1,0:T(8,128)(2,1)S(1)}, u32[]{:S(2)}, u32[]{:S(2)}) collective-permute-start(bf16[768,256]{1,0:T(8,128)(2,1)S(1)} %collective-permute-done.8.refs_0_), channel_id=1, source_target_pairs={{0,16},{16,0},{32,48},{48,32},{64,80},{80,64},{96,112},{112,96},{1... | collective-permute-start | bytes 1179656 | tf_op jit(solution)/shard_map/ppermute | solution.py:34
  47.9 8.5 %collective-permute-start.12 = (bf16[768,256]{1,0:T(8,128)(2,1)S(1)}, bf16[768,256]{1,0:T(8,128)(2,1)S(1)}, u32[]{:S(2)}, u32[]{:S(2)}) collective-permute-start(bf16[768,256]{1,0:T(8,128)(2,1)S(1)} %collective-permute-done.7.refs_1_), channel_id=1, source_target_pairs={{0,32},{16,48},{32,64},{48,80},{64,96},{80,112},{96,128},{112,144}... | collective-permute-start | bytes 1179656 | tf_op jit(solution)/shard_map/ppermute | solution.py:30
  56.5 5.1 %copy-start.2 = (bf16[48,2304]{1,0:T(8,128)(2,1)S(1)}, bf16[48,2304]{1,0:T(8,128)(2,1)}, u32[]{:S(2)}) copy-start(bf16[48,2304]{1,0:T(8,128)(2,1)} %coulomb_ref.1) | copy-start | bytes 663556
  56.6 5.1 %collective-permute-start.19 = (bf16[4,2,48,2304]{3,2,1,0:T(8,128)(2,1)S(1)}, bf16[4,2,48,2304]{3,2,1,0:T(8,128)(2,1)S(1)}, u32[]{:S(2)}, u32[]{:S(2)}) collective-permute-start(bf16[4,2,48,2304]{3,2,1,0:T(8,128)(2,1)S(1)} %shard_map.120.own_ref), channel_id=1, source_target_pairs={{0,1},{1,0},{2,3},{3,2},{4,5},{5,4},{6,7},{7,6},{8,9},{9,8},{10,11... | collective-permute-start | bytes 5308424 | tf_op jit(solution)/shard_map/ppermute | solution.py:46
  56.7 12.7 %collective-permute-start.18 = (bf16[768,256]{1,0:T(8,128)(2,1)S(1)}, bf16[768,256]{1,0:T(8,128)(2,1)S(1)}, u32[]{:S(2)}, u32[]{:S(2)}) collective-permute-start(bf16[768,256]{1,0:T(8,128)(2,1)S(1)} %collective-permute-done.9.refs_2_), channel_id=1, source_target_pairs={{0,32},{16,48},{32,64},{48,80},{64,96},{80,112},{96,128},{112,144}... | collective-permute-start | bytes 1179656 | tf_op jit(solution)/shard_map/ppermute | solution.py:30
  60.4 11.2 %collective-permute-start.17 = (bf16[768,256]{1,0:T(8,128)(2,1)S(1)}, bf16[768,256]{1,0:T(8,128)(2,1)S(1)}, u32[]{:S(2)}, u32[]{:S(2)}) collective-permute-start(bf16[768,256]{1,0:T(8,128)(2,1)S(1)} %collective-permute-done.7.refs_1_), channel_id=1, source_target_pairs={{0,16},{16,0},{32,48},{48,32},{64,80},{80,64},{96,112},{112,96},{1... | collective-permute-start | bytes 1179656 | tf_op jit(solution)/shard_map/ppermute | solution.py:34
  60.8 12.1 %collective-permute-start.16 = (bf16[768,256]{1,0:T(8,128)(2,1)S(1)}, bf16[768,256]{1,0:T(8,128)(2,1)S(1)}, u32[]{:S(2)}, u32[]{:S(2)}) collective-permute-start(bf16[768,256]{1,0:T(8,128)(2,1)S(1)} %collective-permute-done.14.refs_2_), channel_id=1, source_target_pairs={{0,224},{16,240},{32,0},{48,16},{64,32},{80,48},{96,64},{112,80},{... | collective-permute-start | bytes 1179656 | tf_op jit(solution)/shard_map/ppermute | solution.py:30
  79.4 3.7 %collective-permute-start.20 = (bf16[3104,256]{1,0:T(8,128)(2,1)S(1)}, bf16[3104,256]{1,0:T(8,128)(2,1)S(1)}, u32[]{:S(2)}, u32[]{:S(2)}) collective-permute-start(bf16[3104,256]{1,0:T(8,128)(2,1)S(1)} %get-tuple-element.111), channel_id=1, source_target_pairs={{0,1},{1,0},{2,3},{3,2},{4,5},{5,4},{6,7},{7,6},{8,9},{9,8},{10,11... | collective-permute-start | bytes 4767752 | tf_op jit(solution)/shard_map/ppermute | solution.py:46
  83.4 14.5 %collective-permute-start.24 = (bf16[928,256]{1,0:T(8,128)(2,1)S(1)}, bf16[928,256]{1,0:T(8,128)(2,1)S(1)}, u32[]{:S(2)}, u32[]{:S(2)}) collective-permute-start(bf16[928,256]{1,0:T(8,128)(2,1)S(1)} %get-tuple-element.116), channel_id=1, source_target_pairs={{0,2},{1,3},{2,0},{3,1},{4,6},{5,7},{6,4},{7,5},{8,10},{9,11},{10,... | collective-permute-start | bytes 1425416 | tf_op jit(solution)/shard_map/ppermute | solution.py:42
  85.1 10.7 %collective-permute-start.21 = (bf16[320,256]{1,0:T(8,128)(2,1)S(1)}, bf16[320,256]{1,0:T(8,128)(2,1)S(1)}, u32[]{:S(2)}, u32[]{:S(2)}) collective-permute-start(bf16[320,256]{1,0:T(8,128)(2,1)S(1)} %get-tuple-element.113), channel_id=1, source_target_pairs={{0,4},{1,5},{2,6},{3,7},{4,8},{5,9},{6,10},{7,11},{8,12},{9,13},{1... | collective-permute-start | bytes 491528 | tf_op jit(solution)/shard_map/ppermute | solution.py:38
  85.1 10.7 %collective-permute-start.22 = (bf16[320,256]{1,0:T(8,128)(2,1)S(1)}, bf16[320,256]{1,0:T(8,128)(2,1)S(1)}, u32[]{:S(2)}, u32[]{:S(2)}) collective-permute-start(bf16[320,256]{1,0:T(8,128)(2,1)S(1)} %get-tuple-element.114), channel_id=1, source_target_pairs={{0,8},{1,9},{2,10},{3,11},{4,12},{5,13},{6,14},{7,15},{8,0},{9,1},... | collective-permute-start | bytes 491528 | tf_op jit(solution)/shard_map/ppermute | solution.py:38
  87.3 9.1 %collective-permute-start.23 = (bf16[320,256]{1,0:T(8,128)(2,1)S(1)}, bf16[320,256]{1,0:T(8,128)(2,1)S(1)}, u32[]{:S(2)}, u32[]{:S(2)}) collective-permute-start(bf16[320,256]{1,0:T(8,128)(2,1)S(1)} %get-tuple-element.115), channel_id=1, source_target_pairs={{0,12},{1,13},{2,14},{3,15},{4,0},{5,1},{6,2},{7,3},{8,4},{9,5},{1... | collective-permute-start | bytes 491528 | tf_op jit(solution)/shard_map/ppermute | solution.py:38
  98.1 9.3 %collective-permute-start.25 = (bf16[256,256]{1,0:T(8,128)(2,1)S(1)}, bf16[256,256]{1,0:T(8,128)(2,1)S(1)}, u32[]{:S(2)}, u32[]{:S(2)}) collective-permute-start(bf16[256,256]{1,0:T(8,128)(2,1)S(1)} %get-tuple-element.124), channel_id=1, source_target_pairs={{0,4},{1,5},{2,6},{3,7},{4,8},{5,9},{6,10},{7,11},{8,12},{9,13},{1... | collective-permute-start | bytes 393224 | tf_op jit(solution)/shard_map/ppermute | solution.py:38
  98.1 9.2 %collective-permute-start.26 = (bf16[256,256]{1,0:T(8,128)(2,1)S(1)}, bf16[256,256]{1,0:T(8,128)(2,1)S(1)}, u32[]{:S(2)}, u32[]{:S(2)}) collective-permute-start(bf16[256,256]{1,0:T(8,128)(2,1)S(1)} %get-tuple-element.125), channel_id=1, source_target_pairs={{0,8},{1,9},{2,10},{3,11},{4,12},{5,13},{6,14},{7,15},{8,0},{9,1},... | collective-permute-start | bytes 393224 | tf_op jit(solution)/shard_map/ppermute | solution.py:38
  100.4 7.1 %collective-permute-start.27 = (bf16[256,256]{1,0:T(8,128)(2,1)S(1)}, bf16[256,256]{1,0:T(8,128)(2,1)S(1)}, u32[]{:S(2)}, u32[]{:S(2)}) collective-permute-start(bf16[256,256]{1,0:T(8,128)(2,1)S(1)} %get-tuple-element.126), channel_id=1, source_target_pairs={{0,12},{1,13},{2,14},{3,15},{4,0},{5,1},{6,2},{7,3},{8,4},{9,5},{1... | collective-permute-start | bytes 393224 | tf_op jit(solution)/shard_map/ppermute | solution.py:38
  101.4 5.9 %collective-permute-start.28 = (bf16[160,256]{1,0:T(8,128)(2,1)S(1)}, bf16[160,256]{1,0:T(8,128)(2,1)S(1)}, u32[]{:S(2)}, u32[]{:S(2)}) collective-permute-start(bf16[160,256]{1,0:T(8,128)(2,1)S(1)} %get-tuple-element.127), channel_id=1, source_target_pairs={{0,2},{1,3},{2,0},{3,1},{4,6},{5,7},{6,4},{7,5},{8,10},{9,11},{10,... | collective-permute-start | bytes 245768 | tf_op jit(solution)/shard_map/ppermute | solution.py:42
